TPU v7x, 32 devices: a whole 2x2x4 slice. The times are simulated.
32 devices in a mesh: dp: 8 (over y, x, core), etp: 4 (over z).
Axes of the slice: x: 2, y: 2, z: 4, core: 2. Of those that a mesh axis runs over, the one named last changes fastest.
Arguments:
- tokens: bfloat16 [2048, 3072], P('dp'), may hold values from -6 to 6
- cotangent: bfloat16 [2048, 3072], P('dp'), may hold values from -6 to 6
- w_gate: float32 [2, 3072, 6144], P(None, 'dp', 'etp'), may hold values from -0.109375 to 0.109375
- w_up: float32 [2, 3072, 6144], P(None, 'dp', 'etp'), may hold values from -0.109375 to 0.109375
- w_down: float32 [2, 6144, 3072], P(None, 'etp', 'dp'), may hold values from -0.078125 to 0.078125
- slot_token: int32 [4096], P('dp'), may hold values from 0 to 255, as said below
- slot_gate: int32 [4096], P('dp'), may hold values from 0 to 16
- block_expert: int32 [32], P('dp'), may hold values from 0 to 2, as said below
Outputs:
- combined: bfloat16 [2048, 3072], P('dp', 'etp')
- input_grad: bfloat16 [2048, 3072], P('dp', 'etp')
Inputs may be any that keep to these rules, and one draw needn't show every extreme that they name: `slot_token`: within the live blocks of one expert on one dp index no token repeats, so each expert has at most 2 live blocks there. `block_expert`: blocks of the experts and padding blocks stand in any order; each expert has at most 2 blocks on one dp index, and on some dp index every block is live.
All inputs are finite; a program needn't handle non-finite values.
Results may differ from a plain program's by a relative error of at most 0.014.
Values may be sent and summed in bfloat16 or wider, within the bound.
No kernel may reach another device: no remote copies, remote signals or barrier semaphores. Data moves between devices by JAX's collectives and lax.ppermute only.
A program may use at most 128 MiB of HBM per device.

v0:
```python
import jax
import jax.numpy as jnp
from jax import lax
from jax.sharding import PartitionSpec as P

gate_steps = 16.0


def block_terms(
    gate_mat,
    up_mat,
    down_mat,
    tokens,
    cotangent,
    slot_token,
    scale,
    block_index,
    block_rows,
    totals,
):
    y_total, dx_total = totals
    row_start = block_index * block_rows
    token_rows = lax.dynamic_slice_in_dim(slot_token, row_start, block_rows, 0)
    gate_scale = lax.dynamic_slice_in_dim(scale, row_start, block_rows, 0)[:, None]
    inputs = tokens[token_rows]
    upstream = cotangent[token_rows]
    gate_pre = jnp.dot(inputs, gate_mat, preferred_element_type=jnp.float32)
    up_pre = jnp.dot(inputs, up_mat, preferred_element_type=jnp.float32)
    squash = jax.nn.sigmoid(gate_pre)
    active = gate_pre * squash
    hidden = (active * up_pre).astype(jnp.bfloat16)
    produced = jnp.dot(hidden, down_mat, preferred_element_type=jnp.float32) * gate_scale
    d_out = (gate_scale * upstream.astype(jnp.float32)).astype(jnp.bfloat16)
    contract_last = (((1,), (1,)), ((), ()))
    d_hidden = lax.dot_general(d_out, down_mat, contract_last, preferred_element_type=jnp.float32)
    d_pre = (d_hidden * up_pre * squash * (1.0 + gate_pre * (1.0 - squash))).astype(jnp.bfloat16)
    d_up = (d_hidden * active).astype(jnp.bfloat16)
    backward = lax.dot_general(d_pre, gate_mat, contract_last, preferred_element_type=jnp.float32)
    backward = backward + lax.dot_general(
        d_up, up_mat, contract_last, preferred_element_type=jnp.float32
    )
    return (y_total.at[token_rows].add(produced), dx_total.at[token_rows].add(backward))


def shards(tokens, cotangent, w_gate, w_up, w_down, slot_token, slot_gate, block_expert):
    experts_count = w_gate.shape[0]
    block_count = block_expert.shape[0]
    block_rows = slot_token.shape[0] // block_count
    scale = slot_gate.astype(jnp.float32) / gate_steps
    gate_low = w_gate.astype(jnp.bfloat16)
    up_low = w_up.astype(jnp.bfloat16)
    down_low = w_down.astype(jnp.bfloat16)
    zeroed = jnp.zeros(tokens.shape, jnp.float32)
    totals = (zeroed, zeroed)

    def skip_block(state):
        return state

    for expert in range(experts_count):
        gate_mat, up_mat = (
            lax.all_gather(gate_low[expert], "dp", axis=0, tiled=True),
            lax.all_gather(up_low[expert], "dp", axis=0, tiled=True),
        )
        down_mat = lax.all_gather(down_low[expert], "dp", axis=1, tiled=True)

        def visit_one(
            block_index, state, gate_mat=gate_mat, up_mat=up_mat, down_mat=down_mat, expert=expert
        ):

            def compute_block(inner):
                return block_terms(
                    gate_mat,
                    up_mat,
                    down_mat,
                    tokens,
                    cotangent,
                    slot_token,
                    scale,
                    block_index,
                    block_rows,
                    inner,
                )

            return lax.cond(block_expert[block_index] == expert, compute_block, skip_block, state)

        totals = lax.fori_loop(0, block_count, visit_one, totals)
    combined, input_grad = (
        lax.psum_scatter(
            totals[0].astype(jnp.bfloat16), "etp", scatter_dimension=1, tiled=True
        ).astype(jnp.float32),
        lax.psum_scatter(
            totals[1].astype(jnp.bfloat16), "etp", scatter_dimension=1, tiled=True
        ).astype(jnp.float32),
    )
    return (combined.astype(jnp.bfloat16), input_grad.astype(jnp.bfloat16))


def solution(mesh):
    in_specs = (
        P("dp", None),
        P("dp", None),
        P(None, "dp", "etp"),
        P(None, "dp", "etp"),
        P(None, "etp", "dp"),
        P("dp"),
        P("dp"),
        P("dp"),
    )
    out_specs = (P("dp", "etp"), P("dp", "etp"))
    return jax.shard_map(shards, mesh=mesh, in_specs=in_specs, out_specs=out_specs, check_vma=False)
```

profile of v0, /device:TPU:11, one launch (start us, length us, event | category | flops | bytes accessed | tf_op | source)
XLA Modules:
  0.0 592.3 jit_solution(2446377777634838472)
XLA Ops:
  7.2 2.6 convert_element_type.72
  9.8 1.6 fusion.22
  11.5 2.6 convert_element_type.73
  14.1 1.6 fusion.21
  15.7 2.6 convert_element_type.74
  18.3 1.7 fusion.20
  20.7 0.5 all-gather.21.cloned.1.call-update
  21.9 50.1 %all-gather.13.cloned.1.call-done = bf16[1,3072,1536]{2,1,0:T(8,128)(2,1)} async-done(((bf16[1,384,1536]{2,1,0:T(8,128)(2,1)}), bf16[1,3072,1536]{2,1,0:T(8,128)(2,1)}) %all-gather.13.cloned.1.call-update) | async-done | bytes 9437200 | tf_op jit(solution)/shard_map/all_gather | solution.py:61
  72.0 60.7 %all-gather.15.cloned.1.call-done = bf16[1,3072,1536]{2,1,0:T(8,128)(2,1)} async-done(((bf16[1,384,1536]{2,1,0:T(8,128)(2,1)}), bf16[1,3072,1536]{2,1,0:T(8,128)(2,1)}) %all-gather.15.cloned.1.call-update) | async-done | bytes 9437200 | tf_op jit(solution)/shard_map/all_gather | solution.py:62
  132.7 62.5 %all-gather.17.cloned.1.call-done = bf16[1,1536,3072]{2,1,0:T(8,128)(2,1)} async-done(((bf16[1,1536,384]{2,1,0:T(8,128)(2,1)}), bf16[1,1536,3072]{2,1,0:T(8,128)(2,1)}) %all-gather.17.cloned.1.call-update) | async-done | bytes 9437200 | tf_op jit(solution)/shard_map/all_gather | solution.py:64
  195.6 2.0 broadcast_in_dim.11.clone
  197.6 125.8 %while.30 = (s32[]{:T(128)}, f32[256,3072]{1,0:T(8,128)S(1)}, f32[256,3072]{1,0:T(8,128)}, s32[4]{0:T(128)S(1)}, s32[512]{0:T(512)S(1)}, /*index=5*/bf16[256,307...) while((s32[]{:T(128)}, f32[256,3072]{1,0:T(8,128)S(1)}, ...), condition=%wide.region_5.0_spmd, body=%wide.region_0.0_spmd.sunk | while | flops 7254836736 | bytes 151791664 | solution.py:86
  197.9 0.6 dynamic_slice.30
  199.1 0.6 dynamic_slice.30
  200.3 60.4 %conditional.4 = ((f32[256,3072]{1,0:T(8,128)S(1)}, f32[256,3072]{1,0:T(8,128)})) conditional(s32[]{:T(128)} %bitcast.26, (f32[256,3072]{1,0:T(8,128)S(1)}, f32[256,3072]{1,0:T(8,128)}) %tuple.75, (s32[]{:T(128)}, s32[512]{0:T(512)S(1)}, bf16[256,3072]{1,0:T(8,128)(2,1)}, bf16[3072,1536]{1,0:T(8,128)(2,1)}, bf16[3072,1536]{1,0:T(8,128)(2,1)}, ...), branch_computations={%region_1.0_spmd, %region_2.0_spmd} | conditional | flops 7254836736 | bytes 151791424 | solution.py:84
  200.4 4.3 gather_fusion.1
  204.8 8.6 %fusion = f32[128,1536]{1,0:T(8,128)} fusion(bf16[1536,3072]{1,0:T(8,128)(2,1)} %get-tuple-element.404, bf16[128,3072]{1,0:T(8,128)(2,1)} %gather_fusion.1, f32[128]{0:T(128)S(1)} %dynamic_slice.21), kind=kOutput, calls=%fused_computation.11 | convolution fusion | flops 1209139200 | bytes 11010560 | tf_op jit(solution)/shard_map/while/body/eval_jaxpr/cond/branch_1_fun/dot_general | solution.py:35
  213.4 4.3 gather_fusion
  217.7 5.5 fusion.23
  223.3 6.9 %fusion.24 = f32[128,1536]{1,0:T(8,128)} fusion(bf16[128,3072]{1,0:T(8,128)(2,1)S(1)} %copy-done, bf16[3072,1536]{1,0:T(8,128)(2,1)} %get-tuple-element.403), kind=kOutput, calls=%fused_computation.47 | convolution fusion | flops 1207959552 | bytes 11010048 | tf_op jit(solution)/shard_map/while/body/eval_jaxpr/cond/branch_1_fun/dot_general | solution.py:28
  230.2 6.2 %fusion.3 = f32[128,3072]{1,0:T(8,128)} fusion(bf16[3072,1536]{1,0:T(8,128)(2,1)S(1)} %bitcast.36, f32[128,1536]{1,0:T(8,128)S(1)} %fusion.23, f32[128,1536]{1,0:T(8,128)S(1)} %copy-done.4, f32[128,1536]{1,0:T(8,128)} %fusion.24), kind=kOutput, calls=%fused_computation.18 | convolution fusion | flops 1209925632 | bytes 13369344 | tf_op jit(solution)/shard_map/while/body/eval_jaxpr/cond/branch_1_fun/dot_general | solution.py:38
  236.4 5.7 convolution_add_fusion
  242.2 7.0 %scatter_fusion.1 = f32[256,3072]{1,0:T(8,128)} fusion(f32[256,3072]{1,0:T(8,128)} %get-tuple-element.406, s32[128]{0:T(128)S(1)} %compare_select_fusion, f32[128,3072]{1,0:T(8,128)} %convolution_add_fusion), kind=kCustom, calls=%fused_computation.5 | custom fusion | flops 393216 | bytes 4719104 | tf_op jit(solution)/shard_map/while/body/eval_jaxpr/cond/branch_1_fun/scatter-add | solution.py:42
  249.2 6.8 %convolution_multiply_fusion = f32[128,3072]{1,0:T(8,128)} fusion(bf16[1536,3072]{1,0:T(8,128)(2,1)} %get-tuple-element.404, f32[128]{0:T(128)S(1)} %dynamic_slice.21, f32[128,1536]{1,0:T(8,128)} %fusion.24, f32[128,1536]{1,0:T(8,128)} %copy-done.2), kind=kOutput, calls=%fused_computation.8 | convolution fusion | flops 1209532416 | bytes 12583424 | tf_op jit(solution)/shard_map/while/body/eval_jaxpr/cond/branch_1_fun/dot_general | solution.py:32
  256.0 4.6 scatter_fusion
  260.7 0.6 dynamic_slice.30
  261.9 0.6 dynamic_slice.30
  263.0 60.4 %conditional.4 = ((f32[256,3072]{1,0:T(8,128)S(1)}, f32[256,3072]{1,0:T(8,128)})) conditional(s32[]{:T(128)} %bitcast.26, (f32[256,3072]{1,0:T(8,128)S(1)}, f32[256,3072]{1,0:T(8,128)}) %tuple.75, (s32[]{:T(128)}, s32[512]{0:T(512)S(1)}, bf16[256,3072]{1,0:T(8,128)(2,1)}, bf16[3072,1536]{1,0:T(8,128)(2,1)}, bf16[3072,1536]{1,0:T(8,128)(2,1)}, ...), branch_computations={%region_1.0_spmd, %region_2.0_spmd} | conditional | flops 7254836736 | bytes 151791424 | solution.py:84
  263.2 4.4 gather_fusion.1
  267.7 8.1 %fusion = f32[128,1536]{1,0:T(8,128)} fusion(bf16[1536,3072]{1,0:T(8,128)(2,1)} %get-tuple-element.404, bf16[128,3072]{1,0:T(8,128)(2,1)} %gather_fusion.1, f32[128]{0:T(128)S(1)} %dynamic_slice.21), kind=kOutput, calls=%fused_computation.11 | convolution fusion | flops 1209139200 | bytes 11010560 | tf_op jit(solution)/shard_map/while/body/eval_jaxpr/cond/branch_1_fun/dot_general | solution.py:35
  275.8 4.3 gather_fusion
  280.1 5.5 fusion.23
  285.6 7.9 %fusion.24 = f32[128,1536]{1,0:T(8,128)} fusion(bf16[128,3072]{1,0:T(8,128)(2,1)S(1)} %copy-done, bf16[3072,1536]{1,0:T(8,128)(2,1)} %get-tuple-element.403), kind=kOutput, calls=%fused_computation.47 | convolution fusion | flops 1207959552 | bytes 11010048 | tf_op jit(solution)/shard_map/while/body/eval_jaxpr/cond/branch_1_fun/dot_general | solution.py:28
  293.6 5.5 fusion.3
  299.1 5.7 convolution_add_fusion
  304.9 7.0 %scatter_fusion.1 = f32[256,3072]{1,0:T(8,128)} fusion(f32[256,3072]{1,0:T(8,128)} %get-tuple-element.406, s32[128]{0:T(128)S(1)} %compare_select_fusion, f32[128,3072]{1,0:T(8,128)} %convolution_add_fusion), kind=kCustom, calls=%fused_computation.5 | custom fusion | flops 393216 | bytes 4719104 | tf_op jit(solution)/shard_map/while/body/eval_jaxpr/cond/branch_1_fun/scatter-add | solution.py:42
  311.9 6.9 %convolution_multiply_fusion = f32[128,3072]{1,0:T(8,128)} fusion(bf16[1536,3072]{1,0:T(8,128)(2,1)} %get-tuple-element.404, f32[128]{0:T(128)S(1)} %dynamic_slice.21, f32[128,1536]{1,0:T(8,128)} %fusion.24, f32[128,1536]{1,0:T(8,128)} %copy-done.2), kind=kOutput, calls=%fused_computation.8 | convolution fusion | flops 1209532416 | bytes 12583424 | tf_op jit(solution)/shard_map/while/body/eval_jaxpr/cond/branch_1_fun/dot_general | solution.py:32
  318.8 4.6 scatter_fusion
  323.5 55.3 %all-gather.23.cloned.1.call-done = bf16[1,1536,3072]{2,1,0:T(8,128)(2,1)} async-done(((bf16[1,1536,384]{2,1,0:T(8,128)(2,1)}), bf16[1,1536,3072]{2,1,0:T(8,128)(2,1)}) %all-gather.23.cloned.1.call-update) | async-done | bytes 9437200 | tf_op jit(solution)/shard_map/all_gather | solution.py:64
  378.8 16.8 %while.31 = (s32[]{:T(128)}, f32[256,3072]{1,0:T(8,128)S(1)}, f32[256,3072]{1,0:T(8,128)}, s32[4]{0:T(128)S(1)}, s32[512]{0:T(512)S(1)}, /*index=5*/bf16[256,307...) while((s32[]{:T(128)}, f32[256,3072]{1,0:T(8,128)S(1)}, ...), condition=%wide.region_11.0_spmd, body=%wide.region_6.0_spmd.sunk | while | flops 7254836736 | bytes 151791664 | solution.py:86
  390.5 0.6 dynamic_slice.31
  391.7 0.6 dynamic_slice.31
  393.0 0.6 dynamic_slice.31
  394.3 0.6 dynamic_slice.31
  395.6 1.4 convert_element_type.76
  397.0 3.3 convert_element_type.77
  400.3 147.7 %reduce-scatter.3.cloned.1.call-done = bf16[256,768]{1,0:T(8,128)(2,1)} async-done(((bf16[256,3072]{1,0:T(8,128)(2,1)}), bf16[256,768]{1,0:T(8,128)(2,1)}) %reduce-scatter.3.cloned.1.call-update) | async-done | bytes 393232 | tf_op jit(solution)/shard_map/reduce_scatter | solution.py:88
  548.1 37.2 %reduce-scatter.5.cloned.1.call-done = bf16[256,768]{1,0:T(8,128)(2,1)} async-done(((bf16[256,3072]{1,0:T(8,128)(2,1)}), bf16[256,768]{1,0:T(8,128)(2,1)}) %reduce-scatter.5.cloned.1.call-update) | async-done | bytes 393232 | tf_op jit(solution)/shard_map/reduce_scatter | solution.py:91
  (77 shorter events, 2.3 us)
Async XLA Ops:
  7.2 64.8 %all-gather.13.cloned.1.call-start = ((), (), s32[]{:S(2)}) async-start(), calls=%async_computation.4 | async-start | bytes 10616832 | tf_op jit(solution)/shard_map/all_gather | solution.py:61
  11.4 121.3 %all-gather.15.cloned.1.call-start = ((), (), s32[]{:S(2)}) async-start(), calls=%async_computation.5 | async-start | bytes 10616832 | tf_op jit(solution)/shard_map/all_gather | solution.py:62
  15.7 179.5 %all-gather.17.cloned.1.call-start = ((), (), s32[]{:S(2)}) async-start(), calls=%async_computation.6 | async-start | bytes 10616832 | tf_op jit(solution)/shard_map/all_gather | solution.py:64
  20.0 1.8 copy-start.6
  20.1 303.4 %all-gather.19.cloned.1.call-start = ((), (), s32[]{:S(2)}) async-start(), calls=%async_computation.7 | async-start | bytes 10616832 | tf_op jit(solution)/shard_map/all_gather | solution.py:61
  20.6 302.9 %all-gather.21.cloned.1.call-start = ((), (), s32[]{:S(2)}) async-start(), calls=%async_computation.8 | async-start | bytes 10616832 | tf_op jit(solution)/shard_map/all_gather | solution.py:62
  21.2 357.6 %all-gather.23.cloned.1.call-start = ((), (), s32[]{:S(2)}) async-start(), calls=%async_computation.9 | async-start | bytes 10616832 | tf_op jit(solution)/shard_map/all_gather | solution.py:64
  21.8 526.3 %reduce-scatter.3.cloned.1.call-start = ((), (), s32[]{:S(2)}) async-start(), calls=%async_computation.2 | async-start | bytes 1966080 | tf_op jit(solution)/shard_map/reduce_scatter | solution.py:88
  195.2 2.4 copy-start.7
  195.2 2.4 copy-start.8
  217.7 5.5 copy-start
  217.7 12.4 %slice-start.6 = ((s8[9437184]{0:T(1024)(128)(4,1)}), s8[4194304]{0:T(1024)(128)(4,1)S(1)}, s32[]{:S(2)}) async-start(s8[9437184]{0:T(1024)(128)(4,1)} %bitcast.35), calls=%async_computation.16 | async-start | bytes 8388608 | tf_op jit(solution)/shard_map/while/body/eval_jaxpr/cond
  217.7 12.4 %slice-start.7 = ((s8[9437184]{0:T(1024)(128)(4,1)}), s8[4194304]{0:T(1024)(128)(4,1)S(1)}, s32[]{:S(2)}) async-start(s8[9437184]{0:T(1024)(128)(4,1)} %bitcast.35), calls=%async_computation.17 | async-start | bytes 8388608 | tf_op jit(solution)/shard_map/while/body/eval_jaxpr/cond
  223.2 13.2 %copy-start.2 = (f32[128,1536]{1,0:T(8,128)}, f32[128,1536]{1,0:T(8,128)S(1)}, u32[]{:S(2)}) copy-start(f32[128,1536]{1,0:T(8,128)S(1)} %fusion.23) | copy-start | bytes 2359300 | tf_op jit(solution)/shard_map/while/body/eval_jaxpr/cond
  223.2 6.9 %slice-start.8 = ((s8[9437184]{0:T(1024)(128)(4,1)}), s8[1048576]{0:T(1024)(128)(4,1)S(1)}, s32[]{:S(2)}) async-start(s8[9437184]{0:T(1024)(128)(4,1)} %bitcast.35), calls=%async_computation.18 | async-start | bytes 2097152 | tf_op jit(solution)/shard_map/while/body/eval_jaxpr/cond
  223.2 6.9 %copy-start.4 = (f32[128,1536]{1,0:T(8,128)S(1)}, f32[128,1536]{1,0:T(8,128)}, u32[]{:S(2)}) copy-start(f32[128,1536]{1,0:T(8,128)} %fusion) | copy-start | bytes 2359300 | tf_op jit(solution)/shard_map/while/body/eval_jaxpr/cond
  223.2 13.2 %slice-start.9 = ((s8[9437184]{0:T(1024)(128)(4,1)}), s8[4194304]{0:T(1024)(128)(4,1)S(1)}, s32[]{:S(2)}) async-start(s8[9437184]{0:T(1024)(128)(4,1)} %bitcast.38), calls=%async_computation.19 | async-start | bytes 8388608 | tf_op jit(solution)/shard_map/while/body/eval_jaxpr/cond
  223.2 13.2 %slice-start.10 = ((s8[9437184]{0:T(1024)(128)(4,1)}), s8[4194304]{0:T(1024)(128)(4,1)S(1)}, s32[]{:S(2)}) async-start(s8[9437184]{0:T(1024)(128)(4,1)} %bitcast.38), calls=%async_computation.20 | async-start | bytes 8388608 | tf_op jit(solution)/shard_map/while/body/eval_jaxpr/cond
  230.1 6.3 %slice-start.11 = ((s8[9437184]{0:T(1024)(128)(4,1)}), s8[1048576]{0:T(1024)(128)(4,1)S(1)}, s32[]{:S(2)}) async-start(s8[9437184]{0:T(1024)(128)(4,1)} %bitcast.38), calls=%async_computation.21 | async-start | bytes 2097152 | tf_op jit(solution)/shard_map/while/body/eval_jaxpr/cond
  280.1 5.5 copy-start
  280.1 13.5 %slice-start.6 = ((s8[9437184]{0:T(1024)(128)(4,1)}), s8[4194304]{0:T(1024)(128)(4,1)S(1)}, s32[]{:S(2)}) async-start(s8[9437184]{0:T(1024)(128)(4,1)} %bitcast.35), calls=%async_computation.16 | async-start | bytes 8388608 | tf_op jit(solution)/shard_map/while/body/eval_jaxpr/cond
  280.1 13.5 %slice-start.7 = ((s8[9437184]{0:T(1024)(128)(4,1)}), s8[4194304]{0:T(1024)(128)(4,1)S(1)}, s32[]{:S(2)}) async-start(s8[9437184]{0:T(1024)(128)(4,1)} %bitcast.35), calls=%async_computation.17 | async-start | bytes 8388608 | tf_op jit(solution)/shard_map/while/body/eval_jaxpr/cond
  285.5 13.6 %copy-start.2 = (f32[128,1536]{1,0:T(8,128)}, f32[128,1536]{1,0:T(8,128)S(1)}, u32[]{:S(2)}) copy-start(f32[128,1536]{1,0:T(8,128)S(1)} %fusion.23) | copy-start | bytes 2359300 | tf_op jit(solution)/shard_map/while/body/eval_jaxpr/cond
  285.6 8.0 %slice-start.8 = ((s8[9437184]{0:T(1024)(128)(4,1)}), s8[1048576]{0:T(1024)(128)(4,1)S(1)}, s32[]{:S(2)}) async-start(s8[9437184]{0:T(1024)(128)(4,1)} %bitcast.35), calls=%async_computation.18 | async-start | bytes 2097152 | tf_op jit(solution)/shard_map/while/body/eval_jaxpr/cond
  285.6 8.0 %copy-start.4 = (f32[128,1536]{1,0:T(8,128)S(1)}, f32[128,1536]{1,0:T(8,128)}, u32[]{:S(2)}) copy-start(f32[128,1536]{1,0:T(8,128)} %fusion) | copy-start | bytes 2359300 | tf_op jit(solution)/shard_map/while/body/eval_jaxpr/cond
  285.6 13.5 %slice-start.9 = ((s8[9437184]{0:T(1024)(128)(4,1)}), s8[4194304]{0:T(1024)(128)(4,1)S(1)}, s32[]{:S(2)}) async-start(s8[9437184]{0:T(1024)(128)(4,1)} %bitcast.38), calls=%async_computation.19 | async-start | bytes 8388608 | tf_op jit(solution)/shard_map/while/body/eval_jaxpr/cond
  285.6 13.5 %slice-start.10 = ((s8[9437184]{0:T(1024)(128)(4,1)}), s8[4194304]{0:T(1024)(128)(4,1)S(1)}, s32[]{:S(2)}) async-start(s8[9437184]{0:T(1024)(128)(4,1)} %bitcast.38), calls=%async_computation.20 | async-start | bytes 8388608 | tf_op jit(solution)/shard_map/while/body/eval_jaxpr/cond
  293.6 5.5 slice-start.11
  397.0 188.2 %reduce-scatter.5.cloned.1.call-start = ((), (), s32[]{:S(2)}) async-start(), calls=%async_computation.3 | async-start | bytes 1966080 | tf_op jit(solution)/shard_map/reduce_scatter | solution.py:91
Sparse Core Ops, SparseCore 0:
  11.6 60.3 all-gather.12
  73.9 58.8 all-gather.14
  134.6 60.5 all-gather.16
  197.0 58.8 all-gather.18
  257.6 58.8 all-gather.20
  318.2 60.5 all-gather.22
  397.1 150.9 reduce-scatter.2
  550.9 34.2 reduce-scatter.4
where the time goes:
time: 594 us; the launch traced here: 592 us
  waiting for transfers between devices  415 us (70%)
  matrix products  79.4 us (13%)
  other arithmetic  36 us (6%)
  local copies, waits for them, and re-layouts  29.6 us (5%)
  loops' own time  17.4 us (3%)
  between operations  14.4 us (2%)
    reduce_scatter x1, waiting for transfers between devices, shards(): lax.psum_scatter(totals[0].astype(jnp.bfloat16), 'etp', scatter_dimension...  148 us
    all_gather x2, waiting for transfers between devices, shards(): down_mat = lax.all_gather(down_low[expert], 'dp', axis=1, tiled=True)  118 us
    all_gather x2, waiting for transfers between devices, shards(): lax.all_gather(up_low[expert], 'dp', axis=0, tiled=True)  60.8 us
    all_gather x2, waiting for transfers between devices, shards(): lax.all_gather(gate_low[expert], 'dp', axis=0, tiled=True)  50.1 us
    reduce_scatter x1, waiting for transfers between devices, shards(): lax.psum_scatter(totals[1].astype(jnp.bfloat16), 'etp', scatter_dimension...  37.2 us
    another operation x2, loops' own time, shards(): totals = lax.fori_loop(0, block_count, visit_one, totals)  17 us
    dot_general x2, matrix products, block_terms(): lax.dot_general(d_out, down_mat, contract_last, preferred_element_type=jn...  16.7 us
    dot_general x2, matrix products, block_terms(): up_pre = jnp.dot(inputs, up_mat, preferred_element_type=jnp.float32)  14.8 us
  transfers between devices with their start and end apart: 8, of which 6 were waited for; matrix products, arithmetic and copies ran while one was open for 23% of the time, Pallas kernels for 0%

commit v1 on v0

v1 whole, which is shorter than its diff:
```python
import functools

import jax
import jax.numpy as jnp
from jax import lax
from jax.experimental import pallas as pl
from jax.experimental.pallas import tpu as pltpu
from jax.sharding import PartitionSpec as P

gate_steps = 16.0
vmem_limit = 48 * 1024 * 1024
shares = 4


def swap(value, mask, size):
    return lax.ppermute(value, "dp", [(i, i ^ mask) for i in range(size)])


def steps_of(rows):
    return max(step for step in (1, 2, 4) if rows % (16 * step) == 0)


def cast_rows_kernel(pick_ref, gate_ref, up_ref, *out_refs):
    parts = shares // gate_ref.shape[0]
    width = out_refs[0].shape[-1]
    for share, out_ref in enumerate(out_refs):
        expert = pick_ref[share] // parts
        lanes = pl.ds(pl.multiple_of(pick_ref[share] % parts * width, 128), width)
        out_ref[0] = gate_ref[expert, :, lanes].astype(jnp.bfloat16)
        out_ref[1] = up_ref[expert, :, lanes].astype(jnp.bfloat16)


def cast_rows(pick, w_gate, w_up):
    experts, rows, hidden = w_gate.shape
    width = experts * hidden // shares
    steps = steps_of(rows)
    block = pl.BlockSpec((experts, rows // steps, hidden), lambda i, pick: (0, i, 0))
    return pl.pallas_call(
        cast_rows_kernel,
        grid_spec=pltpu.PrefetchScalarGridSpec(
            num_scalar_prefetch=1,
            grid=(steps,),
            in_specs=[block, block],
            out_specs=[pl.BlockSpec((2, rows // steps, width), lambda i, pick: (0, i, 0))] * shares,
        ),
        out_shape=[jax.ShapeDtypeStruct((2, rows, width), jnp.bfloat16)] * shares,
        compiler_params=pltpu.CompilerParams(vmem_limit_bytes=vmem_limit),
        name="cast_rows",
    )(pick, w_gate, w_up)


def cast_turned_kernel(pick_ref, down_ref, *out_refs):
    parts = shares // down_ref.shape[0]
    width = out_refs[0].shape[-1]
    for share, out_ref in enumerate(out_refs):
        expert = pick_ref[share] // parts
        rows = pl.ds(pl.multiple_of(pick_ref[share] % parts * width, 128), width)
        out_ref[...] = down_ref[expert, rows, :].T.astype(jnp.bfloat16)


def cast_turned(pick, w_down):
    experts, hidden, features = w_down.shape
    width = experts * hidden // shares
    tile = 128 if features % 128 == 0 else features
    return pl.pallas_call(
        cast_turned_kernel,
        grid_spec=pltpu.PrefetchScalarGridSpec(
            num_scalar_prefetch=1,
            grid=(features // tile,),
            in_specs=[pl.BlockSpec((experts, hidden, tile), lambda i, pick: (0, 0, i))],
            out_specs=[pl.BlockSpec((tile, width), lambda i, pick: (i, 0))] * shares,
        ),
        out_shape=[jax.ShapeDtypeStruct((features, width), jnp.bfloat16)] * shares,
        compiler_params=pltpu.CompilerParams(vmem_limit_bytes=vmem_limit),
        name="cast_turned",
    )(pick, w_down)


def token_scales(slot_token, slot_gate, block_expert, experts, token_count):
    block_rows = slot_token.shape[0] // block_expert.shape[0]
    scale = slot_gate.astype(jnp.float32) / gate_steps
    slot_expert = jnp.repeat(block_expert, block_rows)
    weight = jnp.where(slot_expert[None, :] == jnp.arange(experts)[:, None], scale[None, :], 0.0)
    hot = (slot_token[:, None] == jnp.arange(token_count)[None, :]).astype(jnp.bfloat16)
    return jnp.dot(weight.astype(jnp.bfloat16), hot, preferred_element_type=jnp.float32)


def shards(n, m, tokens, cotangent, w_gate, w_up, w_down, slot_token, slot_gate, block_expert):
    experts, rows, hidden = w_gate.shape
    width = experts * hidden // shares
    features = tokens.shape[1]
    count = tokens.shape[0]
    me = lax.axis_index("dp")
    top = n // 2
    masks = [0, 1, top, top + 1]
    gather_bits = [1 << i for i in range(1, n.bit_length() - 2)]
    mine = (me & 1) + 2 * (me // top)
    pick = jnp.stack([mine ^ share for share in range(shares)]).astype(jnp.int32)
    low, high = (((1,), (0,)), ((), ())), (((1,), (1,)), ((), ()))
    dot = functools.partial(lax.dot_general, preferred_element_type=jnp.float32)

    def spread(pieces):
        blocks = {masks[0]: pieces[0]}
        for share in range(1, shares):
            blocks[masks[share]] = swap(pieces[share], masks[share], n)
        for bit in gather_bits:
            for key in list(blocks):
                blocks[key ^ bit] = swap(blocks[key], bit, n)
        return blocks

    both = spread(cast_rows(pick, w_gate, w_up))
    turned = spread(cast_turned(pick, w_down))

    scale = token_scales(slot_token, slot_gate, block_expert, experts, count)

    def share_tokens(value):
        far = swap(value, top, n)
        pair = jnp.concatenate([value, far])
        near = swap(pair, 1, n)
        return jnp.concatenate([value, near[:count], far, near[count:]])

    x = share_tokens(tokens)
    u = share_tokens(cotangent)
    s = lax.dynamic_slice_in_dim(share_tokens(scale.T), mine // (shares // experts), 1, 1)

    full = jnp.zeros((2, features, width), jnp.bfloat16)
    for key, block in both.items():
        full = lax.dynamic_update_slice(full, block, (0, (me ^ key) * rows, 0))
    full_down = jnp.zeros((features, width), jnp.bfloat16)
    for key, block in turned.items():
        full_down = lax.dynamic_update_slice(full_down, block, ((me ^ key) * rows, 0))

    gate_pre = dot(x, full[0], low)
    up_pre = dot(x, full[1], low)
    squash = jax.nn.sigmoid(gate_pre)
    active = gate_pre * squash
    hid = (active * up_pre * s).astype(jnp.bfloat16)
    produced = dot(hid, full_down, high).astype(jnp.bfloat16)
    d_hidden = dot(u, full_down, low) * s
    d_pre = (d_hidden * up_pre * squash * (1.0 + gate_pre * (1.0 - squash))).astype(jnp.bfloat16)
    d_up = (d_hidden * active).astype(jnp.bfloat16)
    backward = (dot(d_pre, full[0], high) + dot(d_up, full[1], high)).astype(jnp.bfloat16)

    wide = jnp.float32

    def reduce(partial):
        parts = partial.reshape(shares, count, features)
        near = swap(jnp.stack([parts[1], parts[3]]), 1, n)
        own = parts[0].astype(wide) + near[0].astype(wide)
        other = (parts[2].astype(wide) + near[1].astype(wide)).astype(jnp.bfloat16)
        own = own + swap(other, top, n).astype(wide)
        z = lax.axis_index("etp")
        columns = features // m
        total = lax.dynamic_slice_in_dim(own, z * columns, columns, 1)
        low_own = own.astype(jnp.bfloat16)
        for step in range(1, m):
            target = lax.rem(z + step, m)
            part = lax.dynamic_slice_in_dim(low_own, target * columns, columns, 1)
            got = lax.ppermute(part, "etp", [(i, (i + step) % m) for i in range(m)])
            total = total + got.astype(wide)
        return total.astype(jnp.bfloat16)

    return reduce(produced), reduce(backward)


def solution(mesh):
    in_specs = (
        P("dp", None),
        P("dp", None),
        P(None, "dp", "etp"),
        P(None, "dp", "etp"),
        P(None, "etp", "dp"),
        P("dp"),
        P("dp"),
        P("dp"),
    )
    out_specs = (P("dp", "etp"), P("dp", "etp"))
    body = functools.partial(shards, mesh.shape["dp"], mesh.shape["etp"])
    return jax.shard_map(body, mesh=mesh, in_specs=in_specs, out_specs=out_specs, check_vma=False)
```

time: 594 us -> 421 us (0.71)
  waiting for transfers between devices: 415 us -> 247 us
  starting transfers between devices: 0.32 us -> 37.8 us
  matrix products: 79.4 us -> 60 us
  loops' own time: 17.4 us -> 0 us
  between operations: 14.4 us -> 0.9 us
  other arithmetic: 36 us -> 25.6 us
  Pallas kernels: 0 us -> 9.84 us
  local copies, waits for them, and re-layouts: 29.6 us -> 36.4 us
    ppermute x0 -> x30, waiting for transfers between devices: none -> 247 us  [the longest x24 218 us: swap(): return lax.ppermute(value, 'dp', [(i, i ^ mask) for i in range(size)])]
    all_gather x6 -> x0, waiting for transfers between devices: 229 us -> none  [the longest x2 118 us: shards(): down_mat = lax.all_gather(down_low[expert], 'dp', axis=1, tiled=True)]
    reduce_scatter x2 -> x0, waiting for transfers between devices: 185 us -> none  [the longest x1 148 us: shards(): lax.psum_scatter(totals[0].astype(jnp.bfloat16), 'etp', scatter_dimension...]
    ppermute x0 -> x30, starting transfers between devices: none -> 37.8 us  [the longest x24 28.4 us: swap(): return lax.ppermute(value, 'dp', [(i, i ^ mask) for i in range(size)])]
    scatter-add x4 -> x0, other arithmetic: 23.3 us -> none  [the longest x2 14.1 us: block_terms(): dx_total.at[token_rows].add(backward)]
    dot_general x12 -> x7, matrix products: 79.4 us -> 60 us  [the longest x1 17.3 us: shards(): dot(d_pre, full[0], high) + dot(d_up, full[1], high)]
    gather x4 -> x0, local copies, waits for them, and re-layouts: 17.4 us -> none  [the longest x2 8.76 us: block_terms(): upstream = cotangent[token_rows]]
    another operation x10 -> x0, loops' own time: 17.4 us -> none  [the longest x2 17 us: shards(): totals = lax.fori_loop(0, block_count, visit_one, totals)]
  transfers between devices with their start and end apart: 8 -> 30, of which waited for: 6 -> 14; matrix products, arithmetic and copies ran while one was open for 23% -> 27% of each run, Pallas kernels for 0% -> 2%
where the time goes in v1:
time: 421 us; the launch traced here: 418 us
  waiting for transfers between devices  247 us (59%)
  matrix products  60 us (14%)
  starting transfers between devices  37.8 us (9%)
  local copies, waits for them, and re-layouts  36.4 us (9%)
  other arithmetic  25.6 us (6%)
  Pallas kernels  9.84 us (2%)
    ppermute x24, waiting for transfers between devices, swap(): return lax.ppermute(value, 'dp', [(i, i ^ mask) for i in range(size)])  218 us
    ppermute x6, waiting for transfers between devices, reduce(): got = lax.ppermute(part, 'etp', [(i, (i + step) % m) for i in range(m)])  29.4 us
    ppermute x24, starting transfers between devices, swap(): return lax.ppermute(value, 'dp', [(i, i ^ mask) for i in range(size)])  28.4 us
    dot_general x1, matrix products, shards(): dot(d_pre, full[0], high) + dot(d_up, full[1], high)  17.3 us
    dynamic_update_slice x8, local copies, waits for them, and re-layouts, shards(): full = lax.dynamic_update_slice(full, block, (0, (me ^ key) * rows, 0))  11.4 us
    dot_general x1, matrix products, shards(): dot(d_up, full[1], high)  11 us
    dot_general x1, matrix products, shards(): up_pre = dot(x, full[1], low)  9.55 us
    ppermute x6, starting transfers between devices, reduce(): got = lax.ppermute(part, 'etp', [(i, (i + step) % m) for i in range(m)])  9.35 us
  transfers between devices with their start and end apart: 30, of which 14 were waited for; matrix products, arithmetic and copies ran while one was open for 27% of the time, Pallas kernels for 2%

profile of v1, /device:TPU:11, one launch (start us, length us, event | category | flops | bytes accessed | tf_op | source)
XLA Modules:
  0.0 417.6 jit_solution(16088091324875528640)
XLA Ops:
  2.0 4.0 cast_turned.1
  7.3 1.5 collective-permute-start.13
  9.4 52.2 %collective-permute-done.9 = f32[256,2]{0,1:T(2,128)S(1)} collective-permute-done((f32[256,2]{0,1:T(2,128)S(1)}, f32[256,2]{0,1:T(2,128)S(1)}, u32[]{:S(2)}, u32[]{:S(2)}) %collective-permute-start.9) | collective-permute-done | bytes 2080 | tf_op jit(solution)/shard_map/ppermute | solution.py:16
  61.6 1.5 collective-permute-start.10
  63.1 5.9 %cast_rows.1 = (bf16[2,384,768]{2,1,0:T(8,128)(2,1)S(1)}, bf16[2,384,768]{2,1,0:T(8,128)(2,1)}, bf16[2,384,768]{2,1,0:T(8,128)(2,1)S(1)}, bf16[2,384,768]{2,1,0:T(8,128)(2,1)S(1)}) custom-call(s32[4]{0:T(128)S(1)} %pad_add_fusion.pick_ref, f32[2,384,1536]{2,1,0:T(8,128)} %gate_ref.1, f32[2,384,1536]{2,1,0:T(8,128)} %up_ref.1), custom_call_target="tpu_custom_call" | custom-call | tf_op jit(solution)/shard_map/cast_rows/pallas_call | solution.py:38
  72.0 3.6 pad_maximum_fusion.1
  75.6 7.9 %collective-permute-done.14 = bf16[384,768]{1,0:T(8,128)(2,1)S(1)} collective-permute-done((bf16[384,768]{1,0:T(8,128)(2,1)S(1)}, bf16[384,768]{1,0:T(8,128)(2,1)S(1)}, u32[]{:S(2)}, u32[]{:S(2)}) %collective-permute-start.14) | collective-permute-done | bytes 589856 | tf_op jit(solution)/shard_map/ppermute | solution.py:16
  84.4 2.1 collective-permute-start.1
  86.5 9.8 %collective-permute-done.15 = bf16[384,768]{1,0:T(8,128)(2,1)} collective-permute-done((bf16[384,768]{1,0:T(8,128)(2,1)S(1)}, bf16[384,768]{1,0:T(8,128)(2,1)}, u32[]{:S(2)}, u32[]{:S(2)}) %collective-permute-start.15) | collective-permute-done | bytes 589856 | tf_op jit(solution)/shard_map/ppermute | solution.py:16
  97.6 4.2 %broadcast_in_dim.25 = bf16[2,3072,768]{2,1,0:T(8,128)(2,1)} broadcast(bf16[]{:T(256)} %constant.47.clone.1), dimensions={} | broadcast | bytes 9437186 | tf_op jit(solution)/shard_map/broadcast_in_dim | solution.py:126
  102.9 6.1 %collective-permute-done.16 = bf16[384,768]{1,0:T(8,128)(2,1)} collective-permute-done((bf16[384,768]{1,0:T(8,128)(2,1)}, bf16[384,768]{1,0:T(8,128)(2,1)}, u32[]{:S(2)}, u32[]{:S(2)}) %collective-permute-start.16) | collective-permute-done | bytes 589856 | tf_op jit(solution)/shard_map/ppermute | solution.py:16
  109.0 3.3 collective-permute-start.4
  112.6 9.0 %collective-permute-done.17 = bf16[384,768]{1,0:T(8,128)(2,1)} collective-permute-done((bf16[384,768]{1,0:T(8,128)(2,1)}, bf16[384,768]{1,0:T(8,128)(2,1)}, u32[]{:S(2)}, u32[]{:S(2)}) %collective-permute-start.17) | collective-permute-done | bytes 589856 | tf_op jit(solution)/shard_map/ppermute | solution.py:16
  125.5 2.4 constant_dynamic-update-slice_fusion.14
  130.2 22.2 %collective-permute-done.4 = bf16[2,384,768]{2,1,0:T(8,128)(2,1)S(1)} collective-permute-done((bf16[2,384,768]{2,1,0:T(8,128)(2,1)S(1)}, bf16[2,384,768]{2,1,0:T(8,128)(2,1)S(1)}, u32[]{:S(2)}, u32[]{:S(2)}) %collective-permute-start.4) | collective-permute-done | bytes 1179680 | tf_op jit(solution)/shard_map/ppermute | solution.py:16
  156.2 2.4 constant_dynamic-update-slice_fusion.13
  160.7 20.1 %collective-permute-done.23 = bf16[256,3072]{1,0:T(8,128)(2,1)S(1)} collective-permute-done((bf16[256,3072]{1,0:T(8,128)(2,1)S(1)}, bf16[256,3072]{1,0:T(8,128)(2,1)S(1)}, u32[]{:S(2)}, u32[]{:S(2)}) %collective-permute-start.23) | collective-permute-done | bytes 1572896 | tf_op jit(solution)/shard_map/ppermute | solution.py:16
  182.2 3.1 collective-permute-start.24
  186.5 11.8 %collective-permute-done.7 = bf16[2,384,768]{2,1,0:T(8,128)(2,1)S(1)} collective-permute-done((bf16[2,384,768]{2,1,0:T(8,128)(2,1)}, bf16[2,384,768]{2,1,0:T(8,128)(2,1)S(1)}, u32[]{:S(2)}, u32[]{:S(2)}) %collective-permute-start.7) | collective-permute-done | bytes 1179680 | tf_op jit(solution)/shard_map/ppermute | solution.py:16
  199.5 24.2 %collective-permute-done.8 = bf16[2,384,768]{2,1,0:T(8,128)(2,1)S(1)} collective-permute-done((bf16[2,384,768]{2,1,0:T(8,128)(2,1)S(1)}, bf16[2,384,768]{2,1,0:T(8,128)(2,1)S(1)}, u32[]{:S(2)}, u32[]{:S(2)}) %collective-permute-start.8) | collective-permute-done | bytes 1179680 | tf_op jit(solution)/shard_map/ppermute | solution.py:16
  224.8 2.2 fusion.44
  227.1 9.6 %fusion.10 = f32[1024,768]{1,0:T(8,128)} fusion(bf16[2,3072,768]{2,1,0:T(8,128)(2,1)} %constant_dynamic-update-slice_fusion.8, bf16[256,3072]{1,0:T(8,128)(2,1)S(1)} %get-tuple-element.29, bf16[256,3072]{1,0:T(8,128)(2,1)} %collective-permute-done, bf16[256,3072]{1,0:T(8,128)(2,1)S(1)} %get-tuple-element.28, bf16[256,3072]{1,0:T(8,128)(2,1)S(1)} %copy-done.8), kind=kOutput, calls=%fused_computation.15 | convolution fusion | flops 4857004032 | bytes 14155776 | tf_op jit(solution)/shard_map/dot_general | solution.py:134
  236.7 7.8 %fusion.8 = f32[1024,768]{1,0:T(8,128)S(1)} fusion(bf16[2,3072,768]{2,1,0:T(8,128)(2,1)} %constant_dynamic-update-slice_fusion.8, bf16[256,3072]{1,0:T(8,128)(2,1)S(1)} %get-tuple-element.29, bf16[256,3072]{1,0:T(8,128)(2,1)} %collective-permute-done, bf16[256,3072]{1,0:T(8,128)(2,1)S(1)} %get-tuple-element.28, bf16[256,3072]{1,0:T(8,128)(2,1)S(1)} %copy-done.8), kind=kOutput, calls=%fused_computation.13 | convolution fusion | flops 4857004032 | bytes 14155776 | tf_op jit(solution)/shard_map/dot_general | solution.py:133
  244.5 9.1 %convolution_convert_fusion = bf16[1024,3072]{1,0:T(8,128)(2,1)S(1)} fusion(bf16[3072,768]{1,0:T(8,128)(2,1)S(1)} %constant_dynamic-update-slice_fusion, f32[1024,768]{1,0:T(8,128)} %fusion.10, f32[1024]{0:T(1024)S(1)} %bitcast.47, f32[1024,768]{1,0:T(8,128)S(1)} %fusion.8), kind=kOutput, calls=%fused_computation.10 | convolution fusion | flops 4840488960 | bytes 17305600 | tf_op jit(solution)/shard_map/dot_general | solution.py:138
  253.8 2.4 copy-done.3
  256.2 1.9 pad_maximum_fusion.2
  258.1 2.2 collective-permute-start.18
  260.6 5.0 %fusion = f32[1024,768]{1,0:T(8,128)S(1)} fusion(bf16[3072,768]{1,0:T(8,128)(2,1)S(1)} %constant_dynamic-update-slice_fusion, bf16[256,3072]{1,0:T(8,128)(2,1)S(1)} %get-tuple-element.27, bf16[256,3072]{1,0:T(8,128)(2,1)S(1)} %copy-done.11, bf16[256,3072]{1,0:T(8,128)(2,1)S(1)} %get-tuple-element.26, bf16[256,3072]{1,0:T(8,128)(2,1)S(1)} %copy-done.9), kind=kOutput, calls=%fused_computation.2 | convolution fusion | flops 4857004032 | bytes 14155776 | tf_op jit(solution)/shard_map/dot_general | solution.py:139
  265.6 1.7 copy-done.18
  267.3 11.0 %fusion.9 = f32[1024,3072]{1,0:T(8,128)} fusion(bf16[2,3072,768]{2,1,0:T(8,128)(2,1)} %constant_dynamic-update-slice_fusion.8, f32[1024,768]{1,0:T(8,128)S(1)} %fusion, f32[1024]{0:T(1024)S(1)} %bitcast.48, f32[1024,768]{1,0:T(8,128)S(1)} %copy-done.17), kind=kOutput, calls=%fused_computation.14 | convolution fusion | flops 4837343232 | bytes 23597056 | tf_op jit(solution)/shard_map/dot_general | solution.py:142
  278.3 17.3 %add_convert_fusion = bf16[1024,3072]{1,0:T(8,128)(2,1)} fusion(f32[1024,3072]{1,0:T(8,128)} %fusion.9, bf16[2,3072,768]{2,1,0:T(8,128)(2,1)} %constant_dynamic-update-slice_fusion.8, f32[1024,768]{1,0:T(8,128)} %copy-done.16, f32[1024,768]{1,0:T(8,128)} %fusion.10, f32[1024,768]{1,0:T(8,128)} %copy-done.18, f32[1024]{0:T(1024)S(1)} %bitcast.49), kind=kOutput, calls=%fused_computation | convolution fusion | flops 4846780416 | bytes 33034240 | tf_op jit(solution)/shard_map/dot_general | solution.py:142
  295.6 2.1 slice_bitcast_fusion.9
  299.2 4.4 %fusion.13 = bf16[256,3072]{1,0:T(8,128)(2,1)} fusion(bf16[2,256,3072]{2,1,0:T(8,128)(2,1)S(1)} %collective-permute-done.18, bf16[1024,3072]{1,0:T(8,128)(2,1)} %copy-done.3), kind=kLoop, calls=%fused_computation.25 | loop fusion | flops 3145728 | bytes 4718592 | tf_op jit(solution)/shard_map/convert_element_type | solution.py:150
  304.8 1.6 copy-done.5
  306.4 3.0 fusion.11
  310.4 29.5 %collective-permute-done.19 = bf16[256,3072]{1,0:T(8,128)(2,1)} collective-permute-done((bf16[256,3072]{1,0:T(8,128)(2,1)}, bf16[256,3072]{1,0:T(8,128)(2,1)}, u32[]{:S(2)}, u32[]{:S(2)}) %collective-permute-start.19) | collective-permute-done | bytes 1572896 | tf_op jit(solution)/shard_map/ppermute | solution.py:16
  339.9 3.3 fusion.41
  344.4 2.3 collective-permute-start.21
  346.7 2.2 collective-permute-start.20
  348.9 24.7 %collective-permute-done.26 = bf16[256,3072]{1,0:T(8,128)(2,1)} collective-permute-done((bf16[256,3072]{1,0:T(8,128)(2,1)}, bf16[256,3072]{1,0:T(8,128)(2,1)}, u32[]{:S(2)}, u32[]{:S(2)}) %collective-permute-start.26) | collective-permute-done | bytes 1572896 | tf_op jit(solution)/shard_map/ppermute | solution.py:16
  373.6 4.3 %fusion.39 = (bf16[256,3072]{1,0:T(8,128)(2,1)S(1)}, f32[256,3072]{1,0:T(8,128)}) fusion(bf16[256,3072]{1,0:T(8,128)(2,1)} %collective-permute-done.26, bf16[2,256,3072]{2,1,0:T(8,128)(2,1)S(1)} %copy-done.6, bf16[1024,3072]{1,0:T(8,128)(2,1)} %add_convert_fusion), kind=kLoop, calls=%fused_computation.95 | loop fusion | flops 4718592 | bytes 9437184 | tf_op jit(solution)/shard_map/convert_element_type | solution.py:155
  379.2 2.3 collective-permute-start.28
  381.5 2.2 collective-permute-start.27
  383.7 2.1 add_convert_fusion.2
  385.8 3.4 collective-permute-done.29
  389.2 17.6 %collective-permute-done.28 = bf16[256,768]{1,0:T(8,128)(2,1)} collective-permute-done((bf16[256,768]{1,0:T(8,128)(2,1)}, bf16[256,768]{1,0:T(8,128)(2,1)}, u32[]{:S(2)}, u32[]{:S(2)}) %collective-permute-start.28) | collective-permute-done | bytes 393248 | tf_op jit(solution)/shard_map/ppermute | solution.py:159
  406.8 8.4 %collective-permute-done.27 = bf16[256,768]{1,0:T(8,128)(2,1)} collective-permute-done((bf16[256,768]{1,0:T(8,128)(2,1)}, bf16[256,768]{1,0:T(8,128)(2,1)}, u32[]{:S(2)}, u32[]{:S(2)}) %collective-permute-start.27) | collective-permute-done | bytes 393248 | tf_op jit(solution)/shard_map/ppermute | solution.py:159
  415.2 2.4 add_convert_fusion.1
  (99 shorter events, 33.4 us)
Async XLA Ops:
  0.6 8.2 %copy-start = (s32[4]{0:T(128)S(1)}, s32[4]{0:T(128)}, u32[]{:S(2)}) copy-start(s32[4]{0:T(128)} %param.15) | copy-start | bytes 52
  0.6 8.1 %copy-start.14 = (s32[512]{0:T(512)S(1)}, s32[512]{0:T(512)}, u32[]{:S(2)}) copy-start(s32[512]{0:T(512)} %param.14) | copy-start | bytes 6148
  0.7 8.2 %copy-start.15 = (s32[512]{0:T(512)S(1)}, s32[512]{0:T(512)}, u32[]{:S(2)}) copy-start(s32[512]{0:T(512)} %param.13) | copy-start | bytes 6148
  0.7 70.2 %collective-permute-start = (bf16[256,3072]{1,0:T(8,128)(2,1)}, bf16[256,3072]{1,0:T(8,128)(2,1)}, u32[]{:S(2)}, u32[]{:S(2)}) collective-permute-start(bf16[256,3072]{1,0:T(8,128)(2,1)} %param.8), channel_id=1, source_target_pairs={{0,16},{4,20},{8,24},{12,28},{16,0},{20,4},{24,8},{28,12},{1,17},{... | collective-permute-start | bytes 4718600 | tf_op jit(solution)/shard_map/ppermute | solution.py:16
  6.0 63.0 %collective-permute-start.11 = (bf16[384,768]{1,0:T(8,128)(2,1)S(1)}, bf16[384,768]{1,0:T(8,128)(2,1)S(1)}, u32[]{:S(2)}, u32[]{:S(2)}) collective-permute-start(bf16[384,768]{1,0:T(8,128)(2,1)S(1)} %get-tuple-element.15), channel_id=1, source_target_pairs={{0,4},{4,0},{8,12},{12,8},{16,20},{20,16},{24,28},{28,24},{1,5},{5... | collective-permute-start | bytes 1769480 | tf_op jit(solution)/shard_map/ppermute | solution.py:16
  7.1 62.3 %collective-permute-start.12 = (bf16[384,768]{1,0:T(8,128)(2,1)S(1)}, bf16[384,768]{1,0:T(8,128)(2,1)}, u32[]{:S(2)}, u32[]{:S(2)}) collective-permute-start(bf16[384,768]{1,0:T(8,128)(2,1)S(1)} %get-tuple-element.16), channel_id=1, source_target_pairs={{0,16},{4,20},{8,24},{12,28},{16,0},{20,4},{24,8},{28,12},{1,17},{... | collective-permute-start | bytes 1769480 | tf_op jit(solution)/shard_map/ppermute | solution.py:16
  7.3 63.3 %collective-permute-start.13 = (bf16[384,768]{1,0:T(8,128)(2,1)S(1)}, bf16[384,768]{1,0:T(8,128)(2,1)}, u32[]{:S(2)}, u32[]{:S(2)}) collective-permute-start(bf16[384,768]{1,0:T(8,128)(2,1)S(1)} %get-tuple-element.17), channel_id=1, source_target_pairs={{0,20},{4,16},{8,28},{12,24},{16,4},{20,0},{24,12},{28,8},{1,21},{... | collective-permute-start | bytes 1769480 | tf_op jit(solution)/shard_map/ppermute | solution.py:16
  9.1 52.5 %collective-permute-start.9 = (f32[256,2]{0,1:T(2,128)S(1)}, f32[256,2]{0,1:T(2,128)S(1)}, u32[]{:S(2)}, u32[]{:S(2)}) collective-permute-start(f32[256,2]{0,1:T(2,128)S(1)} %fusion.22), channel_id=1, source_target_pairs={{0,16},{4,20},{8,24},{12,28},{16,0},{20,4},{24,8},{28,12},{1,17},{... | collective-permute-start | bytes 6152 | tf_op jit(solution)/shard_map/ppermute | solution.py:16
  61.6 10.4 %copy-start.7 = (bf16[256,3072]{1,0:T(8,128)(2,1)S(1)}, bf16[256,3072]{1,0:T(8,128)(2,1)}, u32[]{:S(2)}) copy-start(bf16[256,3072]{1,0:T(8,128)(2,1)} %param.8) | copy-start | bytes 4718596
  61.6 7.3 %collective-permute-start.10 = (f32[512,2]{0,1:T(2,128)S(1)}, f32[512,2]{0,1:T(2,128)S(1)}, u32[]{:S(2)}, u32[]{:S(2)}) collective-permute-start(f32[512,2]{0,1:T(2,128)S(1)} %pad_maximum_fusion.7), channel_id=1, source_target_pairs={{0,4},{4,0},{8,12},{12,8},{16,20},{20,16},{24,28},{28,24},{1,5},{5... | collective-permute-start | bytes 12296 | tf_op jit(solution)/shard_map/ppermute | solution.py:16
  68.9 6.7 %copy-start.2 = (bf16[2,384,768]{2,1,0:T(8,128)(2,1)}, bf16[2,384,768]{2,1,0:T(8,128)(2,1)S(1)}, u32[]{:S(2)}) copy-start(bf16[2,384,768]{2,1,0:T(8,128)(2,1)S(1)} %get-tuple-element.12) | copy-start | bytes 3538948
  68.9 52.9 %collective-permute-start.2 = (bf16[2,384,768]{2,1,0:T(8,128)(2,1)}, bf16[2,384,768]{2,1,0:T(8,128)(2,1)}, u32[]{:S(2)}, u32[]{:S(2)}) collective-permute-start(bf16[2,384,768]{2,1,0:T(8,128)(2,1)} %get-tuple-element.11), channel_id=1, source_target_pairs={{0,4},{4,0},{8,12},{12,8},{16,20},{20,16},{24,28},{28,24},{1,5},{5... | collective-permute-start | bytes 3538952 | tf_op jit(solution)/shard_map/ppermute | solution.py:16
  69.0 14.5 %collective-permute-start.14 = (bf16[384,768]{1,0:T(8,128)(2,1)S(1)}, bf16[384,768]{1,0:T(8,128)(2,1)S(1)}, u32[]{:S(2)}, u32[]{:S(2)}) collective-permute-start(bf16[384,768]{1,0:T(8,128)(2,1)S(1)} %get-tuple-element.14), channel_id=1, source_target_pairs={{0,8},{4,12},{8,0},{12,4},{16,24},{20,28},{24,16},{28,20},{1,9},{5... | collective-permute-start | bytes 1769480 | tf_op jit(solution)/shard_map/ppermute | solution.py:16
  69.4 27.0 %collective-permute-start.15 = (bf16[384,768]{1,0:T(8,128)(2,1)S(1)}, bf16[384,768]{1,0:T(8,128)(2,1)}, u32[]{:S(2)}, u32[]{:S(2)}) collective-permute-start(bf16[384,768]{1,0:T(8,128)(2,1)S(1)} %collective-permute-done.11), channel_id=1, source_target_pairs={{0,8},{4,12},{8,0},{12,4},{16,24},{20,28},{24,16},{28,20},{1,9},{5... | collective-permute-start | bytes 1769480 | tf_op jit(solution)/shard_map/ppermute | solution.py:16
  70.6 38.4 %collective-permute-start.16 = (bf16[384,768]{1,0:T(8,128)(2,1)}, bf16[384,768]{1,0:T(8,128)(2,1)}, u32[]{:S(2)}, u32[]{:S(2)}) collective-permute-start(bf16[384,768]{1,0:T(8,128)(2,1)} %collective-permute-done.12), channel_id=1, source_target_pairs={{0,8},{4,12},{8,0},{12,4},{16,24},{20,28},{24,16},{28,20},{1,9},{5... | collective-permute-start | bytes 1769480 | tf_op jit(solution)/shard_map/ppermute | solution.py:16
  70.8 50.8 %collective-permute-start.17 = (bf16[384,768]{1,0:T(8,128)(2,1)}, bf16[384,768]{1,0:T(8,128)(2,1)}, u32[]{:S(2)}, u32[]{:S(2)}) collective-permute-start(bf16[384,768]{1,0:T(8,128)(2,1)} %collective-permute-done.13), channel_id=1, source_target_pairs={{0,8},{4,12},{8,0},{12,4},{16,24},{20,28},{24,16},{28,20},{1,9},{5... | collective-permute-start | bytes 1769480 | tf_op jit(solution)/shard_map/ppermute | solution.py:16
  84.4 140.4 %collective-permute-start.1 = (bf16[512,3072]{1,0:T(8,128)(2,1)}, bf16[512,3072]{1,0:T(8,128)(2,1)}, u32[]{:S(2)}, u32[]{:S(2)}) collective-permute-start(bf16[512,3072]{1,0:T(8,128)(2,1)} %pad_maximum_fusion.1), channel_id=1, source_target_pairs={{0,4},{4,0},{8,12},{12,8},{16,20},{20,16},{24,28},{28,24},{1,5},{5... | collective-permute-start | bytes 9437192 | tf_op jit(solution)/shard_map/ppermute | solution.py:16
  96.3 31.5 %collective-permute-start.3 = (bf16[2,384,768]{2,1,0:T(8,128)(2,1)}, bf16[2,384,768]{2,1,0:T(8,128)(2,1)}, u32[]{:S(2)}, u32[]{:S(2)}) collective-permute-start(bf16[2,384,768]{2,1,0:T(8,128)(2,1)} %copy-done.2), channel_id=1, source_target_pairs={{0,16},{4,20},{8,24},{12,28},{16,0},{20,4},{24,8},{28,12},{1,17},{... | collective-permute-start | bytes 3538952 | tf_op jit(solution)/shard_map/ppermute | solution.py:16
  102.9 19.0 %copy-start.9 = (bf16[256,3072]{1,0:T(8,128)(2,1)S(1)}, bf16[256,3072]{1,0:T(8,128)(2,1)}, u32[]{:S(2)}) copy-start(bf16[256,3072]{1,0:T(8,128)(2,1)} %param.9) | copy-start | bytes 4718596
  109.0 43.5 %collective-permute-start.4 = (bf16[2,384,768]{2,1,0:T(8,128)(2,1)S(1)}, bf16[2,384,768]{2,1,0:T(8,128)(2,1)S(1)}, u32[]{:S(2)}, u32[]{:S(2)}) collective-permute-start(bf16[2,384,768]{2,1,0:T(8,128)(2,1)S(1)} %get-tuple-element.13), channel_id=1, source_target_pairs={{0,20},{4,16},{8,28},{12,24},{16,4},{20,0},{24,12},{28,8},{1,21},{... | collective-permute-start | bytes 3538952 | tf_op jit(solution)/shard_map/ppermute | solution.py:16
  112.5 12.9 %copy-start.13 = (bf16[384,768]{1,0:T(8,128)(2,1)S(1)}, bf16[384,768]{1,0:T(8,128)(2,1)}, u32[]{:S(2)}) copy-start(bf16[384,768]{1,0:T(8,128)(2,1)} %copy-done.12) | copy-start | bytes 1769476
  121.6 32.2 %collective-permute-start.5 = (bf16[2,384,768]{2,1,0:T(8,128)(2,1)S(1)}, bf16[2,384,768]{2,1,0:T(8,128)(2,1)S(1)}, u32[]{:S(2)}, u32[]{:S(2)}) collective-permute-start(bf16[2,384,768]{2,1,0:T(8,128)(2,1)S(1)} %get-tuple-element.10), channel_id=1, source_target_pairs={{0,8},{4,12},{8,0},{12,4},{16,24},{20,28},{24,16},{28,20},{1,9},{5... | collective-permute-start | bytes 3538952 | tf_op jit(solution)/shard_map/ppermute | solution.py:16
  121.9 59.0 %collective-permute-start.23 = (bf16[256,3072]{1,0:T(8,128)(2,1)S(1)}, bf16[256,3072]{1,0:T(8,128)(2,1)S(1)}, u32[]{:S(2)}, u32[]{:S(2)}) collective-permute-start(bf16[256,3072]{1,0:T(8,128)(2,1)S(1)} %copy-done.9), channel_id=1, source_target_pairs={{0,16},{4,20},{8,24},{12,28},{16,0},{20,4},{24,8},{28,12},{1,17},{... | collective-permute-start | bytes 4718600 | tf_op jit(solution)/shard_map/ppermute | solution.py:16
  127.8 57.5 %collective-permute-start.6 = (bf16[2,384,768]{2,1,0:T(8,128)(2,1)}, bf16[2,384,768]{2,1,0:T(8,128)(2,1)S(1)}, u32[]{:S(2)}, u32[]{:S(2)}) collective-permute-start(bf16[2,384,768]{2,1,0:T(8,128)(2,1)} %collective-permute-done.2), channel_id=1, source_target_pairs={{0,8},{4,12},{8,0},{12,4},{16,24},{20,28},{24,16},{28,20},{1,9},{5... | collective-permute-start | bytes 3538952 | tf_op jit(solution)/shard_map/ppermute | solution.py:16
  152.5 45.9 %collective-permute-start.7 = (bf16[2,384,768]{2,1,0:T(8,128)(2,1)}, bf16[2,384,768]{2,1,0:T(8,128)(2,1)S(1)}, u32[]{:S(2)}, u32[]{:S(2)}) collective-permute-start(bf16[2,384,768]{2,1,0:T(8,128)(2,1)} %collective-permute-done.3), channel_id=1, source_target_pairs={{0,8},{4,12},{8,0},{12,4},{16,24},{20,28},{24,16},{28,20},{1,9},{5... | collective-permute-start | bytes 3538952 | tf_op jit(solution)/shard_map/ppermute | solution.py:16
  153.8 69.8 %collective-permute-start.8 = (bf16[2,384,768]{2,1,0:T(8,128)(2,1)S(1)}, bf16[2,384,768]{2,1,0:T(8,128)(2,1)S(1)}, u32[]{:S(2)}, u32[]{:S(2)}) collective-permute-start(bf16[2,384,768]{2,1,0:T(8,128)(2,1)S(1)} %collective-permute-done.4), channel_id=1, source_target_pairs={{0,8},{4,12},{8,0},{12,4},{16,24},{20,28},{24,16},{28,20},{1,9},{5... | collective-permute-start | bytes 3538952 | tf_op jit(solution)/shard_map/ppermute | solution.py:16
  180.8 1.2 copy-start.10
  182.2 78.1 %collective-permute-start.24 = (bf16[512,3072]{1,0:T(8,128)(2,1)S(1)}, bf16[512,3072]{1,0:T(8,128)(2,1)S(1)}, u32[]{:S(2)}, u32[]{:S(2)}) collective-permute-start(bf16[512,3072]{1,0:T(8,128)(2,1)S(1)} %pad_maximum_fusion.3), channel_id=1, source_target_pairs={{0,4},{4,0},{8,12},{12,8},{16,20},{20,16},{24,28},{28,24},{1,5},{5... | collective-permute-start | bytes 9437192 | tf_op jit(solution)/shard_map/ppermute | solution.py:16
  224.8 2.4 copy-start.8
  244.5 9.1 %copy-start.16 = (f32[1024,768]{1,0:T(8,128)}, f32[1024,768]{1,0:T(8,128)S(1)}, u32[]{:S(2)}) copy-start(f32[1024,768]{1,0:T(8,128)S(1)} %fusion.8) | copy-start | bytes 9437188
  253.6 2.6 copy-start.3
  258.1 2.4 copy-start.11
  258.1 41.1 %collective-permute-start.18 = (bf16[2,256,3072]{2,1,0:T(8,128)(2,1)}, bf16[2,256,3072]{2,1,0:T(8,128)(2,1)S(1)}, u32[]{:S(2)}, u32[]{:S(2)}) collective-permute-start(bf16[2,256,3072]{2,1,0:T(8,128)(2,1)} %pad_maximum_fusion.2), channel_id=1, source_target_pairs={{0,4},{4,0},{8,12},{12,8},{16,20},{20,16},{24,28},{28,24},{1,5},{5... | collective-permute-start | bytes 9437192 | tf_op jit(solution)/shard_map/ppermute | solution.py:16
  260.5 6.8 %copy-start.17 = (f32[1024,768]{1,0:T(8,128)S(1)}, f32[1024,768]{1,0:T(8,128)}, u32[]{:S(2)}) copy-start(f32[1024,768]{1,0:T(8,128)} %copy-done.16) | copy-start | bytes 9437188
  265.6 1.7 copy-start.18
  298.0 6.8 %collective-permute-start.25 = (bf16[2,256,3072]{2,1,0:T(8,128)(2,1)S(1)}, bf16[2,256,3072]{2,1,0:T(8,128)(2,1)S(1)}, u32[]{:S(2)}, u32[]{:S(2)}) collective-permute-start(bf16[2,256,3072]{2,1,0:T(8,128)(2,1)S(1)} %pad_maximum_fusion.4), channel_id=1, source_target_pairs={{0,4},{4,0},{8,12},{12,8},{16,20},{20,16},{24,28},{28,24},{1,5},{5... | collective-permute-start | bytes 9437192 | tf_op jit(solution)/shard_map/ppermute | solution.py:16
  299.2 10.3 %copy-start.4 = (bf16[2,256,3072]{2,1,0:T(8,128)(2,1)}, bf16[2,256,3072]{2,1,0:T(8,128)(2,1)S(1)}, u32[]{:S(2)}) copy-start(bf16[2,256,3072]{2,1,0:T(8,128)(2,1)S(1)} %collective-permute-done.18) | copy-start | bytes 9437188
  303.6 36.3 %collective-permute-start.19 = (bf16[256,3072]{1,0:T(8,128)(2,1)}, bf16[256,3072]{1,0:T(8,128)(2,1)}, u32[]{:S(2)}, u32[]{:S(2)}) collective-permute-start(bf16[256,3072]{1,0:T(8,128)(2,1)} %fusion.13), channel_id=1, source_target_pairs={{0,16},{4,20},{8,24},{12,28},{16,0},{20,4},{24,8},{28,12},{1,17},{... | collective-permute-start | bytes 4718600 | tf_op jit(solution)/shard_map/ppermute | solution.py:16
  304.8 1.6 copy-start.5
  309.5 64.1 %collective-permute-start.26 = (bf16[256,3072]{1,0:T(8,128)(2,1)}, bf16[256,3072]{1,0:T(8,128)(2,1)}, u32[]{:S(2)}, u32[]{:S(2)}) collective-permute-start(bf16[256,3072]{1,0:T(8,128)(2,1)} %fusion.11), channel_id=1, source_target_pairs={{0,16},{4,20},{8,24},{12,28},{16,0},{20,4},{24,8},{28,12},{1,17},{... | collective-permute-start | bytes 4718600 | tf_op jit(solution)/shard_map/ppermute | solution.py:16
  339.9 33.7 %copy-start.6 = (bf16[2,256,3072]{2,1,0:T(8,128)(2,1)S(1)}, bf16[2,256,3072]{2,1,0:T(8,128)(2,1)}, u32[]{:S(2)}) copy-start(bf16[2,256,3072]{2,1,0:T(8,128)(2,1)} %copy-done.5) | copy-start | bytes 9437188
  344.2 37.3 %collective-permute-start.22 = (bf16[256,768]{1,0:T(8,128)(2,1)S(1)}, bf16[256,768]{1,0:T(8,128)(2,1)S(1)}, u32[]{:S(2)}, u32[]{:S(2)}) collective-permute-start(bf16[256,768]{1,0:T(8,128)(2,1)S(1)} %get-tuple-element.34), channel_id=1, source_target_pairs={{0,3},{1,0},{2,1},{3,2},{4,7},{5,4},{6,5},{7,6},{8,11},{9,8},{10,9... | collective-permute-start | bytes 1179656 | tf_op jit(solution)/shard_map/ppermute | solution.py:159
  344.4 39.3 %collective-permute-start.21 = (bf16[256,768]{1,0:T(8,128)(2,1)}, bf16[256,768]{1,0:T(8,128)(2,1)}, u32[]{:S(2)}, u32[]{:S(2)}) collective-permute-start(bf16[256,768]{1,0:T(8,128)(2,1)} %get-tuple-element.35), channel_id=1, source_target_pairs={{0,2},{1,3},{2,0},{3,1},{4,6},{5,7},{6,4},{7,5},{8,10},{9,11},{10,... | collective-permute-start | bytes 1179656 | tf_op jit(solution)/shard_map/ppermute | solution.py:159
  346.7 37.0 %collective-permute-start.20 = (bf16[256,768]{1,0:T(8,128)(2,1)}, bf16[256,768]{1,0:T(8,128)(2,1)}, u32[]{:S(2)}, u32[]{:S(2)}) collective-permute-start(bf16[256,768]{1,0:T(8,128)(2,1)} %get-tuple-element.33), channel_id=1, source_target_pairs={{0,1},{1,2},{2,3},{3,0},{4,5},{5,6},{6,7},{7,4},{8,9},{9,10},{10,1... | collective-permute-start | bytes 1179656 | tf_op jit(solution)/shard_map/ppermute | solution.py:159
  377.9 39.7 %copy-start.1 = (s32[4]{0:T(128)S(1)}, s32[4]{0:T(128)}, u32[]{:S(2)}) copy-start(s32[4]{0:T(128)} %param.15) | copy-start | bytes 52
  379.0 10.1 %collective-permute-start.29 = (bf16[256,768]{1,0:T(8,128)(2,1)}, bf16[256,768]{1,0:T(8,128)(2,1)}, u32[]{:S(2)}, u32[]{:S(2)}) collective-permute-start(bf16[256,768]{1,0:T(8,128)(2,1)} %get-tuple-element.31), channel_id=1, source_target_pairs={{0,3},{1,0},{2,1},{3,2},{4,7},{5,4},{6,5},{7,6},{8,11},{9,8},{10,9... | collective-permute-start | bytes 1179656 | tf_op jit(solution)/shard_map/ppermute | solution.py:159
  379.2 27.6 %collective-permute-start.28 = (bf16[256,768]{1,0:T(8,128)(2,1)}, bf16[256,768]{1,0:T(8,128)(2,1)}, u32[]{:S(2)}, u32[]{:S(2)}) collective-permute-start(bf16[256,768]{1,0:T(8,128)(2,1)} %get-tuple-element.32), channel_id=1, source_target_pairs={{0,2},{1,3},{2,0},{3,1},{4,6},{5,7},{6,4},{7,5},{8,10},{9,11},{10,... | collective-permute-start | bytes 1179656 | tf_op jit(solution)/shard_map/ppermute | solution.py:159
  381.5 33.7 %collective-permute-start.27 = (bf16[256,768]{1,0:T(8,128)(2,1)}, bf16[256,768]{1,0:T(8,128)(2,1)}, u32[]{:S(2)}, u32[]{:S(2)}) collective-permute-start(bf16[256,768]{1,0:T(8,128)(2,1)} %get-tuple-element.30), channel_id=1, source_target_pairs={{0,1},{1,2},{2,3},{3,0},{4,5},{5,6},{6,7},{7,4},{8,9},{9,10},{10,1... | collective-permute-start | bytes 1179656 | tf_op jit(solution)/shard_map/ppermute | solution.py:159
  (1 other events, 0.8 us)

commit v2 on v1

v2 whole, which is shorter than its diff:
```python
import functools

import jax
import jax.numpy as jnp
from jax import lax
from jax.experimental import pallas as pl
from jax.experimental.pallas import tpu as pltpu
from jax.sharding import PartitionSpec as P

gate_steps = 16.0
vmem_limit = 48 * 1024 * 1024
shares = 4
slot_us = 5.0
flop_rate = 1_150_000_000
low, high = (((1,), (0,)), ((), ())), (((1,), (1,)), ((), ()))
dot = functools.partial(lax.dot_general, preferred_element_type=jnp.float32)
params = pltpu.CompilerParams(vmem_limit_bytes=vmem_limit)
anywhere = pl.BlockSpec(memory_space=pl.ANY)


def shape_of(value):
    return jax.ShapeDtypeStruct(value.shape, value.dtype)


class Clock:
    def __init__(self):
        self.token = blank((16, 128))

    def tick(self, release, wait=()):
        held = [self.token, *release]
        known = {id(value) for value in held}
        wait = [value for value in wait if id(value) not in known]
        self.token, *out = pl.pallas_call(
            lambda *refs: None,
            in_specs=[anywhere] * (len(held) + len(wait)),
            out_specs=[anywhere] * len(held),
            out_shape=[shape_of(value) for value in held],
            input_output_aliases={i: i for i in range(len(held))},
            cost_estimate=pl.CostEstimate(flops=int(slot_us * flop_rate), bytes_accessed=0, transcendentals=0),
            name="tick",
        )(*held, *wait)
        return out


def blank(shape):
    return pl.pallas_call(
        lambda *refs: None,
        out_specs=anywhere,
        out_shape=jax.ShapeDtypeStruct(shape, jnp.bfloat16),
        name="blank",
    )()


def swap(value, mask, size):
    return lax.ppermute(value, "dp", [(i, i ^ mask) for i in range(size)])


def steps_of(rows):
    return max(step for step in (1, 2, 4) if rows % (16 * step) == 0)


def cast_rows_kernel(pick_ref, gate_ref, up_ref, *out_refs):
    parts = shares // gate_ref.shape[0]
    width = out_refs[0].shape[-1]
    for share, out_ref in enumerate(out_refs):
        expert = pick_ref[share] // parts
        lanes = pl.ds(pl.multiple_of(pick_ref[share] % parts * width, 128), width)
        out_ref[0] = gate_ref[expert, :, lanes].astype(jnp.bfloat16)
        out_ref[1] = up_ref[expert, :, lanes].astype(jnp.bfloat16)


def cast_rows(pick, w_gate, w_up):
    experts, rows, hidden = w_gate.shape
    width = experts * hidden // shares
    steps = steps_of(rows)
    block = pl.BlockSpec((experts, rows // steps, hidden), lambda i, pick: (0, i, 0))
    return pl.pallas_call(
        cast_rows_kernel,
        grid_spec=pltpu.PrefetchScalarGridSpec(
            num_scalar_prefetch=1,
            grid=(steps,),
            in_specs=[block, block],
            out_specs=[pl.BlockSpec((2, rows // steps, width), lambda i, pick: (0, i, 0))] * shares,
        ),
        out_shape=[jax.ShapeDtypeStruct((2, rows, width), jnp.bfloat16)] * shares,
        compiler_params=params,
        name="cast_rows",
    )(pick, w_gate, w_up)


def cast_turned_kernel(pick_ref, down_ref, *refs):
    out_refs = refs[-shares:]
    parts = shares // down_ref.shape[0]
    width = out_refs[0].shape[-1]
    for share, out_ref in enumerate(out_refs):
        expert = pick_ref[share] // parts
        rows = pl.ds(pl.multiple_of(pick_ref[share] % parts * width, 128), width)
        out_ref[...] = down_ref[expert, rows, :].T.astype(jnp.bfloat16)


def cast_turned(pick, w_down, *earlier):
    experts, hidden, features = w_down.shape
    width = experts * hidden // shares
    tile = 128 if features % 128 == 0 else features
    return pl.pallas_call(
        cast_turned_kernel,
        grid_spec=pltpu.PrefetchScalarGridSpec(
            num_scalar_prefetch=1,
            grid=(features // tile,),
            in_specs=[pl.BlockSpec((experts, hidden, tile), lambda i, pick: (0, 0, i))]
            + [anywhere] * len(earlier),
            out_specs=[pl.BlockSpec((tile, width), lambda i, pick: (i, 0))] * shares,
        ),
        out_shape=[jax.ShapeDtypeStruct((features, width), jnp.bfloat16)] * shares,
        compiler_params=params,
        name="cast_turned",
    )(pick, w_down, *earlier)


def fetch(keys, refs, me, chunk, span, target, sems, start):
    rows = refs[0].shape[-2]
    per = span // rows
    for i, (key, ref) in enumerate(zip(keys, refs)):
        block = me ^ key

        @pl.when(block // per == chunk)
        def _(ref=ref, i=i, block=block):
            place = pl.ds(pl.multiple_of(block % per * rows, 16), rows)
            view = target.at[place] if len(target.shape) == 2 else target.at[:, place]
            copy = pltpu.make_async_copy(ref, view, sems.at[i])
            if start:
                copy.start()
            else:
                copy.wait()


def load(n, me, parts, blocks, x, weights, x_sems, sems):
    step = pl.program_id(0)
    copies = [pltpu.make_async_copy(part, x.at[i], x_sems.at[i]) for i, part in enumerate(parts)]

    @pl.when(step == 0)
    def _():
        fetch(range(n), blocks, me, 0, weights.shape[-2], weights, sems, True)
        for copy in copies:
            copy.start()
        fetch(range(n), blocks, me, 0, weights.shape[-2], weights, sems, False)

    for i, copy in enumerate(copies):

        @pl.when(step == i)
        def _(copy=copy):
            copy.wait()


def forward_kernel(n, info_ref, *refs):
    hidden_ref, pre_ref, up_ref, x, weights, x_sems, sems = refs[shares + n :]
    load(n, info_ref[0], refs[:shares], refs[shares : shares + n], x, weights, x_sems, sems)
    part = pl.program_id(0)
    inputs = x[part, : hidden_ref.shape[1]]
    gate_pre = dot(inputs, weights[0], low)
    up_pre = dot(inputs, weights[1], low)
    count = hidden_ref.shape[1]
    square = lax.broadcasted_iota(jnp.int32, (count, count), 0) == lax.broadcasted_iota(jnp.int32, (count, count), 1)
    row = x[part, pl.ds(count, 1), pl.ds(pl.multiple_of(info_ref[1] * count, 128), count)].astype(jnp.float32)
    scale = jnp.sum(jnp.where(square, row, 0.0), axis=1, keepdims=True)
    squash = 1.0 / (1.0 + jnp.exp(-gate_pre))
    active = gate_pre * squash * scale
    hidden_ref[0] = (active * up_pre).astype(jnp.bfloat16)
    slope = up_pre * squash * (1.0 + gate_pre * (1.0 - squash)) * scale
    pre_ref[0] = slope.astype(jnp.bfloat16)
    up_ref[0] = active.astype(jnp.bfloat16)


def grow_kernel(n, me_ref, slope_ref, active_ref, *refs):
    pre_ref, up_ref, u, weights, u_sems, sems = refs[shares + n :]
    load(n, me_ref[0], refs[:shares], refs[shares : shares + n], u, weights, u_sems, sems)
    d_hidden = dot(u[pl.program_id(0)], weights[...], low)
    pre_ref[0] = (d_hidden * slope_ref[0].astype(jnp.float32)).astype(jnp.bfloat16)
    up_ref[0] = (d_hidden * active_ref[0].astype(jnp.float32)).astype(jnp.bfloat16)


def on_tokens(name, kernel, prefetch, first, count, parts, blocks, outputs):
    features = parts[0].shape[1]
    n, width = len(blocks), blocks[0].shape[-1]
    each = pl.BlockSpec((1, count, width), lambda r, info: (r, 0, 0))
    return pl.pallas_call(
        functools.partial(kernel, n),
        grid_spec=pltpu.PrefetchScalarGridSpec(
            num_scalar_prefetch=1,
            grid=(shares,),
            in_specs=[each] * len(first) + [anywhere] * (shares + n),
            out_specs=[each] * outputs,
            scratch_shapes=[
                pltpu.VMEM((shares, *parts[0].shape), jnp.bfloat16),
                pltpu.VMEM((*blocks[0].shape[:-2], features, width), jnp.bfloat16),
                pltpu.SemaphoreType.DMA((shares,)),
                pltpu.SemaphoreType.DMA((n,)),
            ],
        ),
        out_shape=[jax.ShapeDtypeStruct((shares, count, width), jnp.bfloat16)] * outputs,
        compiler_params=params,
        cost_estimate=pl.CostEstimate(
            flops=2 * shares * count * n * blocks[0].size,
            bytes_accessed=2 * shares * count * features + 2 * n * blocks[0].size,
            transcendentals=0,
        ),
        name=name,
    )(prefetch, *first, *parts, *blocks)


def forward(info, count, x_parts, blocks):
    return on_tokens("forward", forward_kernel, info, [], count, x_parts, blocks, 3)


def grow(info, count, u_parts, blocks, factors):
    return on_tokens("grow", grow_kernel, info, factors, count, u_parts, blocks, 2)


def produce_kernel(keys, me_ref, ids_ref, hidden_ref, *refs):
    keep_ref, send_ref, down, sems = refs[len(keys) :]
    chunk, part = pl.program_id(0), pl.program_id(1)

    @pl.when(part == 0)
    def _():
        for start in (True, False):
            fetch(keys, refs[: len(keys)], me_ref[0], ids_ref[chunk], down.shape[0], down, sems, start)

    count, width = hidden_ref.shape[1:]
    produced = dot(hidden_ref[...].reshape(2 * count, width), down[...], high).astype(jnp.bfloat16)
    keep_ref[0, 0] = produced[:count]
    send_ref[0, 0] = produced[count:]


def produce(me, ids, chunks, hidden, keys, blocks, features):
    _, count, width = hidden.shape
    columns, size = features // chunks, ids.shape[0]
    half = pl.BlockSpec((1, 1, count, columns), lambda c, r, me, ids: (c, r, 0, 0))
    return pl.pallas_call(
        functools.partial(produce_kernel, keys),
        grid_spec=pltpu.PrefetchScalarGridSpec(
            num_scalar_prefetch=2,
            grid=(size, shares // 2),
            in_specs=[pl.BlockSpec((2, count, width), lambda c, r, me, ids: (r, 0, 0))] + [anywhere] * len(blocks),
            out_specs=[half, half],
            scratch_shapes=[pltpu.VMEM((columns, width), jnp.bfloat16), pltpu.SemaphoreType.DMA((len(keys),))],
        ),
        out_shape=[jax.ShapeDtypeStruct((size, shares // 2, count, columns), jnp.bfloat16)] * 2,
        compiler_params=params,
        cost_estimate=pl.CostEstimate(
            flops=2 * hidden.size * columns * size,
            bytes_accessed=2 * hidden.size * (size + 1),
            transcendentals=0,
        ),
        name="produce",
    )(me, ids, hidden, *blocks)


def back_kernel(n, me_ref, ids_ref, pre_ref, up_ref, *refs):
    block_refs = refs[:n]
    keep_ref, send_ref, weights, sems = refs[n:]
    chunk, part = pl.program_id(0), pl.program_id(1)
    size, span = weights.shape[0], weights.shape[2]

    for c in range(size):

        @pl.when((chunk == 0) & (part == 0))
        def _(c=c):
            fetch(range(n), block_refs, me_ref[0], ids_ref[c], span, weights.at[c], sems.at[c], True)

    for c in range(size):

        @pl.when((chunk == c) & (part == 0))
        def _(c=c):
            fetch(range(n), block_refs, me_ref[0], ids_ref[c], span, weights.at[c], sems.at[c], False)

    count, width = pre_ref.shape[1:]
    grown = dot(pre_ref[...].reshape(2 * count, width), weights[chunk, 0], high)
    grown = grown + dot(up_ref[...].reshape(2 * count, width), weights[chunk, 1], high)
    keep_ref[0, 0] = grown[:count].astype(jnp.bfloat16)
    send_ref[0, 0] = grown[count:].astype(jnp.bfloat16)


def back(me, ids, chunks, d_pre, d_up, blocks):
    _, count, width = d_pre.shape
    n, size = len(blocks), ids.shape[0]
    columns = n * blocks[0].shape[1] // chunks
    part = pl.BlockSpec((2, count, width), lambda c, r, me, ids: (r, 0, 0))
    half = pl.BlockSpec((1, 1, count, columns), lambda c, r, me, ids: (c, r, 0, 0))
    return pl.pallas_call(
        functools.partial(back_kernel, n),
        grid_spec=pltpu.PrefetchScalarGridSpec(
            num_scalar_prefetch=2,
            grid=(size, shares // 2),
            in_specs=[part, part] + [anywhere] * n,
            out_specs=[half, half],
            scratch_shapes=[
                pltpu.VMEM((size, 2, columns, width), jnp.bfloat16),
                pltpu.SemaphoreType.DMA((size, n)),
            ],
        ),
        out_shape=[jax.ShapeDtypeStruct((size, shares // 2, count, columns), jnp.bfloat16)] * 2,
        compiler_params=params,
        cost_estimate=pl.CostEstimate(
            flops=4 * size * shares * count * width * columns,
            bytes_accessed=4 * d_pre.size + 4 * size * columns * width,
            transcendentals=0,
        ),
        name="back",
    )(me, ids, d_pre, d_up, *blocks)


def pack_kernel(value_ref, scale_ref, tick_ref, out_ref):
    count, (experts, tokens) = value_ref.shape[0], scale_ref.shape
    out_ref[:count] = value_ref[...]
    if out_ref.shape[0] > count:
        out_ref[count:] = jnp.zeros((out_ref.shape[0] - count, out_ref.shape[1]), out_ref.dtype)
        for expert in range(experts):
            out_ref[pl.ds(count, 16), pl.ds(expert * tokens, tokens)] = jnp.broadcast_to(
                scale_ref[pl.ds(expert, 1), :], (16, tokens)
            ).astype(out_ref.dtype)


def pack(value, scale, tick, extra):
    return pl.pallas_call(
        pack_kernel,
        in_specs=[pl.BlockSpec(memory_space=pltpu.VMEM)] * 2 + [anywhere],
        out_specs=pl.BlockSpec(memory_space=pltpu.VMEM),
        out_shape=jax.ShapeDtypeStruct((value.shape[0] + extra, value.shape[1]), value.dtype),
        compiler_params=params,
        name="pack",
    )(value, scale, tick)


def token_scales(slot_token, slot_gate, block_expert, experts, token_count):
    block_rows = slot_token.shape[0] // block_expert.shape[0]
    scale = slot_gate.astype(jnp.float32) / gate_steps
    slot_expert = jnp.repeat(block_expert, block_rows)
    weight = jnp.where(slot_expert[None, :] == jnp.arange(experts)[:, None], scale[None, :], 0.0)
    hot = (slot_token[:, None] == jnp.arange(token_count)[None, :]).astype(jnp.bfloat16)
    return jnp.dot(weight.astype(jnp.bfloat16), hot, preferred_element_type=jnp.float32)


def shards(n, m, tokens, cotangent, w_gate, w_up, w_down, slot_token, slot_gate, block_expert):
    experts = w_gate.shape[0]
    count, features = tokens.shape
    columns = features // m
    me, z = lax.axis_index("dp"), lax.axis_index("etp")
    top, chip, here = n // 2, me // 2, me.reshape(1)
    gather_bits = [1 << i for i in range(1, n.bit_length() - 2)]
    single = len(gather_bits) == 1
    mine = (me & 1) + 2 * (me // top)
    pick = jnp.stack([mine ^ share for share in range(shares)]).astype(jnp.int32)
    clock = Clock()
    wide = functools.partial(jnp.asarray, dtype=jnp.float32)

    def shift(value, step, targets=None):
        if targets is None:
            return lax.ppermute(value, "etp", [(i, (i + step) % m) for i in range(m)])
        pairs = [
            (d * m + i, d * m + (i + step) % m)
            for d in range(n)
            for i in range(m)
            if (i + step) % m in targets(d)
        ]
        return lax.ppermute(value, ("dp", "etp"), pairs)

    have, starts, needs = {}, {}, {}
    scale = token_scales(slot_token, slot_gate, block_expert, experts, count)

    def plan(slot, until, name, source, mask):
        starts.setdefault(slot, []).append((name, source, mask))
        needs.setdefault(until, []).append(name)

    plan(0, 1, ("rows", 1), ("rows piece", 1), 1)
    plan(0, 2, ("rows", top), ("rows piece", 2), top)
    plan(1, 3, ("rows", top + 1), ("rows piece", 3), top + 1)
    plan(2, 3, ("turned", top), ("turned piece", 2), top)
    plan(3, 6, "x near", "x", 1)
    plan(3, 5, "x far", "x", top)
    plan(3, 5, ("turned", 1), ("turned piece", 1), 1)
    plan(4, 8, ("turned", top + 1), ("turned piece", 3), top + 1)
    plan(5, 6, "x far near", "x far", 1)
    plan(6, 8, "u far", "u", top)
    plan(4, 8, "u near", "u", 1)
    plan(8, 9, "u far near", "u far", 1)
    slots = [(0, 2), (1, 3), (2, 4), (3, 5), (4, 6), (5, 7), (7, 9), (8, 9)]
    moves = 0
    for kind in ("rows", "turned"):
        held = [0, 1, top, top + 1]
        for bit in gather_bits:
            for key in list(held):
                begin, until = slots[moves] if single else (moves + 3, moves + 5)
                plan(begin, until, (kind, key ^ bit), (kind, key), bit)
                held.append(key ^ bit)
                moves += 1

    def tick(at, extra=()):
        begin = starts.get(at, [])
        names = list(dict.fromkeys(source for _, source, _ in begin))
        wait = [have[name] for name in needs.get(at, [])]
        have.update(zip(names, clock.tick([have[name] for name in names], [*wait, *extra])))
        for name, source, mask in begin:
            have[name] = swap(have[source], mask, n)

    pieces = cast_rows(pick, w_gate, w_up)
    have["rows", 0] = pieces[0]
    have.update({("rows piece", share): pieces[share] for share in range(1, shares)})
    tick(0)
    pieces = cast_turned(pick, w_down, clock.token)
    have["turned", 0] = pieces[0]
    have.update({("turned piece", share): pieces[share] for share in range(1, shares)})
    tick(1)
    have["x"] = pack(tokens, scale, clock.token, 16)
    tick(2)
    have["u"] = pack(cotangent, scale, clock.token, 0)
    last = max(needs)
    halves = n == 2 * m and single
    for at in range(3, 7 if halves else last + 1):
        tick(at)

    blocks = [have["rows", key] for key in range(n)]
    info = jnp.stack([me, mine // (shares // experts)]).astype(jnp.int32)
    hidden, *factors = forward(info, count, [have[k] for k in ("x", "x near", "x far", "x far near")], blocks)

    def run(keys, ids, hidden):
        return produce(here, ids, m, hidden, keys, [have["turned", key] for key in keys], features)

    def add(keep, near):
        return (wide(keep[:, 1]) + wide(near[:, 1])).astype(jnp.bfloat16), wide(keep[:, 0]) + wide(near[:, 0])

    def choose(target, keys, values):
        if keys is None:
            return lax.dynamic_index_in_dim(jnp.stack(list(values)), target, 0, False)
        return jnp.where(target == chip ^ (keys[0] // 2), values[0], values[1])

    order = [m // 2] + [step for step in range(1, m) if step != m // 2] + [0]

    def outward(total, keys):
        own = choose(z, keys, total)
        if keys is not None:
            there = (z == chip ^ (keys[0] // 2)) | (z == chip ^ (keys[1] // 2))
            own = jnp.where(there, own, 0.0)
        total = [part.astype(jnp.bfloat16) for part in total]
        return own, [choose(lax.rem(z + step, m), keys, total) for step in order[:-1]]

    def pass_on(values, keys):
        targets = None if keys is None else lambda d: [(d ^ key) // 2 for key in keys]
        return [shift(value, step, targets) for value, step in zip(values, order)]

    gained, u_names = [], ("u", "u near", "u far", "u far near")
    downs = lambda: [have["turned", key] for key in range(n)]
    if halves:
        bit = gather_bits[0]
        tick(7, [hidden])
        keep_a, send_a = run([0, 1, top, top + 1], jnp.stack([chip, chip ^ (top // 2)]), hidden)
        tick(8, [send_a])
        (send_a,) = clock.tick([send_a])
        near = swap(send_a, 1, n)
        keep_b, send_b = run([bit, bit + 1], (chip ^ (bit // 2)).reshape(1), hidden)
        (send_b,) = clock.tick([send_b], [near, have["turned", top ^ bit]])
        other, own_a = add(keep_a, near)
        near = swap(send_b, 1, n)
        (other,) = clock.tick([other], [near])
        far_a = swap(other, top, n)
        other, own_b = add(keep_b, near)
        (other,) = clock.tick([other], [have["turned", top ^ bit ^ 1]])
        far_b = swap(other, top, n)
        clock.tick([], [far_a, far_b])
        own, values = outward([own_a[0] + wide(far_a[1]), own_a[1] + wide(far_a[0])], (0, top))
        values = clock.tick(values)
        gained.append(own)
        early = pass_on(values, (0, top))
        gained += [wide(value) for value in early]
        tick(9)
        (hidden,) = clock.tick([hidden])
        ids, keys = (chip ^ ((bit ^ top) // 2)).reshape(1), [bit + top, bit + top + 1]
    else:
        ids, keys, early = jnp.arange(m, dtype=jnp.int32), list(range(n)), []
    keep, send = run(keys, ids, hidden)
    u_parts = [have[name] for name in u_names]
    send, u_parts[0] = clock.tick([send, u_parts[0]])
    near = swap(send, 1, n)
    d_pre, d_up = grow(info, count, u_parts, downs(), factors)
    (d_pre,) = clock.tick([d_pre], [near])
    other, own = add(keep, near)
    (other,) = clock.tick([other])
    got = swap(other, top, n)
    steps = jnp.array([order[: m // 2], order[m // 2 :]], jnp.int32)
    keep_0, send_0 = back(here, lax.rem(z + steps[0], m), m, d_pre, d_up, blocks)
    send_0, d_pre = clock.tick([send_0, d_pre], early)
    near_0 = swap(send_0, 1, n)
    keep_1, send_1 = back(here, lax.rem(z + steps[1], m), m, d_pre, d_up, blocks)
    (send_1,) = clock.tick([send_1], [near_0, got])
    near_1 = swap(send_1, 1, n)
    other, own_0 = add(keep_0, near_0)
    (other,) = clock.tick([other])
    got_0 = swap(other, top, n)
    if halves:
        total = [own_b[0] + wide(got[0]), own[0] + wide(far_b[0])]
        keys = (bit, bit ^ top)
    else:
        total, keys = own + wide(got), None
    own, values = outward(total, keys)
    values = clock.tick(values, [near_1])
    gained.append(own)
    gained += [wide(value) for value in pass_on(values, keys)]
    other, own_1 = add(keep_1, near_1)
    (other,) = clock.tick([other])
    got_1 = swap(other, top, n)
    clock.tick([], [got_0])
    owns, gots = [own_0, own_1], [got_0, got_1]
    combined = sum(gained)
    grad = 0.0
    for i, step in enumerate(order):
        half, at = divmod(i, m // 2)
        value = owns[half][at] + wide(gots[half][at])
        if step:
            (value,) = clock.tick([value.astype(jnp.bfloat16)])
            value = wide(shift(value, step))
        grad = grad + value
    return combined.astype(jnp.bfloat16), grad.astype(jnp.bfloat16)


def solution(mesh):
    in_specs = (
        P("dp", None),
        P("dp", None),
        P(None, "dp", "etp"),
        P(None, "dp", "etp"),
        P(None, "etp", "dp"),
        P("dp"),
        P("dp"),
        P("dp"),
    )
    out_specs = (P("dp", "etp"), P("dp", "etp"))
    body = functools.partial(shards, mesh.shape["dp"], mesh.shape["etp"])
    return jax.shard_map(body, mesh=mesh, in_specs=in_specs, out_specs=out_specs, check_vma=False)
```

time: 421 us -> 378 us (0.90)
  waiting for transfers between devices: 247 us -> 165 us
  Pallas kernels: 9.84 us -> 74.5 us
  matrix products: 60 us -> 0.26 us
  starting transfers between devices: 37.8 us -> 67.9 us
    pallas_call x0 -> x39, Pallas kernels: none -> 64.5 us  [the longest x2 30.6 us: on_tokens(): pl.pallas_call(functools.partial(kernel, n), grid_spec=pltpu.PrefetchScal...]
    ppermute x24 -> x30, waiting for transfers between devices: 218 us -> 154 us  [swap(): return lax.ppermute(value, 'dp', [(i, i ^ mask) for i in range(size)])]
    dot_general x6 -> x0, matrix products: 59.8 us -> none  [the longest x1 17.3 us: shards(): dot(d_pre, full[0], high) + dot(d_up, full[1], high)]
    ppermute x6 -> x9, starting transfers between devices: 9.35 us -> 44.8 us  [the longest x3 26.8 us: shift(): return lax.ppermute(value, 'etp', [(i, (i + step) % m) for i in range(m)])]
    unnamed x38 -> x110, local copies, waits for them, and re-layouts: 7.97 us -> 37 us
    ppermute x6 -> x9, waiting for transfers between devices: 29.4 us -> 11.4 us  [the longest x6 7.06 us: shift(): return lax.ppermute(value, ('dp', 'etp'), pairs)]
    dynamic_update_slice x16 -> x0, local copies, waits for them, and re-layouts: 17.1 us -> none  [the longest x8 11.4 us: shards(): full = lax.dynamic_update_slice(full, block, (0, (me ^ key) * rows, 0))]
    add x0 -> x2, other arithmetic: none -> 6.66 us  [add(): wide(keep[:, 0]) + wide(near[:, 0])]
  transfers between devices with their start and end apart: 30 -> 39, of which waited for: 14 -> 15; matrix products, arithmetic and copies ran while one was open for 27% -> 6% of each run, Pallas kernels for 2% -> 18%
where the time goes in v2:
time: 378 us; the launch traced here: 374 us
  waiting for transfers between devices  165 us (44%)
  Pallas kernels  74.5 us (20%)
  starting transfers between devices  67.9 us (18%)
  local copies, waits for them, and re-layouts  37 us (10%)
  other arithmetic  28.3 us (7%)
    ppermute x30, waiting for transfers between devices, swap(): return lax.ppermute(value, 'dp', [(i, i ^ mask) for i in range(size)])  154 us
    unnamed x110, local copies, waits for them, and re-layouts  37 us
    pallas_call x2, Pallas kernels, on_tokens(): pl.pallas_call(functools.partial(kernel, n), grid_spec=pltpu.PrefetchScal...  30.6 us
    ppermute x3, starting transfers between devices, shift(): return lax.ppermute(value, 'etp', [(i, (i + step) % m) for i in range(m)])  26.8 us
    ppermute x30, starting transfers between devices, swap(): return lax.ppermute(value, 'dp', [(i, i ^ mask) for i in range(size)])  23 us
    pallas_call x2, Pallas kernels, back(): pl.pallas_call(functools.partial(back_kernel, n), grid_spec=pltpu.Prefetc...  20.9 us
    ppermute x6, starting transfers between devices, shift(): return lax.ppermute(value, ('dp', 'etp'), pairs)  18 us
    pallas_call x3, Pallas kernels, produce(): pl.pallas_call(functools.partial(produce_kernel, keys), grid_spec=pltpu.P...  12.7 us
  transfers between devices with their start and end apart: 39, of which 15 were waited for; matrix products, arithmetic and copies ran while one was open for 6% of the time, Pallas kernels for 18%

profile of v2, /device:TPU:11, one launch (start us, length us, event | category | flops | bytes accessed | tf_op | source)
XLA Modules:
  0.0 374.0 jit_solution(9003491417701131429)
XLA Ops:
  0.8 5.1 %cast_rows.1 = (bf16[2,384,768]{2,1,0:T(8,128)(2,1)S(1)}, bf16[2,384,768]{2,1,0:T(8,128)(2,1)S(1)}, bf16[2,384,768]{2,1,0:T(8,128)(2,1)S(1)}, bf16[2,384,768]{2,1,0:T(8,128)(2,1)S(1)}) custom-call(s32[4]{0:T(128)S(1)} %pad_add_fusion.2.pick_ref, f32[2,384,1536]{2,1,0:T(8,128)} %gate_ref.1, f32[2,384,1536]{2,1,0:T(8,128)} %up_ref.1), custom_call_target="tpu_custom_call" | custom-call | tf_op jit(solution)/shard_map/cast_rows/pallas_call | solution.py:77
  12.9 4.8 %cast_turned.1 = (bf16[384,768]{1,0:T(8,128)(2,1)S(1)}, bf16[384,768]{1,0:T(8,128)(2,1)S(1)}, bf16[384,768]{1,0:T(8,128)(2,1)S(1)}, bf16[384,768]{1,0:T(8,128)(2,1)}) custom-call(s32[4]{0:T(128)S(1)} %pad_add_fusion.2.pick_ref, f32[2,1536,384]{2,1,0:T(8,128)} %down_ref.1, bf16[16,128]{1,0:T(8,128)(2,1)S(1)} %copy-done.7), custom_call_target="tpu_custom_call" | custom-call | tf_op jit(solution)/shard_map/cast_turned/pallas_call | solution.py:105
  25.5 13.2 %collective-permute-done.1.refs_2_ = bf16[2,384,768]{2,1,0:T(8,128)(2,1)} collective-permute-done((bf16[2,384,768]{2,1,0:T(8,128)(2,1)}, bf16[2,384,768]{2,1,0:T(8,128)(2,1)}, u32[]{:S(2)}, u32[]{:S(2)}) %collective-permute-start.1) | collective-permute-done | bytes 1179680 | tf_op jit(solution)/shard_map/ppermute | solution.py:55
  43.9 32.6 %collective-permute-done.4.refs_4_.refs_1_ = bf16[384,768]{1,0:T(8,128)(2,1)} collective-permute-done((bf16[384,768]{1,0:T(8,128)(2,1)}, bf16[384,768]{1,0:T(8,128)(2,1)}, u32[]{:S(2)}, u32[]{:S(2)}) %collective-permute-start.4) | collective-permute-done | bytes 589856 | tf_op jit(solution)/shard_map/ppermute | solution.py:55
  76.6 1.3 collective-permute-start.8
  78.1 1.3 collective-permute-start.9
  79.5 10.7 %collective-permute-done.7.refs_4_.refs_10_.refs_6_ = bf16[2,384,768]{2,1,0:T(8,128)(2,1)} collective-permute-done((bf16[2,384,768]{2,1,0:T(8,128)(2,1)}, bf16[2,384,768]{2,1,0:T(8,128)(2,1)}, u32[]{:S(2)}, u32[]{:S(2)}) %collective-permute-start.7) | collective-permute-done | bytes 1179680 | tf_op jit(solution)/shard_map/ppermute | solution.py:55
  90.1 25.3 %collective-permute-done.10.refs_3_.refs_11_.refs_7_ = bf16[2,384,768]{2,1,0:T(8,128)(2,1)} collective-permute-done((bf16[2,384,768]{2,1,0:T(8,128)(2,1)}, bf16[2,384,768]{2,1,0:T(8,128)(2,1)}, u32[]{:S(2)}, u32[]{:S(2)}) %collective-permute-start.10) | collective-permute-done | bytes 1179680 | tf_op jit(solution)/shard_map/ppermute | solution.py:55
  120.4 13.7 %collective-permute-done.12.refs_4_.refs_0_.refs_6_ = bf16[384,768]{1,0:T(8,128)(2,1)S(1)} collective-permute-done((bf16[384,768]{1,0:T(8,128)(2,1)S(1)}, bf16[384,768]{1,0:T(8,128)(2,1)S(1)}, u32[]{:S(2)}, u32[]{:S(2)}) %collective-permute-start.12) | collective-permute-done | bytes 589856 | tf_op jit(solution)/shard_map/ppermute | solution.py:55
  137.8 18.1 %forward.1 = (bf16[4,256,768]{2,1,0:T(8,128)(2,1)}, bf16[4,256,768]{2,1,0:T(8,128)(2,1)}, bf16[4,256,768]{2,1,0:T(8,128)(2,1)}) custom-call(s32[2]{0:T(128)S(1)} %pad_add_fusion.1.info_ref.me_ref, bf16[272,3072]{1,0:T(8,128)(2,1)} %get-tuple-element.107.refs_0_, bf16[272,3072]{1,0:T(8,128)(2,1)} %collective-permute-done.6.refs_1_.refs_2_, ...), custom_call_target="tpu_custom_call" | custom-call | flops 9663676416 | bytes 15728640 | tf_op jit(solution)/shard_map/forward/pallas_call | solution.py:186
  158.0 6.9 %produce.3 = (bf16[2,2,256,768]{3,2,1,0:T(8,128)(2,1)S(1)}, bf16[2,2,256,768]{3,2,1,0:T(8,128)(2,1)S(1)}) custom-call(s32[1]{0:T(128)} %bitcast.me_ref, s32[2]{0:T(128)S(1)} %pad_add_fusion.ids_ref, bf16[4,256,768]{2,1,0:T(8,128)(2,1)} %get-tuple-element.116.refs_3_.hidden_ref.refs_1_, bf16[384,768]{1,0:T(8,128)(2,1)S(1)} %copy-done.31, ...), custom_call_target="tpu_custom_call" | custom-call | flops 2415919104 | bytes 4718592 | tf_op jit(solution)/shard_map/produce/pallas_call | solution.py:238
  166.1 4.2 %collective-permute-done.15.refs_1_ = bf16[256,3072]{1,0:T(8,128)(2,1)} collective-permute-done((bf16[256,3072]{1,0:T(8,128)(2,1)}, bf16[256,3072]{1,0:T(8,128)(2,1)}, u32[]{:S(2)}, u32[]{:S(2)}) %collective-permute-start.15) | collective-permute-done | bytes 1572896 | tf_op jit(solution)/shard_map/ppermute | solution.py:55
  170.3 1.7 collective-permute-start.17
  173.9 1.4 copy-done.38
  175.3 2.9 produce.4
  179.0 8.3 %collective-permute-done.18.refs_3_.refs_2_.refs_0_.refs_10_ = bf16[384,768]{1,0:T(8,128)(2,1)} collective-permute-done((bf16[384,768]{1,0:T(8,128)(2,1)}, bf16[384,768]{1,0:T(8,128)(2,1)}, u32[]{:S(2)}, u32[]{:S(2)}) %collective-permute-start.18) | collective-permute-done | bytes 589856 | tf_op jit(solution)/shard_map/ppermute | solution.py:55
  189.2 3.1 convert_add_fusion.2
  192.8 1.9 fusion.27.refs_1_
  194.6 8.7 %collective-permute-done.21.refs_2_.refs_3_.refs_1_.refs_11_ = bf16[384,768]{1,0:T(8,128)(2,1)} collective-permute-done((bf16[384,768]{1,0:T(8,128)(2,1)}, bf16[384,768]{1,0:T(8,128)(2,1)}, u32[]{:S(2)}, u32[]{:S(2)}) %collective-permute-start.21) | collective-permute-done | bytes 589856 | tf_op jit(solution)/shard_map/ppermute | solution.py:55
  203.8 7.8 %collective-permute-done.20.refs_1_ = bf16[2,256,768]{2,1,0:T(8,128)(2,1)} collective-permute-done((bf16[2,256,768]{2,1,0:T(8,128)(2,1)}, bf16[2,256,768]{2,1,0:T(8,128)(2,1)}, u32[]{:S(2)}, u32[]{:S(2)}) %collective-permute-start.20) | collective-permute-done | bytes 786464 | tf_op jit(solution)/shard_map/ppermute | solution.py:55
  211.6 2.1 select_bitcast_fusion
  214.6 5.4 %collective-permute-done.22.refs_2_ = bf16[1,256,768]{2,1,0:T(8,128)(2,1)} collective-permute-done((bf16[1,256,768]{2,1,0:T(8,128)(2,1)}, bf16[1,256,768]{2,1,0:T(8,128)(2,1)}, u32[]{:S(2)}, u32[]{:S(2)}) %collective-permute-start.22) | collective-permute-done | bytes 393248 | tf_op jit(solution)/shard_map/ppermute | solution.py:55
  220.0 1.4 copy-done.39
  221.4 2.9 produce.5
  226.2 4.2 %collective-permute-start.23 = (bf16[256,768]{1,0:T(8,128)(2,1)}, bf16[256,768]{1,0:T(8,128)(2,1)}, u32[]{:S(2)}, u32[]{:S(2)}) collective-permute-start(bf16[256,768]{1,0:T(8,128)(2,1)} %get-tuple-element.140), channel_id=1, source_target_pairs={{0,2},{2,0},{4,6},{6,4},{9,11},{11,9},{13,15},{15,13},{16,18},{18,... | collective-permute-start | bytes 1179656 | tf_op jit(solution)/shard_map/ppermute | solution.py:365
  230.4 1.3 collective-permute-start.24
  231.7 1.5 collective-permute-start.25
  235.4 12.6 %grow.1 = (bf16[4,256,768]{2,1,0:T(8,128)(2,1)}, bf16[4,256,768]{2,1,0:T(8,128)(2,1)}) custom-call(s32[2]{0:T(128)S(1)} %pad_add_fusion.1.info_ref.me_ref, bf16[4,256,768]{2,1,0:T(8,128)(2,1)} %get-tuple-element.149.slope_ref, bf16[4,256,768]{2,1,0:T(8,128)(2,1)} %get-tuple-element.150.active_ref, bf16[256,3072]{1,0:T(8,128)(2,1)} %get-tuple-element.151.refs_0_, ...), custom_call_target="tpu_custom_call" | custom-call | flops 4831838208 | bytes 11010048 | tf_op jit(solution)/shard_map/grow/pallas_call | solution.py:186
  252.3 10.6 %back.2 = (bf16[2,2,256,768]{3,2,1,0:T(8,128)(2,1)}, bf16[2,2,256,768]{3,2,1,0:T(8,128)(2,1)}) custom-call(s32[1]{0:T(128)} %bitcast.me_ref, s32[2]{0:T(128)S(1)} %compare_select_fusion.3.ids_ref, bf16[4,256,768]{2,1,0:T(8,128)(2,1)} %get-tuple-element.158.pre_ref.refs_2_, bf16[4,256,768]{2,1,0:T(8,128)(2,1)} %get-tuple-element.159.up_ref, ...), custom_call_target="tpu_custom_call" | custom-call | flops 4831838208 | bytes 7864320 | tf_op jit(solution)/shard_map/back/pallas_call | solution.py:289
  265.3 1.3 copy-done.21
  266.5 10.4 %back.3 = (bf16[2,2,256,768]{3,2,1,0:T(8,128)(2,1)}, bf16[2,2,256,768]{3,2,1,0:T(8,128)(2,1)}) custom-call(s32[1]{0:T(128)} %bitcast.me_ref, s32[2]{0:T(128)S(1)} %compare_select_fusion.1.ids_ref, bf16[4,256,768]{2,1,0:T(8,128)(2,1)} %get-tuple-element.162.pre_ref, bf16[4,256,768]{2,1,0:T(8,128)(2,1)} %get-tuple-element.159.up_ref, ...), custom_call_target="tpu_custom_call" | custom-call | flops 4831838208 | bytes 7864320 | tf_op jit(solution)/shard_map/back/pallas_call | solution.py:289
  278.5 3.6 convert_add_fusion.1
  282.1 2.0 collective-permute-start.34
  284.1 2.2 broadcast_select_fusion
  287.2 15.0 %collective-permute-done.34.refs_1_ = bf16[2,256,768]{2,1,0:T(8,128)(2,1)S(1)} collective-permute-done((bf16[2,256,768]{2,1,0:T(8,128)(2,1)}, bf16[2,256,768]{2,1,0:T(8,128)(2,1)S(1)}, u32[]{:S(2)}, u32[]{:S(2)}) %collective-permute-start.34) | collective-permute-done | bytes 786464 | tf_op jit(solution)/shard_map/ppermute | solution.py:55
  304.2 3.2 fusion.2
  308.6 2.7 collective-permute-start.36
  311.3 1.9 collective-permute-start.35
  313.2 1.4 collective-permute-start.31
  314.6 3.6 collective-permute-start.32
  318.2 7.9 %collective-permute-done.37 = bf16[2,256,768]{2,1,0:T(8,128)(2,1)S(1)} collective-permute-done((bf16[2,256,768]{2,1,0:T(8,128)(2,1)}, bf16[2,256,768]{2,1,0:T(8,128)(2,1)S(1)}, u32[]{:S(2)}, u32[]{:S(2)}) %collective-permute-start.37) | collective-permute-done | bytes 786464 | tf_op jit(solution)/shard_map/ppermute | solution.py:55
  326.2 6.1 %collective-permute-start.33 = (bf16[256,768]{1,0:T(8,128)(2,1)}, bf16[256,768]{1,0:T(8,128)(2,1)}, u32[]{:S(2)}, u32[]{:S(2)}) collective-permute-start(bf16[256,768]{1,0:T(8,128)(2,1)} %get-tuple-element.171), channel_id=1, source_target_pairs={{0,3},{2,1},{4,7},{6,5},{9,8},{11,10},{13,12},{15,14},{16,19},{18,... | collective-permute-start | bytes 1179656 | tf_op jit(solution)/shard_map/ppermute | solution.py:365
  332.2 2.0 fusion.31.refs_1_
  334.2 22.2 %collective-permute-start.38 = (bf16[256,768]{1,0:T(8,128)(2,1)}, bf16[256,768]{1,0:T(8,128)(2,1)S(1)}, u32[]{:S(2)}, u32[]{:S(2)}) collective-permute-start(bf16[256,768]{1,0:T(8,128)(2,1)} %get-tuple-element.181), channel_id=1, source_target_pairs={{0,3},{1,0},{2,1},{3,2},{4,7},{5,4},{6,5},{7,6},{8,11},{9,8},{10,9... | collective-permute-start | bytes 1179656 | tf_op jit(solution)/shard_map/ppermute | solution.py:358
  356.4 7.0 %collective-permute-done.33 = bf16[256,768]{1,0:T(8,128)(2,1)} collective-permute-done((bf16[256,768]{1,0:T(8,128)(2,1)}, bf16[256,768]{1,0:T(8,128)(2,1)}, u32[]{:S(2)}, u32[]{:S(2)}) %collective-permute-start.33) | collective-permute-done | bytes 393248 | tf_op jit(solution)/shard_map/ppermute | solution.py:365
  363.4 4.1 %fusion.21 = bf16[256,768]{1,0:T(8,128)(2,1)} fusion(bf16[256,768]{1,0:T(8,128)(2,1)} %collective-permute-done.33, bf16[256,768]{1,0:T(8,128)(2,1)} %collective-permute-done.32, bf16[256,768]{1,0:T(8,128)(2,1)} %collective-permute-done.31, bf16[256,768]{1,0:T(8,128)(2,1)} %collective-permute-done.25.refs_5_, ...), kind=kLoop, calls=%fused_computation.36 | loop fusion | flops 6291456 | bytes 7471108 | tf_op jit(solution)/shard_map/convert_element_type | solution.py:521
  367.5 4.3 %collective-permute-done.38 = bf16[256,768]{1,0:T(8,128)(2,1)S(1)} collective-permute-done((bf16[256,768]{1,0:T(8,128)(2,1)}, bf16[256,768]{1,0:T(8,128)(2,1)S(1)}, u32[]{:S(2)}, u32[]{:S(2)}) %collective-permute-start.38) | collective-permute-done | bytes 393248 | tf_op jit(solution)/shard_map/ppermute | solution.py:358
  371.8 2.1 fusion.6
  (202 shorter events, 55.2 us)
Async XLA Ops:
  0.6 19.5 %copy-start = (s32[4]{0:T(128)S(1)}, s32[4]{0:T(128)}, u32[]{:S(2)}) copy-start(s32[4]{0:T(128)} %param.16) | copy-start | bytes 52
  10.0 10.2 %collective-permute-start = (bf16[2,384,768]{2,1,0:T(8,128)(2,1)}, bf16[2,384,768]{2,1,0:T(8,128)(2,1)S(1)}, u32[]{:S(2)}, u32[]{:S(2)}) collective-permute-start(bf16[2,384,768]{2,1,0:T(8,128)(2,1)} %get-tuple-element.97), channel_id=1, source_target_pairs={{0,4},{4,0},{8,12},{12,8},{16,20},{20,16},{24,28},{28,24},{1,5},{5... | collective-permute-start | bytes 3538952 | tf_op jit(solution)/shard_map/ppermute | solution.py:55
  10.7 27.9 %collective-permute-start.1 = (bf16[2,384,768]{2,1,0:T(8,128)(2,1)}, bf16[2,384,768]{2,1,0:T(8,128)(2,1)}, u32[]{:S(2)}, u32[]{:S(2)}) collective-permute-start(bf16[2,384,768]{2,1,0:T(8,128)(2,1)} %get-tuple-element.100), channel_id=1, source_target_pairs={{0,16},{4,20},{8,24},{12,28},{16,0},{20,4},{24,8},{28,12},{1,17},{... | collective-permute-start | bytes 3538952 | tf_op jit(solution)/shard_map/ppermute | solution.py:55
  12.0 27.6 %collective-permute-start.2 = (bf16[2,384,768]{2,1,0:T(8,128)(2,1)}, bf16[2,384,768]{2,1,0:T(8,128)(2,1)S(1)}, u32[]{:S(2)}, u32[]{:S(2)}) collective-permute-start(bf16[2,384,768]{2,1,0:T(8,128)(2,1)} %get-tuple-element.101.refs_4_.refs_0_), channel_id=1, source_target_pairs={{0,8},{4,12},{8,0},{12,4},{16,24},{20,28},{24,16},{28,20},{1,9},{5... | collective-permute-start | bytes 3538952 | tf_op jit(solution)/shard_map/ppermute | solution.py:55
  12.9 7.3 %copy-start.50 = (s32[512]{0:T(512)S(1)}, s32[512]{0:T(512)}, u32[]{:S(2)}) copy-start(s32[512]{0:T(512)} %param.15) | copy-start | bytes 6148
  21.3 55.2 %collective-permute-start.3 = (bf16[2,384,768]{2,1,0:T(8,128)(2,1)}, bf16[2,384,768]{2,1,0:T(8,128)(2,1)}, u32[]{:S(2)}, u32[]{:S(2)}) collective-permute-start(bf16[2,384,768]{2,1,0:T(8,128)(2,1)} %get-tuple-element.104), channel_id=1, source_target_pairs={{0,20},{4,16},{8,28},{12,24},{16,4},{20,0},{24,12},{28,8},{1,21},{... | collective-permute-start | bytes 3538952 | tf_op jit(solution)/shard_map/ppermute | solution.py:55
  22.0 54.5 %collective-permute-start.5 = (bf16[2,384,768]{2,1,0:T(8,128)(2,1)}, bf16[2,384,768]{2,1,0:T(8,128)(2,1)}, u32[]{:S(2)}, u32[]{:S(2)}) collective-permute-start(bf16[2,384,768]{2,1,0:T(8,128)(2,1)} %get-tuple-element.106.refs_5_.refs_1_), channel_id=1, source_target_pairs={{0,8},{4,12},{8,0},{12,4},{16,24},{20,28},{24,16},{28,20},{1,9},{5... | collective-permute-start | bytes 3538952 | tf_op jit(solution)/shard_map/ppermute | solution.py:55
  40.6 36.0 %collective-permute-start.4 = (bf16[384,768]{1,0:T(8,128)(2,1)}, bf16[384,768]{1,0:T(8,128)(2,1)}, u32[]{:S(2)}, u32[]{:S(2)}) collective-permute-start(bf16[384,768]{1,0:T(8,128)(2,1)} %get-tuple-element.105), channel_id=1, source_target_pairs={{0,16},{4,20},{8,24},{12,28},{16,0},{20,4},{24,8},{28,12},{1,17},{... | collective-permute-start | bytes 1769480 | tf_op jit(solution)/shard_map/ppermute | solution.py:55
  40.9 49.2 %collective-permute-start.7 = (bf16[2,384,768]{2,1,0:T(8,128)(2,1)}, bf16[2,384,768]{2,1,0:T(8,128)(2,1)}, u32[]{:S(2)}, u32[]{:S(2)}) collective-permute-start(bf16[2,384,768]{2,1,0:T(8,128)(2,1)} %get-tuple-element.111.refs_8_.refs_4_), channel_id=1, source_target_pairs={{0,8},{4,12},{8,0},{12,4},{16,24},{20,28},{24,16},{28,20},{1,9},{5... | collective-permute-start | bytes 3538952 | tf_op jit(solution)/shard_map/ppermute | solution.py:55
  76.6 38.8 %collective-permute-start.8 = (bf16[272,3072]{1,0:T(8,128)(2,1)}, bf16[272,3072]{1,0:T(8,128)(2,1)S(1)}, u32[]{:S(2)}, u32[]{:S(2)}) collective-permute-start(bf16[272,3072]{1,0:T(8,128)(2,1)} %get-tuple-element.107.refs_0_), channel_id=1, source_target_pairs={{0,16},{4,20},{8,24},{12,28},{16,0},{20,4},{24,8},{28,12},{1,17},{... | collective-permute-start | bytes 5013512 | tf_op jit(solution)/shard_map/ppermute | solution.py:55
  77.9 37.5 %collective-permute-start.10 = (bf16[2,384,768]{2,1,0:T(8,128)(2,1)}, bf16[2,384,768]{2,1,0:T(8,128)(2,1)}, u32[]{:S(2)}, u32[]{:S(2)}) collective-permute-start(bf16[2,384,768]{2,1,0:T(8,128)(2,1)} %get-tuple-element.114.refs_9_.refs_5_), channel_id=1, source_target_pairs={{0,8},{4,12},{8,0},{12,4},{16,24},{20,28},{24,16},{28,20},{1,9},{5... | collective-permute-start | bytes 3538952 | tf_op jit(solution)/shard_map/ppermute | solution.py:55
  78.1 12.0 %collective-permute-start.9 = (bf16[384,768]{1,0:T(8,128)(2,1)}, bf16[384,768]{1,0:T(8,128)(2,1)S(1)}, u32[]{:S(2)}, u32[]{:S(2)}) collective-permute-start(bf16[384,768]{1,0:T(8,128)(2,1)} %get-tuple-element.113), channel_id=1, source_target_pairs={{0,4},{4,0},{8,12},{12,8},{16,20},{20,16},{24,28},{28,24},{1,5},{5... | collective-permute-start | bytes 1769480 | tf_op jit(solution)/shard_map/ppermute | solution.py:55
  79.5 54.9 %collective-permute-start.6 = (bf16[272,3072]{1,0:T(8,128)(2,1)}, bf16[272,3072]{1,0:T(8,128)(2,1)}, u32[]{:S(2)}, u32[]{:S(2)}) collective-permute-start(bf16[272,3072]{1,0:T(8,128)(2,1)} %get-tuple-element.107.refs_0_), channel_id=1, source_target_pairs={{0,4},{4,0},{8,12},{12,8},{16,20},{20,16},{24,28},{28,24},{1,5},{5... | collective-permute-start | bytes 5013512 | tf_op jit(solution)/shard_map/ppermute | solution.py:55
  90.1 26.5 %copy-start.35 = (bf16[384,768]{1,0:T(8,128)(2,1)}, bf16[384,768]{1,0:T(8,128)(2,1)S(1)}, u32[]{:S(2)}) copy-start(bf16[384,768]{1,0:T(8,128)(2,1)S(1)} %collective-permute-done.9.refs_2_) | copy-start | bytes 1769476
  116.7 2.5 copy-start.30
  116.7 17.7 %collective-permute-start.11 = (bf16[272,3072]{1,0:T(8,128)(2,1)}, bf16[272,3072]{1,0:T(8,128)(2,1)}, u32[]{:S(2)}, u32[]{:S(2)}) collective-permute-start(bf16[272,3072]{1,0:T(8,128)(2,1)} %get-tuple-element.115.refs_2_), channel_id=1, source_target_pairs={{0,4},{4,0},{8,12},{12,8},{16,20},{20,16},{24,28},{28,24},{1,5},{5... | collective-permute-start | bytes 5013512 | tf_op jit(solution)/shard_map/ppermute | solution.py:55
  118.1 16.3 %collective-permute-start.16 = (bf16[256,3072]{1,0:T(8,128)(2,1)S(1)}, bf16[256,3072]{1,0:T(8,128)(2,1)}, u32[]{:S(2)}, u32[]{:S(2)}) collective-permute-start(bf16[256,3072]{1,0:T(8,128)(2,1)S(1)} %copy-done.6), channel_id=1, source_target_pairs={{0,4},{4,0},{8,12},{12,8},{16,20},{20,16},{24,28},{28,24},{1,5},{5... | collective-permute-start | bytes 4718600 | tf_op jit(solution)/shard_map/ppermute | solution.py:55
  119.2 14.9 %collective-permute-start.12 = (bf16[384,768]{1,0:T(8,128)(2,1)S(1)}, bf16[384,768]{1,0:T(8,128)(2,1)S(1)}, u32[]{:S(2)}, u32[]{:S(2)}) collective-permute-start(bf16[384,768]{1,0:T(8,128)(2,1)S(1)} %copy-done.30), channel_id=1, source_target_pairs={{0,8},{4,12},{8,0},{12,4},{16,24},{20,28},{24,16},{28,20},{1,9},{5... | collective-permute-start | bytes 1769480 | tf_op jit(solution)/shard_map/ppermute | solution.py:55
  119.6 36.3 %collective-permute-start.14 = (bf16[384,768]{1,0:T(8,128)(2,1)}, bf16[384,768]{1,0:T(8,128)(2,1)}, u32[]{:S(2)}, u32[]{:S(2)}) collective-permute-start(bf16[384,768]{1,0:T(8,128)(2,1)} %get-tuple-element.123), channel_id=1, source_target_pairs={{0,20},{4,16},{8,28},{12,24},{16,4},{20,0},{24,12},{28,8},{1,21},{... | collective-permute-start | bytes 1769480 | tf_op jit(solution)/shard_map/ppermute | solution.py:55
  134.1 21.8 %collective-permute-start.13 = (bf16[384,768]{1,0:T(8,128)(2,1)}, bf16[384,768]{1,0:T(8,128)(2,1)}, u32[]{:S(2)}, u32[]{:S(2)}) collective-permute-start(bf16[384,768]{1,0:T(8,128)(2,1)} %get-tuple-element.118.refs_1_.refs_5_), channel_id=1, source_target_pairs={{0,8},{4,12},{8,0},{12,4},{16,24},{20,28},{24,16},{28,20},{1,9},{5... | collective-permute-start | bytes 1769480 | tf_op jit(solution)/shard_map/ppermute | solution.py:55
  134.9 35.4 %collective-permute-start.15 = (bf16[256,3072]{1,0:T(8,128)(2,1)}, bf16[256,3072]{1,0:T(8,128)(2,1)}, u32[]{:S(2)}, u32[]{:S(2)}) collective-permute-start(bf16[256,3072]{1,0:T(8,128)(2,1)} %get-tuple-element.126.refs_2_), channel_id=1, source_target_pairs={{0,16},{4,20},{8,24},{12,28},{16,0},{20,4},{24,8},{28,12},{1,17},{... | collective-permute-start | bytes 4718600 | tf_op jit(solution)/shard_map/ppermute | solution.py:55
  170.3 17.0 %collective-permute-start.17 = (bf16[2,2,256,768]{3,2,1,0:T(8,128)(2,1)}, bf16[2,2,256,768]{3,2,1,0:T(8,128)(2,1)}, u32[]{:S(2)}, u32[]{:S(2)}) collective-permute-start(bf16[2,2,256,768]{3,2,1,0:T(8,128)(2,1)} %get-tuple-element.129), channel_id=1, source_target_pairs={{0,4},{4,0},{8,12},{12,8},{16,20},{20,16},{24,28},{28,24},{1,5},{5... | collective-permute-start | bytes 4718600 | tf_op jit(solution)/shard_map/ppermute | solution.py:55
  172.0 15.3 %collective-permute-start.18 = (bf16[384,768]{1,0:T(8,128)(2,1)}, bf16[384,768]{1,0:T(8,128)(2,1)}, u32[]{:S(2)}, u32[]{:S(2)}) collective-permute-start(bf16[384,768]{1,0:T(8,128)(2,1)} %get-tuple-element.122.refs_2_.refs_8_), channel_id=1, source_target_pairs={{0,8},{4,12},{8,0},{12,4},{16,24},{20,28},{24,16},{28,20},{1,9},{5... | collective-permute-start | bytes 1769480 | tf_op jit(solution)/shard_map/ppermute | solution.py:55
  187.3 5.0 %collective-permute-start.19 = (bf16[1,2,256,768]{3,2,1,0:T(8,128)(2,1)}, bf16[1,2,256,768]{3,2,1,0:T(8,128)(2,1)}, u32[]{:S(2)}, u32[]{:S(2)}) collective-permute-start(bf16[1,2,256,768]{3,2,1,0:T(8,128)(2,1)} %get-tuple-element.133), channel_id=1, source_target_pairs={{0,4},{4,0},{8,12},{12,8},{16,20},{20,16},{24,28},{28,24},{1,5},{5... | collective-permute-start | bytes 2359304 | tf_op jit(solution)/shard_map/ppermute | solution.py:55
  188.1 15.2 %collective-permute-start.21 = (bf16[384,768]{1,0:T(8,128)(2,1)}, bf16[384,768]{1,0:T(8,128)(2,1)}, u32[]{:S(2)}, u32[]{:S(2)}) collective-permute-start(bf16[384,768]{1,0:T(8,128)(2,1)} %get-tuple-element.137.refs_9_), channel_id=1, source_target_pairs={{0,8},{4,12},{8,0},{12,4},{16,24},{20,28},{24,16},{28,20},{1,9},{5... | collective-permute-start | bytes 1769480 | tf_op jit(solution)/shard_map/ppermute | solution.py:55
  188.9 31.2 %collective-permute-start.26 = (bf16[256,3072]{1,0:T(8,128)(2,1)}, bf16[256,3072]{1,0:T(8,128)(2,1)}, u32[]{:S(2)}, u32[]{:S(2)}) collective-permute-start(bf16[256,3072]{1,0:T(8,128)(2,1)} %get-tuple-element.144.refs_2_), channel_id=1, source_target_pairs={{0,4},{4,0},{8,12},{12,8},{16,20},{20,16},{24,28},{28,24},{1,5},{5... | collective-permute-start | bytes 4718600 | tf_op jit(solution)/shard_map/ppermute | solution.py:55
  192.3 19.3 %collective-permute-start.20 = (bf16[2,256,768]{2,1,0:T(8,128)(2,1)}, bf16[2,256,768]{2,1,0:T(8,128)(2,1)}, u32[]{:S(2)}, u32[]{:S(2)}) collective-permute-start(bf16[2,256,768]{2,1,0:T(8,128)(2,1)} %get-tuple-element.134), channel_id=1, source_target_pairs={{0,16},{4,20},{8,24},{12,28},{16,0},{20,4},{24,8},{28,12},{1,17},{... | collective-permute-start | bytes 2359304 | tf_op jit(solution)/shard_map/ppermute | solution.py:55
  203.3 8.3 %copy-start.40 = (f32[2,1,256,768]{3,2,1,0:T(8,128)S(1)}, f32[2,1,256,768]{3,2,1,0:T(8,128)}, u32[]{:S(2)}) copy-start(f32[2,1,256,768]{3,2,1,0:T(8,128)} %get-tuple-element.192) | copy-start | bytes 4718596
  203.3 16.7 %collective-permute-start.22 = (bf16[1,256,768]{2,1,0:T(8,128)(2,1)}, bf16[1,256,768]{2,1,0:T(8,128)(2,1)}, u32[]{:S(2)}, u32[]{:S(2)}) collective-permute-start(bf16[1,256,768]{2,1,0:T(8,128)(2,1)} %get-tuple-element.139), channel_id=1, source_target_pairs={{0,16},{4,20},{8,24},{12,28},{16,0},{20,4},{24,8},{28,12},{1,17},{... | collective-permute-start | bytes 1179656 | tf_op jit(solution)/shard_map/ppermute | solution.py:55
  225.2 8.0 %copy-start.28 = (bf16[384,768]{1,0:T(8,128)(2,1)S(1)}, bf16[384,768]{1,0:T(8,128)(2,1)}, u32[]{:S(2)}) copy-start(bf16[384,768]{1,0:T(8,128)(2,1)} %copy-done.26) | copy-start | bytes 1769476
  225.2 22.7 %collective-permute-start.27 = (bf16[1,2,256,768]{3,2,1,0:T(8,128)(2,1)}, bf16[1,2,256,768]{3,2,1,0:T(8,128)(2,1)S(1)}, u32[]{:S(2)}, u32[]{:S(2)}) collective-permute-start(bf16[1,2,256,768]{3,2,1,0:T(8,128)(2,1)} %get-tuple-element.153), channel_id=1, source_target_pairs={{0,4},{4,0},{8,12},{12,8},{16,20},{20,16},{24,28},{28,24},{1,5},{5... | collective-permute-start | bytes 2359304 | tf_op jit(solution)/shard_map/ppermute | solution.py:55
  226.2 36.6 %collective-permute-start.23 = (bf16[256,768]{1,0:T(8,128)(2,1)}, bf16[256,768]{1,0:T(8,128)(2,1)}, u32[]{:S(2)}, u32[]{:S(2)}) collective-permute-start(bf16[256,768]{1,0:T(8,128)(2,1)} %get-tuple-element.140), channel_id=1, source_target_pairs={{0,2},{2,0},{4,6},{6,4},{9,11},{11,9},{13,15},{15,13},{16,18},{18,... | collective-permute-start | bytes 1179656 | tf_op jit(solution)/shard_map/ppermute | solution.py:365
  230.4 32.4 %collective-permute-start.24 = (bf16[256,768]{1,0:T(8,128)(2,1)}, bf16[256,768]{1,0:T(8,128)(2,1)}, u32[]{:S(2)}, u32[]{:S(2)}) collective-permute-start(bf16[256,768]{1,0:T(8,128)(2,1)} %get-tuple-element.141), channel_id=1, source_target_pairs={{1,2},{3,0},{5,6},{7,4},{8,9},{10,11},{12,13},{14,15},{17,18},{19,... | collective-permute-start | bytes 1179656 | tf_op jit(solution)/shard_map/ppermute | solution.py:365
  231.7 31.1 %collective-permute-start.25 = (bf16[256,768]{1,0:T(8,128)(2,1)}, bf16[256,768]{1,0:T(8,128)(2,1)}, u32[]{:S(2)}, u32[]{:S(2)}) collective-permute-start(bf16[256,768]{1,0:T(8,128)(2,1)} %get-tuple-element.142), channel_id=1, source_target_pairs={{1,0},{3,2},{5,4},{7,6},{8,11},{10,9},{12,15},{14,13},{17,16},{19,... | collective-permute-start | bytes 1179656 | tf_op jit(solution)/shard_map/ppermute | solution.py:365
  262.9 14.0 %collective-permute-start.29 = (bf16[2,2,256,768]{3,2,1,0:T(8,128)(2,1)}, bf16[2,2,256,768]{3,2,1,0:T(8,128)(2,1)}, u32[]{:S(2)}, u32[]{:S(2)}) collective-permute-start(bf16[2,2,256,768]{3,2,1,0:T(8,128)(2,1)} %get-tuple-element.164), channel_id=1, source_target_pairs={{0,4},{4,0},{8,12},{12,8},{16,20},{20,16},{24,28},{28,24},{1,5},{5... | collective-permute-start | bytes 4718600 | tf_op jit(solution)/shard_map/ppermute | solution.py:55
  263.9 13.0 %collective-permute-start.28 = (bf16[1,256,768]{2,1,0:T(8,128)(2,1)S(1)}, bf16[1,256,768]{2,1,0:T(8,128)(2,1)S(1)}, u32[]{:S(2)}, u32[]{:S(2)}) collective-permute-start(bf16[1,256,768]{2,1,0:T(8,128)(2,1)S(1)} %copy-done.49), channel_id=1, source_target_pairs={{0,16},{4,20},{8,24},{12,28},{16,0},{20,4},{24,8},{28,12},{1,17},{... | collective-permute-start | bytes 1179656 | tf_op jit(solution)/shard_map/ppermute | solution.py:55
  277.7 25.7 %collective-permute-start.30 = (bf16[2,2,256,768]{3,2,1,0:T(8,128)(2,1)}, bf16[2,2,256,768]{3,2,1,0:T(8,128)(2,1)}, u32[]{:S(2)}, u32[]{:S(2)}) collective-permute-start(bf16[2,2,256,768]{3,2,1,0:T(8,128)(2,1)} %get-tuple-element.168), channel_id=1, source_target_pairs={{0,4},{4,0},{8,12},{12,8},{16,20},{20,16},{24,28},{28,24},{1,5},{5... | collective-permute-start | bytes 4718600 | tf_op jit(solution)/shard_map/ppermute | solution.py:55
  282.1 20.1 %collective-permute-start.34 = (bf16[2,256,768]{2,1,0:T(8,128)(2,1)}, bf16[2,256,768]{2,1,0:T(8,128)(2,1)S(1)}, u32[]{:S(2)}, u32[]{:S(2)}) collective-permute-start(bf16[2,256,768]{2,1,0:T(8,128)(2,1)} %get-tuple-element.175), channel_id=1, source_target_pairs={{0,16},{4,20},{8,24},{12,28},{16,0},{20,4},{24,8},{28,12},{1,17},{... | collective-permute-start | bytes 2359304 | tf_op jit(solution)/shard_map/ppermute | solution.py:55
  286.3 15.9 %copy-start.41 = (f32[2,1,256,768]{3,2,1,0:T(8,128)S(1)}, f32[2,1,256,768]{3,2,1,0:T(8,128)}, u32[]{:S(2)}) copy-start(f32[2,1,256,768]{3,2,1,0:T(8,128)} %get-tuple-element.188) | copy-start | bytes 4718596
  307.3 18.8 %collective-permute-start.37 = (bf16[2,256,768]{2,1,0:T(8,128)(2,1)}, bf16[2,256,768]{2,1,0:T(8,128)(2,1)S(1)}, u32[]{:S(2)}, u32[]{:S(2)}) collective-permute-start(bf16[2,256,768]{2,1,0:T(8,128)(2,1)} %get-tuple-element.180), channel_id=1, source_target_pairs={{0,16},{4,20},{8,24},{12,28},{16,0},{20,4},{24,8},{28,12},{1,17},{... | collective-permute-start | bytes 2359304 | tf_op jit(solution)/shard_map/ppermute | solution.py:55
  308.6 58.9 %collective-permute-start.36 = (bf16[256,768]{1,0:T(8,128)(2,1)}, bf16[256,768]{1,0:T(8,128)(2,1)}, u32[]{:S(2)}, u32[]{:S(2)}) collective-permute-start(bf16[256,768]{1,0:T(8,128)(2,1)} %get-tuple-element.178), channel_id=1, source_target_pairs={{0,1},{1,2},{2,3},{3,0},{4,5},{5,6},{6,7},{7,4},{8,9},{9,10},{10,1... | collective-permute-start | bytes 1179656 | tf_op jit(solution)/shard_map/ppermute | solution.py:358
  311.3 56.2 %collective-permute-start.35 = (bf16[256,768]{1,0:T(8,128)(2,1)}, bf16[256,768]{1,0:T(8,128)(2,1)}, u32[]{:S(2)}, u32[]{:S(2)}) collective-permute-start(bf16[256,768]{1,0:T(8,128)(2,1)} %get-tuple-element.176), channel_id=1, source_target_pairs={{0,2},{1,3},{2,0},{3,1},{4,6},{5,7},{6,4},{7,5},{8,10},{9,11},{10,... | collective-permute-start | bytes 1179656 | tf_op jit(solution)/shard_map/ppermute | solution.py:358
  313.2 21.0 %collective-permute-start.31 = (bf16[256,768]{1,0:T(8,128)(2,1)}, bf16[256,768]{1,0:T(8,128)(2,1)}, u32[]{:S(2)}, u32[]{:S(2)}) collective-permute-start(bf16[256,768]{1,0:T(8,128)(2,1)} %get-tuple-element.169), channel_id=1, source_target_pairs={{1,3},{3,1},{5,7},{7,5},{8,10},{10,8},{12,14},{14,12},{17,19},{19,... | collective-permute-start | bytes 1179656 | tf_op jit(solution)/shard_map/ppermute | solution.py:365
  314.6 41.7 %collective-permute-start.32 = (bf16[256,768]{1,0:T(8,128)(2,1)}, bf16[256,768]{1,0:T(8,128)(2,1)}, u32[]{:S(2)}, u32[]{:S(2)}) collective-permute-start(bf16[256,768]{1,0:T(8,128)(2,1)} %get-tuple-element.170), channel_id=1, source_target_pairs={{0,1},{2,3},{4,5},{6,7},{9,10},{11,8},{13,14},{15,12},{16,17},{18,... | collective-permute-start | bytes 1179656 | tf_op jit(solution)/shard_map/ppermute | solution.py:365
  326.2 37.2 %collective-permute-start.33 = (bf16[256,768]{1,0:T(8,128)(2,1)}, bf16[256,768]{1,0:T(8,128)(2,1)}, u32[]{:S(2)}, u32[]{:S(2)}) collective-permute-start(bf16[256,768]{1,0:T(8,128)(2,1)} %get-tuple-element.171), channel_id=1, source_target_pairs={{0,3},{2,1},{4,7},{6,5},{9,8},{11,10},{13,12},{15,14},{16,19},{18,... | collective-permute-start | bytes 1179656 | tf_op jit(solution)/shard_map/ppermute | solution.py:365
  334.2 37.7 %copy-start.42 = (f32[2,1,256,768]{3,2,1,0:T(8,128)S(1)}, f32[2,1,256,768]{3,2,1,0:T(8,128)}, u32[]{:S(2)}) copy-start(f32[2,1,256,768]{3,2,1,0:T(8,128)} %get-tuple-element.191) | copy-start | bytes 4718596
  334.2 37.7 %collective-permute-start.38 = (bf16[256,768]{1,0:T(8,128)(2,1)}, bf16[256,768]{1,0:T(8,128)(2,1)S(1)}, u32[]{:S(2)}, u32[]{:S(2)}) collective-permute-start(bf16[256,768]{1,0:T(8,128)(2,1)} %get-tuple-element.181), channel_id=1, source_target_pairs={{0,3},{1,0},{2,1},{3,2},{4,7},{5,4},{6,5},{7,6},{8,11},{9,8},{10,9... | collective-permute-start | bytes 1179656 | tf_op jit(solution)/shard_map/ppermute | solution.py:358
  363.4 10.6 %copy-start.1 = (s32[4]{0:T(128)S(1)}, s32[4]{0:T(128)}, u32[]{:S(2)}) copy-start(s32[4]{0:T(128)} %param.16) | copy-start | bytes 52
  (46 other events, 54.2 us)

commit v3 on v2

--- a/solution.py
+++ b/solution.py
@@ -82,7 +82,7 @@
             in_specs=[block, block],
             out_specs=[pl.BlockSpec((2, rows // steps, width), lambda i, pick: (0, i, 0))] * shares,
         ),
-        out_shape=[jax.ShapeDtypeStruct((2, rows, width), jnp.bfloat16)] * shares,
+        out_shape=[pltpu.HBM((2, rows, width), jnp.bfloat16)] * shares,
         compiler_params=params,
         name="cast_rows",
     )(pick, w_gate, w_up)
@@ -111,7 +111,7 @@
             + [anywhere] * len(earlier),
             out_specs=[pl.BlockSpec((tile, width), lambda i, pick: (i, 0))] * shares,
         ),
-        out_shape=[jax.ShapeDtypeStruct((features, width), jnp.bfloat16)] * shares,
+        out_shape=[pltpu.HBM((features, width), jnp.bfloat16)] * shares,
         compiler_params=params,
         name="cast_turned",
     )(pick, w_down, *earlier)
@@ -244,7 +244,7 @@
             out_specs=[half, half],
             scratch_shapes=[pltpu.VMEM((columns, width), jnp.bfloat16), pltpu.SemaphoreType.DMA((len(keys),))],
         ),
-        out_shape=[jax.ShapeDtypeStruct((size, shares // 2, count, columns), jnp.bfloat16)] * 2,
+        out_shape=[pltpu.HBM((size, shares // 2, count, columns), jnp.bfloat16)] * 2,
         compiler_params=params,
         cost_estimate=pl.CostEstimate(
             flops=2 * hidden.size * columns * size,
@@ -298,7 +298,7 @@
                 pltpu.SemaphoreType.DMA((size, n)),
             ],
         ),
-        out_shape=[jax.ShapeDtypeStruct((size, shares // 2, count, columns), jnp.bfloat16)] * 2,
+        out_shape=[pltpu.HBM((size, shares // 2, count, columns), jnp.bfloat16)] * 2,
         compiler_params=params,
         cost_estimate=pl.CostEstimate(
             flops=4 * size * shares * count * width * columns,
@@ -353,16 +353,8 @@
     clock = Clock()
     wide = functools.partial(jnp.asarray, dtype=jnp.float32)
 
-    def shift(value, step, targets=None):
-        if targets is None:
-            return lax.ppermute(value, "etp", [(i, (i + step) % m) for i in range(m)])
-        pairs = [
-            (d * m + i, d * m + (i + step) % m)
-            for d in range(n)
-            for i in range(m)
-            if (i + step) % m in targets(d)
-        ]
-        return lax.ppermute(value, ("dp", "etp"), pairs)
+    def shift(value, step):
+        return lax.ppermute(value, "etp", [(i, (i + step) % m) for i in range(m)])
 
     have, starts, needs = {}, {}, {}
     scale = token_scales(slot_token, slot_gate, block_expert, experts, count)
@@ -374,16 +366,16 @@
     plan(0, 1, ("rows", 1), ("rows piece", 1), 1)
     plan(0, 2, ("rows", top), ("rows piece", 2), top)
     plan(1, 3, ("rows", top + 1), ("rows piece", 3), top + 1)
+    plan(1, 2, ("turned", 1), ("turned piece", 1), 1)
     plan(2, 3, ("turned", top), ("turned piece", 2), top)
-    plan(3, 6, "x near", "x", 1)
     plan(3, 5, "x far", "x", top)
-    plan(3, 5, ("turned", 1), ("turned piece", 1), 1)
-    plan(4, 8, ("turned", top + 1), ("turned piece", 3), top + 1)
+    plan(3, 5, "x near", "x", 1)
+    plan(3, 5, ("turned", top + 1), ("turned piece", 3), top + 1)
     plan(5, 6, "x far near", "x far", 1)
     plan(6, 8, "u far", "u", top)
-    plan(4, 8, "u near", "u", 1)
+    plan(6, 8, "u near", "u", 1)
     plan(8, 9, "u far near", "u far", 1)
-    slots = [(0, 2), (1, 3), (2, 4), (3, 5), (4, 6), (5, 7), (7, 9), (8, 9)]
+    slots = [(0, 2), (1, 3), (2, 4), (3, 5), (4, 5), (5, 7), (5, 7), (6, 8)]
     moves = 0
     for kind in ("rows", "turned"):
         held = [0, 1, top, top + 1]
@@ -418,7 +410,11 @@
     for at in range(3, 7 if halves else last + 1):
         tick(at)
 
-    blocks = [have["rows", key] for key in range(n)]
+    def hold(values, *wait):
+        (first,) = clock.tick(values[:1], wait)
+        return [first, *values[1:]]
+
+    blocks = hold([have["rows", key] for key in range(n)])
     info = jnp.stack([me, mine // (shares // experts)]).astype(jnp.int32)
     hidden, *factors = forward(info, count, [have[k] for k in ("x", "x near", "x far", "x far near")], blocks)
 
@@ -428,94 +424,77 @@
     def add(keep, near):
         return (wide(keep[:, 1]) + wide(near[:, 1])).astype(jnp.bfloat16), wide(keep[:, 0]) + wide(near[:, 0])
 
-    def choose(target, keys, values):
-        if keys is None:
-            return lax.dynamic_index_in_dim(jnp.stack(list(values)), target, 0, False)
-        return jnp.where(target == chip ^ (keys[0] // 2), values[0], values[1])
-
     order = [m // 2] + [step for step in range(1, m) if step != m // 2] + [0]
 
-    def outward(total, keys):
-        own = choose(z, keys, total)
-        if keys is not None:
-            there = (z == chip ^ (keys[0] // 2)) | (z == chip ^ (keys[1] // 2))
-            own = jnp.where(there, own, 0.0)
-        total = [part.astype(jnp.bfloat16) for part in total]
-        return own, [choose(lax.rem(z + step, m), keys, total) for step in order[:-1]]
-
-    def pass_on(values, keys):
-        targets = None if keys is None else lambda d: [(d ^ key) // 2 for key in keys]
-        return [shift(value, step, targets) for value, step in zip(values, order)]
-
-    gained, u_names = [], ("u", "u near", "u far", "u far near")
-    downs = lambda: [have["turned", key] for key in range(n)]
     if halves:
         bit = gather_bits[0]
+        first, second = [0, top], [bit, bit ^ top]
         tick(7, [hidden])
-        keep_a, send_a = run([0, 1, top, top + 1], jnp.stack([chip, chip ^ (top // 2)]), hidden)
-        tick(8, [send_a])
-        (send_a,) = clock.tick([send_a])
-        near = swap(send_a, 1, n)
-        keep_b, send_b = run([bit, bit + 1], (chip ^ (bit // 2)).reshape(1), hidden)
-        (send_b,) = clock.tick([send_b], [near, have["turned", top ^ bit]])
-        other, own_a = add(keep_a, near)
-        near = swap(send_b, 1, n)
-        (other,) = clock.tick([other], [near])
+        keep_a, send_a = run([0, 1, top, top + 1], jnp.stack([chip ^ (key // 2) for key in first]), hidden)
+        (send_a,) = clock.tick([send_a], [have["u far"], have["turned", top + 1 + bit]])
+        near_a = swap(send_a, 1, n)
+        tick(8)
+        tick(9)
+        keys = [bit, bit + 1, bit + top, bit + top + 1]
+        have["turned", bit] = hold([have["turned", bit]], near_a)[0]
+        keep, send = run(keys, jnp.stack([chip ^ (key // 2) for key in second]), hidden)
+        (send,) = clock.tick([send])
+        near = swap(send, 1, n)
+        other, own_a = add(keep_a, near_a)
+        (other,) = clock.tick([other])
         far_a = swap(other, top, n)
-        other, own_b = add(keep_b, near)
-        (other,) = clock.tick([other], [have["turned", top ^ bit ^ 1]])
-        far_b = swap(other, top, n)
-        clock.tick([], [far_a, far_b])
-        own, values = outward([own_a[0] + wide(far_a[1]), own_a[1] + wide(far_a[0])], (0, top))
-        values = clock.tick(values)
-        gained.append(own)
-        early = pass_on(values, (0, top))
-        gained += [wide(value) for value in early]
-        tick(9)
-        (hidden,) = clock.tick([hidden])
-        ids, keys = (chip ^ ((bit ^ top) // 2)).reshape(1), [bit + top, bit + top + 1]
     else:
-        ids, keys, early = jnp.arange(m, dtype=jnp.int32), list(range(n)), []
-    keep, send = run(keys, ids, hidden)
-    u_parts = [have[name] for name in u_names]
-    send, u_parts[0] = clock.tick([send, u_parts[0]])
-    near = swap(send, 1, n)
-    d_pre, d_up = grow(info, count, u_parts, downs(), factors)
-    (d_pre,) = clock.tick([d_pre], [near])
+        keep, send = run(list(range(n)), jnp.arange(m, dtype=jnp.int32), hidden)
+        near = swap(send, 1, n)
+    clock.tick([], [near])
     other, own = add(keep, near)
     (other,) = clock.tick([other])
     got = swap(other, top, n)
+    u_parts = hold([have[name] for name in ("u", "u near", "u far", "u far near")])
+    d_pre, d_up = grow(info, count, u_parts, [have["turned", key] for key in range(n)], factors)
     steps = jnp.array([order[: m // 2], order[m // 2 :]], jnp.int32)
+    blocks = hold(blocks, d_pre)
     keep_0, send_0 = back(here, lax.rem(z + steps[0], m), m, d_pre, d_up, blocks)
-    send_0, d_pre = clock.tick([send_0, d_pre], early)
+    (send_0,) = clock.tick([send_0], [far_a, got] if halves else [got])
     near_0 = swap(send_0, 1, n)
-    keep_1, send_1 = back(here, lax.rem(z + steps[1], m), m, d_pre, d_up, blocks)
-    (send_1,) = clock.tick([send_1], [near_0, got])
-    near_1 = swap(send_1, 1, n)
+    if halves:
+        sums = [own_a[0] + wide(far_a[1]), own_a[1] + wide(far_a[0]), own[0] + wide(got[1]), own[1] + wide(got[0])]
+        where = [chip ^ (key // 2) for key in first + second]
+    else:
+        sums = list(own + wide(got))
+        where = list(range(m))
+
+    def chunk_of(target, values):
+        chosen = values[-1]
+        for value, place in zip(values[:-1], where):
+            chosen = jnp.where(target == place, value, chosen)
+        return chosen
+
+    combined = chunk_of(z, sums)
+    low_sums = [value.astype(jnp.bfloat16) for value in sums]
+    values = clock.tick([chunk_of(lax.rem(z + step, m), low_sums) for step in order[:-1]])
+    late = [shift(value, step) for value, step in zip(values, order)]
+    clock.tick([], [near_0])
     other, own_0 = add(keep_0, near_0)
     (other,) = clock.tick([other])
     got_0 = swap(other, top, n)
-    if halves:
-        total = [own_b[0] + wide(got[0]), own[0] + wide(far_b[0])]
-        keys = (bit, bit ^ top)
-    else:
-        total, keys = own + wide(got), None
-    own, values = outward(total, keys)
-    values = clock.tick(values, [near_1])
-    gained.append(own)
-    gained += [wide(value) for value in pass_on(values, keys)]
+    blocks = hold(blocks)
+    keep_1, send_1 = back(here, lax.rem(z + steps[1], m), m, d_pre, d_up, blocks)
+    (send_1,) = clock.tick([send_1], [got_0, *late[1:]])
+    near_1 = swap(send_1, 1, n)
+    clock.tick([], [near_1])
     other, own_1 = add(keep_1, near_1)
     (other,) = clock.tick([other])
     got_1 = swap(other, top, n)
-    clock.tick([], [got_0])
+    for value in late:
+        combined = combined + wide(value)
     owns, gots = [own_0, own_1], [got_0, got_1]
-    combined = sum(gained)
     grad = 0.0
     for i, step in enumerate(order):
         half, at = divmod(i, m // 2)
         value = owns[half][at] + wide(gots[half][at])
         if step:
-            (value,) = clock.tick([value.astype(jnp.bfloat16)])
+            (value,) = clock.tick([value.astype(jnp.bfloat16)], late[:1] if i == 0 else [])
             value = wide(shift(value, step))
         grad = grad + value
     return combined.astype(jnp.bfloat16), grad.astype(jnp.bfloat16)

time: 378 us -> 320 us (0.85)
  starting transfers between devices: 67.9 us -> 27.5 us
  waiting for transfers between devices: 165 us -> 154 us
    ppermute x30 -> x28, waiting for transfers between devices: 154 us -> 117 us  [swap(): return lax.ppermute(value, 'dp', [(i, i ^ mask) for i in range(size)])]
    ppermute x3 -> x6, waiting for transfers between devices: 4.31 us -> 36.4 us  [shift(): return lax.ppermute(value, 'etp', [(i, (i + step) % m) for i in range(m)])]
    ppermute x3 -> x6, starting transfers between devices: 26.8 us -> 8.51 us  [shift(): return lax.ppermute(value, 'etp', [(i, (i + step) % m) for i in range(m)])]
    ppermute x6 -> x0, starting transfers between devices: 18 us -> none  [shift(): return lax.ppermute(value, ('dp', 'etp'), pairs)]
    ppermute x6 -> x0, waiting for transfers between devices: 7.06 us -> none  [shift(): return lax.ppermute(value, ('dp', 'etp'), pairs)]
    add x2 -> x3, other arithmetic: 6.66 us -> 10.9 us  [add(): wide(keep[:, 0]) + wide(near[:, 0])]
    ppermute x30 -> x28, starting transfers between devices: 23 us -> 19 us  [swap(): return lax.ppermute(value, 'dp', [(i, i ^ mask) for i in range(size)])]
    pallas_call x3 -> x2, Pallas kernels: 12.7 us -> 11.8 us  [produce(): pl.pallas_call(functools.partial(produce_kernel, keys), grid_spec=pltpu.P...]
  transfers between devices with their start and end apart: 39 -> 34, of which waited for: 15 -> 18; matrix products, arithmetic and copies ran while one was open for 6% -> 8% of each run, Pallas kernels for 18% -> 19%
where the time goes in v3:
time: 320 us; the launch traced here: 319 us
  waiting for transfers between devices  154 us (48%)
  Pallas kernels  72.3 us (23%)
  local copies, waits for them, and re-layouts  37 us (12%)
  starting transfers between devices  27.5 us (9%)
  other arithmetic  26.8 us (8%)
    ppermute x28, waiting for transfers between devices, swap(): return lax.ppermute(value, 'dp', [(i, i ^ mask) for i in range(size)])  117 us
    unnamed x116, local copies, waits for them, and re-layouts  37 us
    ppermute x6, waiting for transfers between devices, shift(): return lax.ppermute(value, 'etp', [(i, (i + step) % m) for i in range(m)])  36.4 us
    pallas_call x2, Pallas kernels, on_tokens(): pl.pallas_call(functools.partial(kernel, n), grid_spec=pltpu.PrefetchScal...  30.6 us
    pallas_call x2, Pallas kernels, back(): pl.pallas_call(functools.partial(back_kernel, n), grid_spec=pltpu.Prefetc...  20.9 us
    ppermute x28, starting transfers between devices, swap(): return lax.ppermute(value, 'dp', [(i, i ^ mask) for i in range(size)])  19 us
    pallas_call x2, Pallas kernels, produce(): pl.pallas_call(functools.partial(produce_kernel, keys), grid_spec=pltpu.P...  11.8 us
    add x3, other arithmetic, add(): wide(keep[:, 0]) + wide(near[:, 0])  10.9 us
  transfers between devices with their start and end apart: 34, of which 18 were waited for; matrix products, arithmetic and copies ran while one was open for 8% of the time, Pallas kernels for 19%

profile of v3, /device:TPU:11, one launch (start us, length us, event | category | flops | bytes accessed | tf_op | source)
XLA Modules:
  0.0 318.8 jit_solution(5165456139171126747)
XLA Ops:
  0.8 2.3 copy-done.2
  3.1 5.8 %cast_rows.1 = (bf16[2,384,768]{2,1,0:T(8,128)(2,1)}, bf16[2,384,768]{2,1,0:T(8,128)(2,1)}, bf16[2,384,768]{2,1,0:T(8,128)(2,1)}, bf16[2,384,768]{2,1,0:T(8,128)(2,1)}) custom-call(s32[4]{0:T(128)S(1)} %pad_add_fusion.2.pick_ref, f32[2,384,1536]{2,1,0:T(8,128)S(1)} %copy-done.2, f32[2,384,1536]{2,1,0:T(8,128)} %up_ref.1), custom_call_target="tpu_custom_call" | custom-call | tf_op jit(solution)/shard_map/cast_rows/pallas_call | solution.py:77
  9.5 1.2 collective-permute-start.1
  11.0 2.3 copy-done.3
  14.0 3.0 cast_turned.1
  19.5 1.2 collective-permute-start.6
  23.0 14.4 %collective-permute-done.1.refs_2_ = bf16[2,384,768]{2,1,0:T(8,128)(2,1)} collective-permute-done((bf16[2,384,768]{2,1,0:T(8,128)(2,1)}, bf16[2,384,768]{2,1,0:T(8,128)(2,1)}, u32[]{:S(2)}, u32[]{:S(2)}) %collective-permute-start.1) | collective-permute-done | bytes 1179680 | tf_op jit(solution)/shard_map/ppermute | solution.py:55
  42.9 20.7 %collective-permute-done.4.refs_3_ = bf16[2,384,768]{2,1,0:T(8,128)(2,1)} collective-permute-done((bf16[2,384,768]{2,1,0:T(8,128)(2,1)}, bf16[2,384,768]{2,1,0:T(8,128)(2,1)}, u32[]{:S(2)}, u32[]{:S(2)}) %collective-permute-start.4) | collective-permute-done | bytes 1179680 | tf_op jit(solution)/shard_map/ppermute | solution.py:55
  63.6 11.7 %collective-permute-done.5.refs_4_.refs_3_ = bf16[384,768]{1,0:T(8,128)(2,1)S(1)} collective-permute-done((bf16[384,768]{1,0:T(8,128)(2,1)}, bf16[384,768]{1,0:T(8,128)(2,1)S(1)}, u32[]{:S(2)}, u32[]{:S(2)}) %collective-permute-start.5) | collective-permute-done | bytes 589856 | tf_op jit(solution)/shard_map/ppermute | solution.py:55
  76.1 1.2 collective-permute-start.9
  79.0 9.8 %collective-permute-done.8.refs_2_.refs_10_.refs_6_ = bf16[2,384,768]{2,1,0:T(8,128)(2,1)} collective-permute-done((bf16[2,384,768]{2,1,0:T(8,128)(2,1)}, bf16[2,384,768]{2,1,0:T(8,128)(2,1)}, u32[]{:S(2)}, u32[]{:S(2)}) %collective-permute-start.8) | collective-permute-done | bytes 1179680 | tf_op jit(solution)/shard_map/ppermute | solution.py:55
  89.1 38.3 %collective-permute-done.10.refs_5_.refs_2_ = bf16[384,768]{1,0:T(8,128)(2,1)S(1)} collective-permute-done((bf16[384,768]{1,0:T(8,128)(2,1)}, bf16[384,768]{1,0:T(8,128)(2,1)S(1)}, u32[]{:S(2)}, u32[]{:S(2)}) %collective-permute-start.10) | collective-permute-done | bytes 589856 | tf_op jit(solution)/shard_map/ppermute | solution.py:55
  130.8 1.9 collective-permute-done.13.refs_3_
  136.7 1.3 copy-done.15
  138.0 18.1 %forward.1 = (bf16[4,256,768]{2,1,0:T(8,128)(2,1)}, bf16[4,256,768]{2,1,0:T(8,128)(2,1)}, bf16[4,256,768]{2,1,0:T(8,128)(2,1)}) custom-call(s32[2]{0:T(128)S(1)} %pad_add_fusion.1.info_ref.me_ref, bf16[272,3072]{1,0:T(8,128)(2,1)} %get-tuple-element.101.refs_0_, bf16[272,3072]{1,0:T(8,128)(2,1)} %copy-done.55, bf16[272,3072]{1,0:T(8,128)(2,1)} %get-tuple-element.109.refs_2_, ...), custom_call_target="tpu_custom_call" | custom-call | flops 9663676416 | bytes 15728640 | tf_op jit(solution)/shard_map/forward/pallas_call | solution.py:186
  156.2 1.4 copy-done.37
  157.6 5.4 %produce.2 = (bf16[2,2,256,768]{3,2,1,0:T(8,128)(2,1)}, bf16[2,2,256,768]{3,2,1,0:T(8,128)(2,1)}) custom-call(s32[1]{0:T(128)} %bitcast.me_ref, s32[2]{0:T(128)S(1)} %pad_add_fusion.3.ids_ref, bf16[4,256,768]{2,1,0:T(8,128)(2,1)S(1)} %copy-done.37, bf16[384,768]{1,0:T(8,128)(2,1)S(1)} %copy-done.32, bf16[384,768]{1,0:T(8,128)(2,1)S(1)} %copy-done.30, ...), custom_call_target="tpu_custom_call" | custom-call | flops 2415919104 | bytes 4718592 | tf_op jit(solution)/shard_map/produce/pallas_call | solution.py:238
  164.1 5.5 %collective-permute-done.17.refs_3_.refs_11_ = bf16[384,768]{1,0:T(8,128)(2,1)} collective-permute-done((bf16[384,768]{1,0:T(8,128)(2,1)}, bf16[384,768]{1,0:T(8,128)(2,1)}, u32[]{:S(2)}, u32[]{:S(2)}) %collective-permute-start.17) | collective-permute-done | bytes 589856 | tf_op jit(solution)/shard_map/ppermute | solution.py:55
  171.5 3.2 %collective-permute-done.19.refs_1_.refs_3_ = bf16[256,3072]{1,0:T(8,128)(2,1)} collective-permute-done((bf16[256,3072]{1,0:T(8,128)(2,1)}, bf16[256,3072]{1,0:T(8,128)(2,1)}, u32[]{:S(2)}, u32[]{:S(2)}) %collective-permute-start.19) | collective-permute-done | bytes 1572896 | tf_op jit(solution)/shard_map/ppermute | solution.py:55
  174.7 2.2 collective-permute-done.20.refs_2_
  178.0 1.4 copy-done.38
  179.4 6.4 %produce.3 = (bf16[2,2,256,768]{3,2,1,0:T(8,128)(2,1)}, bf16[2,2,256,768]{3,2,1,0:T(8,128)(2,1)}) custom-call(s32[1]{0:T(128)} %bitcast.me_ref, s32[2]{0:T(128)S(1)} %pad_add_fusion.ids_ref, bf16[4,256,768]{2,1,0:T(8,128)(2,1)S(1)} %copy-done.38, bf16[384,768]{1,0:T(8,128)(2,1)S(1)} %copy-done.19, bf16[384,768]{1,0:T(8,128)(2,1)S(1)} %copy-done.22, ...), custom_call_target="tpu_custom_call" | custom-call | flops 2415919104 | bytes 4718592 | tf_op jit(solution)/shard_map/produce/pallas_call | solution.py:238
  186.5 3.6 %convert_add_fusion.2 = (f32[2,1,256,768]{3,2,1,0:T(8,128)}, bf16[2,256,768]{2,1,0:T(8,128)(2,1)}) fusion(bf16[2,2,256,768]{3,2,1,0:T(8,128)(2,1)} %collective-permute-done.20.refs_2_, bf16[2,2,256,768]{3,2,1,0:T(8,128)(2,1)} %get-tuple-element.130), kind=kLoop, calls=%fused_computation.4 | loop fusion | flops 2752512 | bytes 5505024 | tf_op jit(solution)/shard_map/add | solution.py:425
  191.0 3.6 %convert_add_fusion.3 = (f32[2,1,256,768]{3,2,1,0:T(8,128)}, bf16[2,256,768]{2,1,0:T(8,128)(2,1)}) fusion(bf16[2,2,256,768]{3,2,1,0:T(8,128)(2,1)} %collective-permute-done.21.refs_1_, bf16[2,2,256,768]{3,2,1,0:T(8,128)(2,1)} %get-tuple-element.125), kind=kLoop, calls=%fused_computation.7 | loop fusion | flops 2752512 | bytes 5505024 | tf_op jit(solution)/shard_map/add | solution.py:425
  201.1 12.5 %grow.1 = (bf16[4,256,768]{2,1,0:T(8,128)(2,1)}, bf16[4,256,768]{2,1,0:T(8,128)(2,1)}) custom-call(s32[2]{0:T(128)S(1)} %pad_add_fusion.1.info_ref.me_ref, bf16[4,256,768]{2,1,0:T(8,128)(2,1)} %get-tuple-element.136.slope_ref, bf16[4,256,768]{2,1,0:T(8,128)(2,1)} %get-tuple-element.137.active_ref, bf16[256,3072]{1,0:T(8,128)(2,1)} %get-tuple-element.138.refs_0_, ...), custom_call_target="tpu_custom_call" | custom-call | flops 4831838208 | bytes 11010048 | tf_op jit(solution)/shard_map/grow/pallas_call | solution.py:186
  213.6 1.3 copy-done.16
  214.8 10.6 %back.2 = (bf16[2,2,256,768]{3,2,1,0:T(8,128)(2,1)}, bf16[2,2,256,768]{3,2,1,0:T(8,128)(2,1)}) custom-call(s32[1]{0:T(128)} %bitcast.me_ref, s32[2]{0:T(128)S(1)} %get-tuple-element.184.ids_ref, bf16[4,256,768]{2,1,0:T(8,128)(2,1)} %get-tuple-element.139.refs_2_.pre_ref, bf16[4,256,768]{2,1,0:T(8,128)(2,1)} %get-tuple-element.141.up_ref, ...), custom_call_target="tpu_custom_call" | custom-call | flops 4831838208 | bytes 7864320 | tf_op jit(solution)/shard_map/back/pallas_call | solution.py:289
  227.3 3.4 %select_bitcast_fusion = (bf16[256,768]{1,0:T(8,128)(2,1)}, bf16[1,256,768]{2,1,0:T(8,128)(2,1)S(1)}, bf16[1,256,768]{2,1,0:T(8,128)(2,1)S(1)}, bf16[1,256,768]{2,1,0:T(8,128)(2,1)S(1)}, bf16[1,256,768]{2,1,0:T(8,128)(2,1)S(1)}) fusion(pred[]{:T(512)S(6)} %eq.80, pred[]{:T(512)S(6)} %eq.81, pred[]{:T(512)S(6)} %eq.82, ...), kind=kLoop, calls=%fused_computation.47 | loop fusion | flops 2949120 | bytes 6684675 | tf_op jit(solution)/shard_map/jit(_where)/select_n | solution.py:470
  231.7 1.3 collective-permute-start.25
  233.1 3.6 %convert_add_fusion.1 = (f32[2,1,256,768]{3,2,1,0:T(8,128)}, bf16[2,256,768]{2,1,0:T(8,128)(2,1)}) fusion(bf16[2,2,256,768]{3,2,1,0:T(8,128)(2,1)} %collective-permute-done.27.refs_1_, bf16[2,2,256,768]{3,2,1,0:T(8,128)(2,1)} %get-tuple-element.150), kind=kLoop, calls=%fused_computation.1 | loop fusion | flops 2752512 | bytes 5505024 | tf_op jit(solution)/shard_map/add | solution.py:425
  237.7 1.3 copy-done.17
  239.0 10.3 %back.3 = (bf16[2,2,256,768]{3,2,1,0:T(8,128)(2,1)}, bf16[2,2,256,768]{3,2,1,0:T(8,128)(2,1)}) custom-call(s32[1]{0:T(128)} %bitcast.me_ref, s32[2]{0:T(128)S(1)} %get-tuple-element.183.ids_ref, bf16[4,256,768]{2,1,0:T(8,128)(2,1)} %get-tuple-element.139.refs_2_.pre_ref, bf16[4,256,768]{2,1,0:T(8,128)(2,1)} %get-tuple-element.141.up_ref, ...), custom_call_target="tpu_custom_call" | custom-call | flops 4831838208 | bytes 7864320 | tf_op jit(solution)/shard_map/back/pallas_call | solution.py:289
  249.3 3.0 collective-permute-done.26.refs_4_
  252.3 3.2 %collective-permute-done.28.refs_2_ = bf16[2,256,768]{2,1,0:T(8,128)(2,1)S(1)} collective-permute-done((bf16[2,256,768]{2,1,0:T(8,128)(2,1)}, bf16[2,256,768]{2,1,0:T(8,128)(2,1)S(1)}, u32[]{:S(2)}, u32[]{:S(2)}) %collective-permute-start.28) | collective-permute-done | bytes 786464 | tf_op jit(solution)/shard_map/ppermute | solution.py:55
  256.4 1.4 collective-permute-start.29
  257.8 2.3 collective-permute-start.24
  260.2 2.3 fusion.27
  262.4 1.2 copy-done.45
  263.6 1.4 copy-done.44
  265.0 2.6 fusion.3
  268.6 8.8 %collective-permute-done.24.refs_2_ = bf16[256,768]{1,0:T(8,128)(2,1)} collective-permute-done((bf16[256,768]{1,0:T(8,128)(2,1)S(1)}, bf16[256,768]{1,0:T(8,128)(2,1)}, u32[]{:S(2)}, u32[]{:S(2)}) %collective-permute-start.24) | collective-permute-done | bytes 393248 | tf_op jit(solution)/shard_map/ppermute | solution.py:357
  278.3 3.3 %collective-permute-start.30 = (bf16[256,768]{1,0:T(8,128)(2,1)S(1)}, bf16[256,768]{1,0:T(8,128)(2,1)}, u32[]{:S(2)}, u32[]{:S(2)}) collective-permute-start(bf16[256,768]{1,0:T(8,128)(2,1)S(1)} %copy-done.49), channel_id=1, source_target_pairs={{0,2},{1,3},{2,0},{3,1},{4,6},{5,7},{6,4},{7,5},{8,10},{9,11},{10,... | collective-permute-start | bytes 1179656 | tf_op jit(solution)/shard_map/ppermute | solution.py:357
  281.6 4.2 %collective-permute-done.32 = bf16[2,256,768]{2,1,0:T(8,128)(2,1)S(1)} collective-permute-done((bf16[2,256,768]{2,1,0:T(8,128)(2,1)}, bf16[2,256,768]{2,1,0:T(8,128)(2,1)S(1)}, u32[]{:S(2)}, u32[]{:S(2)}) %collective-permute-start.32) | collective-permute-done | bytes 786464 | tf_op jit(solution)/shard_map/ppermute | solution.py:55
  286.9 1.3 collective-permute-start.33
  288.8 3.1 fusion.20
  291.9 19.1 %collective-permute-done.30 = bf16[256,768]{1,0:T(8,128)(2,1)} collective-permute-done((bf16[256,768]{1,0:T(8,128)(2,1)S(1)}, bf16[256,768]{1,0:T(8,128)(2,1)}, u32[]{:S(2)}, u32[]{:S(2)}) %collective-permute-start.30) | collective-permute-done | bytes 393248 | tf_op jit(solution)/shard_map/ppermute | solution.py:357
  311.0 5.6 %collective-permute-done.33 = bf16[256,768]{1,0:T(8,128)(2,1)} collective-permute-done((bf16[256,768]{1,0:T(8,128)(2,1)}, bf16[256,768]{1,0:T(8,128)(2,1)}, u32[]{:S(2)}, u32[]{:S(2)}) %collective-permute-start.33) | collective-permute-done | bytes 393248 | tf_op jit(solution)/shard_map/ppermute | solution.py:357
  316.5 2.2 fusion.7
  (195 shorter events, 42.4 us)
Async XLA Ops:
  0.6 18.1 %copy-start = (s32[4]{0:T(128)S(1)}, s32[4]{0:T(128)}, u32[]{:S(2)}) copy-start(s32[4]{0:T(128)} %param.16) | copy-start | bytes 52
  0.8 2.3 copy-start.2
  8.9 8.2 %collective-permute-start = (bf16[2,384,768]{2,1,0:T(8,128)(2,1)}, bf16[2,384,768]{2,1,0:T(8,128)(2,1)S(1)}, u32[]{:S(2)}, u32[]{:S(2)}) collective-permute-start(bf16[2,384,768]{2,1,0:T(8,128)(2,1)} %get-tuple-element.90), channel_id=1, source_target_pairs={{0,4},{4,0},{8,12},{12,8},{16,20},{20,16},{24,28},{28,24},{1,5},{5... | collective-permute-start | bytes 3538952 | tf_op jit(solution)/shard_map/ppermute | solution.py:55
  9.5 27.8 %collective-permute-start.1 = (bf16[2,384,768]{2,1,0:T(8,128)(2,1)}, bf16[2,384,768]{2,1,0:T(8,128)(2,1)}, u32[]{:S(2)}, u32[]{:S(2)}) collective-permute-start(bf16[2,384,768]{2,1,0:T(8,128)(2,1)} %get-tuple-element.93), channel_id=1, source_target_pairs={{0,16},{4,20},{8,24},{12,28},{16,0},{20,4},{24,8},{28,12},{1,17},{... | collective-permute-start | bytes 3538952 | tf_op jit(solution)/shard_map/ppermute | solution.py:55
  10.8 27.5 %collective-permute-start.3 = (bf16[2,384,768]{2,1,0:T(8,128)(2,1)}, bf16[2,384,768]{2,1,0:T(8,128)(2,1)S(1)}, u32[]{:S(2)}, u32[]{:S(2)}) collective-permute-start(bf16[2,384,768]{2,1,0:T(8,128)(2,1)} %get-tuple-element.95.refs_1_), channel_id=1, source_target_pairs={{0,8},{4,12},{8,0},{12,4},{16,24},{20,28},{24,16},{28,20},{1,9},{5... | collective-permute-start | bytes 3538952 | tf_op jit(solution)/shard_map/ppermute | solution.py:55
  18.1 2.6 copy-start.57
  18.1 2.9 copy-start.5
  18.1 20.2 %collective-permute-start.2 = (bf16[384,768]{1,0:T(8,128)(2,1)}, bf16[384,768]{1,0:T(8,128)(2,1)S(1)}, u32[]{:S(2)}, u32[]{:S(2)}) collective-permute-start(bf16[384,768]{1,0:T(8,128)(2,1)} %get-tuple-element.94), channel_id=1, source_target_pairs={{0,4},{4,0},{8,12},{12,8},{16,20},{20,16},{24,28},{28,24},{1,5},{5... | collective-permute-start | bytes 1769480 | tf_op jit(solution)/shard_map/ppermute | solution.py:55
  18.8 44.8 %collective-permute-start.4 = (bf16[2,384,768]{2,1,0:T(8,128)(2,1)}, bf16[2,384,768]{2,1,0:T(8,128)(2,1)}, u32[]{:S(2)}, u32[]{:S(2)}) collective-permute-start(bf16[2,384,768]{2,1,0:T(8,128)(2,1)} %get-tuple-element.98), channel_id=1, source_target_pairs={{0,20},{4,16},{8,28},{12,24},{16,4},{20,0},{24,12},{28,8},{1,21},{... | collective-permute-start | bytes 3538952 | tf_op jit(solution)/shard_map/ppermute | solution.py:55
  19.5 44.1 %collective-permute-start.6 = (bf16[2,384,768]{2,1,0:T(8,128)(2,1)}, bf16[2,384,768]{2,1,0:T(8,128)(2,1)}, u32[]{:S(2)}, u32[]{:S(2)}) collective-permute-start(bf16[2,384,768]{2,1,0:T(8,128)(2,1)} %get-tuple-element.100.refs_5_.refs_1_), channel_id=1, source_target_pairs={{0,8},{4,12},{8,0},{12,4},{16,24},{20,28},{24,16},{28,20},{1,9},{5... | collective-permute-start | bytes 3538952 | tf_op jit(solution)/shard_map/ppermute | solution.py:55
  39.5 35.8 %collective-permute-start.5 = (bf16[384,768]{1,0:T(8,128)(2,1)}, bf16[384,768]{1,0:T(8,128)(2,1)S(1)}, u32[]{:S(2)}, u32[]{:S(2)}) collective-permute-start(bf16[384,768]{1,0:T(8,128)(2,1)} %get-tuple-element.99), channel_id=1, source_target_pairs={{0,16},{4,20},{8,24},{12,28},{16,0},{20,4},{24,8},{28,12},{1,17},{... | collective-permute-start | bytes 1769480 | tf_op jit(solution)/shard_map/ppermute | solution.py:55
  39.8 49.0 %collective-permute-start.8 = (bf16[2,384,768]{2,1,0:T(8,128)(2,1)}, bf16[2,384,768]{2,1,0:T(8,128)(2,1)}, u32[]{:S(2)}, u32[]{:S(2)}) collective-permute-start(bf16[2,384,768]{2,1,0:T(8,128)(2,1)} %get-tuple-element.104.refs_8_.refs_4_), channel_id=1, source_target_pairs={{0,8},{4,12},{8,0},{12,4},{16,24},{20,28},{24,16},{28,20},{1,9},{5... | collective-permute-start | bytes 3538952 | tf_op jit(solution)/shard_map/ppermute | solution.py:55
  76.1 51.3 %collective-permute-start.9 = (bf16[272,3072]{1,0:T(8,128)(2,1)}, bf16[272,3072]{1,0:T(8,128)(2,1)}, u32[]{:S(2)}, u32[]{:S(2)}) collective-permute-start(bf16[272,3072]{1,0:T(8,128)(2,1)} %get-tuple-element.101.refs_0_), channel_id=1, source_target_pairs={{0,16},{4,20},{8,24},{12,28},{16,0},{20,4},{24,8},{28,12},{1,17},{... | collective-permute-start | bytes 5013512 | tf_op jit(solution)/shard_map/ppermute | solution.py:55
  77.4 50.1 %collective-permute-start.7 = (bf16[272,3072]{1,0:T(8,128)(2,1)}, bf16[272,3072]{1,0:T(8,128)(2,1)S(1)}, u32[]{:S(2)}, u32[]{:S(2)}) collective-permute-start(bf16[272,3072]{1,0:T(8,128)(2,1)} %get-tuple-element.101.refs_0_), channel_id=1, source_target_pairs={{0,4},{4,0},{8,12},{12,8},{16,20},{20,16},{24,28},{28,24},{1,5},{5... | collective-permute-start | bytes 5013512 | tf_op jit(solution)/shard_map/ppermute | solution.py:55
  78.4 49.1 %collective-permute-start.11 = (bf16[2,384,768]{2,1,0:T(8,128)(2,1)}, bf16[2,384,768]{2,1,0:T(8,128)(2,1)}, u32[]{:S(2)}, u32[]{:S(2)}) collective-permute-start(bf16[2,384,768]{2,1,0:T(8,128)(2,1)} %get-tuple-element.107.refs_9_.refs_5_), channel_id=1, source_target_pairs={{0,8},{4,12},{8,0},{12,4},{16,24},{20,28},{24,16},{28,20},{1,9},{5... | collective-permute-start | bytes 3538952 | tf_op jit(solution)/shard_map/ppermute | solution.py:55
  78.6 48.8 %collective-permute-start.10 = (bf16[384,768]{1,0:T(8,128)(2,1)}, bf16[384,768]{1,0:T(8,128)(2,1)S(1)}, u32[]{:S(2)}, u32[]{:S(2)}) collective-permute-start(bf16[384,768]{1,0:T(8,128)(2,1)} %get-tuple-element.106), channel_id=1, source_target_pairs={{0,20},{4,16},{8,28},{12,24},{16,4},{20,0},{24,12},{28,8},{1,21},{... | collective-permute-start | bytes 1769480 | tf_op jit(solution)/shard_map/ppermute | solution.py:55
  88.9 38.6 %collective-permute-start.12 = (bf16[384,768]{1,0:T(8,128)(2,1)}, bf16[384,768]{1,0:T(8,128)(2,1)S(1)}, u32[]{:S(2)}, u32[]{:S(2)}) collective-permute-start(bf16[384,768]{1,0:T(8,128)(2,1)} %get-tuple-element.108.refs_0_.refs_4_), channel_id=1, source_target_pairs={{0,8},{4,12},{8,0},{12,4},{16,24},{20,28},{24,16},{28,20},{1,9},{5... | collective-permute-start | bytes 1769480 | tf_op jit(solution)/shard_map/ppermute | solution.py:55
  129.0 3.8 %collective-permute-start.13 = (bf16[272,3072]{1,0:T(8,128)(2,1)}, bf16[272,3072]{1,0:T(8,128)(2,1)S(1)}, u32[]{:S(2)}, u32[]{:S(2)}) collective-permute-start(bf16[272,3072]{1,0:T(8,128)(2,1)} %get-tuple-element.109.refs_2_), channel_id=1, source_target_pairs={{0,4},{4,0},{8,12},{12,8},{16,20},{20,16},{24,28},{28,24},{1,5},{5... | collective-permute-start | bytes 5013512 | tf_op jit(solution)/shard_map/ppermute | solution.py:55
  129.4 33.7 %collective-permute-start.14 = (bf16[384,768]{1,0:T(8,128)(2,1)}, bf16[384,768]{1,0:T(8,128)(2,1)S(1)}, u32[]{:S(2)}, u32[]{:S(2)}) collective-permute-start(bf16[384,768]{1,0:T(8,128)(2,1)} %get-tuple-element.115.refs_1_.refs_5_), channel_id=1, source_target_pairs={{0,8},{4,12},{8,0},{12,4},{16,24},{20,28},{24,16},{28,20},{1,9},{5... | collective-permute-start | bytes 1769480 | tf_op jit(solution)/shard_map/ppermute | solution.py:55
  129.6 33.4 %collective-permute-start.15 = (bf16[384,768]{1,0:T(8,128)(2,1)}, bf16[384,768]{1,0:T(8,128)(2,1)S(1)}, u32[]{:S(2)}, u32[]{:S(2)}) collective-permute-start(bf16[384,768]{1,0:T(8,128)(2,1)} %get-tuple-element.116.refs_2_.refs_8_), channel_id=1, source_target_pairs={{0,8},{4,12},{8,0},{12,4},{16,24},{20,28},{24,16},{28,20},{1,9},{5... | collective-permute-start | bytes 1769480 | tf_op jit(solution)/shard_map/ppermute | solution.py:55
  134.0 36.2 %collective-permute-start.18 = (bf16[256,3072]{1,0:T(8,128)(2,1)}, bf16[256,3072]{1,0:T(8,128)(2,1)}, u32[]{:S(2)}, u32[]{:S(2)}) collective-permute-start(bf16[256,3072]{1,0:T(8,128)(2,1)} %get-tuple-element.119.refs_1_), channel_id=1, source_target_pairs={{0,4},{4,0},{8,12},{12,8},{16,20},{20,16},{24,28},{28,24},{1,5},{5... | collective-permute-start | bytes 4718600 | tf_op jit(solution)/shard_map/ppermute | solution.py:55
  134.2 36.0 %collective-permute-start.16 = (bf16[256,3072]{1,0:T(8,128)(2,1)}, bf16[256,3072]{1,0:T(8,128)(2,1)}, u32[]{:S(2)}, u32[]{:S(2)}) collective-permute-start(bf16[256,3072]{1,0:T(8,128)(2,1)} %get-tuple-element.119.refs_1_), channel_id=1, source_target_pairs={{0,16},{4,20},{8,24},{12,28},{16,0},{20,4},{24,8},{28,12},{1,17},{... | collective-permute-start | bytes 4718600 | tf_op jit(solution)/shard_map/ppermute | solution.py:55
  135.1 34.5 %collective-permute-start.17 = (bf16[384,768]{1,0:T(8,128)(2,1)}, bf16[384,768]{1,0:T(8,128)(2,1)}, u32[]{:S(2)}, u32[]{:S(2)}) collective-permute-start(bf16[384,768]{1,0:T(8,128)(2,1)} %get-tuple-element.117.refs_3_.refs_9_), channel_id=1, source_target_pairs={{0,8},{4,12},{8,0},{12,4},{16,24},{20,28},{24,16},{28,20},{1,9},{5... | collective-permute-start | bytes 1769480 | tf_op jit(solution)/shard_map/ppermute | solution.py:55
  138.0 18.1 %copy-start.27 = (bf16[384,768]{1,0:T(8,128)(2,1)S(1)}, bf16[384,768]{1,0:T(8,128)(2,1)}, u32[]{:S(2)}) copy-start(bf16[384,768]{1,0:T(8,128)(2,1)} %get-tuple-element.117.refs_3_.refs_9_) | copy-start | bytes 1769476
  138.0 18.2 %copy-start.30 = (bf16[384,768]{1,0:T(8,128)(2,1)S(1)}, bf16[384,768]{1,0:T(8,128)(2,1)}, u32[]{:S(2)}) copy-start(bf16[384,768]{1,0:T(8,128)(2,1)} %get-tuple-element.115.refs_1_.refs_5_) | copy-start | bytes 1769476
  138.0 18.2 %copy-start.32 = (bf16[384,768]{1,0:T(8,128)(2,1)S(1)}, bf16[384,768]{1,0:T(8,128)(2,1)}, u32[]{:S(2)}) copy-start(bf16[384,768]{1,0:T(8,128)(2,1)} %get-tuple-element.108.refs_0_.refs_4_) | copy-start | bytes 1769476
  138.0 18.2 %copy-start.35 = (bf16[384,768]{1,0:T(8,128)(2,1)S(1)}, bf16[384,768]{1,0:T(8,128)(2,1)}, u32[]{:S(2)}) copy-start(bf16[384,768]{1,0:T(8,128)(2,1)} %get-tuple-element.116.refs_2_.refs_8_) | copy-start | bytes 1769476
  170.2 4.5 %collective-permute-start.19 = (bf16[256,3072]{1,0:T(8,128)(2,1)}, bf16[256,3072]{1,0:T(8,128)(2,1)}, u32[]{:S(2)}, u32[]{:S(2)}) collective-permute-start(bf16[256,3072]{1,0:T(8,128)(2,1)} %get-tuple-element.122.refs_2_), channel_id=1, source_target_pairs={{0,4},{4,0},{8,12},{12,8},{16,20},{20,16},{24,28},{28,24},{1,5},{5... | collective-permute-start | bytes 4718600 | tf_op jit(solution)/shard_map/ppermute | solution.py:55
  171.3 5.6 %collective-permute-start.20 = (bf16[2,2,256,768]{3,2,1,0:T(8,128)(2,1)}, bf16[2,2,256,768]{3,2,1,0:T(8,128)(2,1)}, u32[]{:S(2)}, u32[]{:S(2)}) collective-permute-start(bf16[2,2,256,768]{3,2,1,0:T(8,128)(2,1)} %get-tuple-element.123), channel_id=1, source_target_pairs={{0,4},{4,0},{8,12},{12,8},{16,20},{20,16},{24,28},{28,24},{1,5},{5... | collective-permute-start | bytes 4718600 | tf_op jit(solution)/shard_map/ppermute | solution.py:55
  185.9 5.2 %collective-permute-start.21 = (bf16[2,2,256,768]{3,2,1,0:T(8,128)(2,1)}, bf16[2,2,256,768]{3,2,1,0:T(8,128)(2,1)}, u32[]{:S(2)}, u32[]{:S(2)}) collective-permute-start(bf16[2,2,256,768]{3,2,1,0:T(8,128)(2,1)} %get-tuple-element.128), channel_id=1, source_target_pairs={{0,4},{4,0},{8,12},{12,8},{16,20},{20,16},{24,28},{28,24},{1,5},{5... | collective-permute-start | bytes 4718600 | tf_op jit(solution)/shard_map/ppermute | solution.py:55
  190.1 35.3 %collective-permute-start.23 = (bf16[2,256,768]{2,1,0:T(8,128)(2,1)}, bf16[2,256,768]{2,1,0:T(8,128)(2,1)}, u32[]{:S(2)}, u32[]{:S(2)}) collective-permute-start(bf16[2,256,768]{2,1,0:T(8,128)(2,1)} %get-tuple-element.133), channel_id=1, source_target_pairs={{0,16},{4,20},{8,24},{12,28},{16,0},{20,4},{24,8},{28,12},{1,17},{... | collective-permute-start | bytes 2359304 | tf_op jit(solution)/shard_map/ppermute | solution.py:55
  194.7 31.4 %collective-permute-start.22 = (bf16[2,256,768]{2,1,0:T(8,128)(2,1)}, bf16[2,256,768]{2,1,0:T(8,128)(2,1)}, u32[]{:S(2)}, u32[]{:S(2)}) collective-permute-start(bf16[2,256,768]{2,1,0:T(8,128)(2,1)} %get-tuple-element.132), channel_id=1, source_target_pairs={{0,16},{4,20},{8,24},{12,28},{16,0},{20,4},{24,8},{28,12},{1,17},{... | collective-permute-start | bytes 2359304 | tf_op jit(solution)/shard_map/ppermute | solution.py:55
  226.1 7.1 %collective-permute-start.27 = (bf16[2,2,256,768]{3,2,1,0:T(8,128)(2,1)}, bf16[2,2,256,768]{3,2,1,0:T(8,128)(2,1)}, u32[]{:S(2)}, u32[]{:S(2)}) collective-permute-start(bf16[2,2,256,768]{3,2,1,0:T(8,128)(2,1)} %get-tuple-element.149), channel_id=1, source_target_pairs={{0,4},{4,0},{8,12},{12,8},{16,20},{20,16},{24,28},{28,24},{1,5},{5... | collective-permute-start | bytes 4718600 | tf_op jit(solution)/shard_map/ppermute | solution.py:55
  231.7 17.6 %collective-permute-start.25 = (bf16[256,768]{1,0:T(8,128)(2,1)}, bf16[256,768]{1,0:T(8,128)(2,1)S(1)}, u32[]{:S(2)}, u32[]{:S(2)}) collective-permute-start(bf16[256,768]{1,0:T(8,128)(2,1)} %get-tuple-element.146), channel_id=1, source_target_pairs={{0,1},{1,2},{2,3},{3,0},{4,5},{5,6},{6,7},{7,4},{8,9},{9,10},{10,1... | collective-permute-start | bytes 1179656 | tf_op jit(solution)/shard_map/ppermute | solution.py:357
  233.0 19.4 %collective-permute-start.26 = (bf16[256,768]{1,0:T(8,128)(2,1)}, bf16[256,768]{1,0:T(8,128)(2,1)}, u32[]{:S(2)}, u32[]{:S(2)}) collective-permute-start(bf16[256,768]{1,0:T(8,128)(2,1)} %get-tuple-element.147), channel_id=1, source_target_pairs={{0,3},{1,0},{2,1},{3,2},{4,7},{5,4},{6,5},{7,6},{8,11},{9,8},{10,9... | collective-permute-start | bytes 1179656 | tf_op jit(solution)/shard_map/ppermute | solution.py:357
  236.8 18.7 %collective-permute-start.28 = (bf16[2,256,768]{2,1,0:T(8,128)(2,1)}, bf16[2,256,768]{2,1,0:T(8,128)(2,1)S(1)}, u32[]{:S(2)}, u32[]{:S(2)}) collective-permute-start(bf16[2,256,768]{2,1,0:T(8,128)(2,1)} %get-tuple-element.155), channel_id=1, source_target_pairs={{0,16},{4,20},{8,24},{12,28},{16,0},{20,4},{24,8},{28,12},{1,17},{... | collective-permute-start | bytes 2359304 | tf_op jit(solution)/shard_map/ppermute | solution.py:55
  249.3 6.2 %copy-start.51 = (bf16[256,768]{1,0:T(8,128)(2,1)}, bf16[256,768]{1,0:T(8,128)(2,1)S(1)}, u32[]{:S(2)}) copy-start(bf16[256,768]{1,0:T(8,128)(2,1)S(1)} %collective-permute-done.25.refs_3_) | copy-start | bytes 1179652
  256.4 3.7 %copy-start.41 = (f32[2,1,256,768]{3,2,1,0:T(8,128)S(1)}, f32[2,1,256,768]{3,2,1,0:T(8,128)}, u32[]{:S(2)}) copy-start(f32[2,1,256,768]{3,2,1,0:T(8,128)} %get-tuple-element.171) | copy-start | bytes 4718596
  256.4 6.0 %collective-permute-start.29 = (bf16[2,2,256,768]{3,2,1,0:T(8,128)(2,1)}, bf16[2,2,256,768]{3,2,1,0:T(8,128)(2,1)S(1)}, u32[]{:S(2)}, u32[]{:S(2)}) collective-permute-start(bf16[2,2,256,768]{3,2,1,0:T(8,128)(2,1)} %get-tuple-element.157), channel_id=1, source_target_pairs={{0,4},{4,0},{8,12},{12,8},{16,20},{20,16},{24,28},{28,24},{1,5},{5... | collective-permute-start | bytes 4718600 | tf_op jit(solution)/shard_map/ppermute | solution.py:55
  257.8 19.5 %collective-permute-start.24 = (bf16[256,768]{1,0:T(8,128)(2,1)S(1)}, bf16[256,768]{1,0:T(8,128)(2,1)}, u32[]{:S(2)}, u32[]{:S(2)}) collective-permute-start(bf16[256,768]{1,0:T(8,128)(2,1)S(1)} %copy-done.50), channel_id=1, source_target_pairs={{0,2},{1,3},{2,0},{3,1},{4,6},{5,7},{6,4},{7,5},{8,10},{9,11},{10,... | collective-permute-start | bytes 1179656 | tf_op jit(solution)/shard_map/ppermute | solution.py:357
  267.7 18.1 %copy-start.42 = (f32[2,1,256,768]{3,2,1,0:T(8,128)}, f32[2,1,256,768]{3,2,1,0:T(8,128)S(1)}, u32[]{:S(2)}) copy-start(f32[2,1,256,768]{3,2,1,0:T(8,128)S(1)} %get-tuple-element.174) | copy-start | bytes 4718596
  267.7 18.1 %collective-permute-start.32 = (bf16[2,256,768]{2,1,0:T(8,128)(2,1)}, bf16[2,256,768]{2,1,0:T(8,128)(2,1)S(1)}, u32[]{:S(2)}, u32[]{:S(2)}) collective-permute-start(bf16[2,256,768]{2,1,0:T(8,128)(2,1)} %get-tuple-element.164), channel_id=1, source_target_pairs={{0,16},{4,20},{8,24},{12,28},{16,0},{20,4},{24,8},{28,12},{1,17},{... | collective-permute-start | bytes 2359304 | tf_op jit(solution)/shard_map/ppermute | solution.py:55
  277.3 14.6 %collective-permute-start.31 = (bf16[256,768]{1,0:T(8,128)(2,1)}, bf16[256,768]{1,0:T(8,128)(2,1)}, u32[]{:S(2)}, u32[]{:S(2)}) collective-permute-start(bf16[256,768]{1,0:T(8,128)(2,1)} %get-tuple-element.162), channel_id=1, source_target_pairs={{0,1},{1,2},{2,3},{3,0},{4,5},{5,6},{6,7},{7,4},{8,9},{9,10},{10,1... | collective-permute-start | bytes 1179656 | tf_op jit(solution)/shard_map/ppermute | solution.py:357
  278.3 32.7 %collective-permute-start.30 = (bf16[256,768]{1,0:T(8,128)(2,1)S(1)}, bf16[256,768]{1,0:T(8,128)(2,1)}, u32[]{:S(2)}, u32[]{:S(2)}) collective-permute-start(bf16[256,768]{1,0:T(8,128)(2,1)S(1)} %copy-done.49), channel_id=1, source_target_pairs={{0,2},{1,3},{2,0},{3,1},{4,6},{5,7},{6,4},{7,5},{8,10},{9,11},{10,... | collective-permute-start | bytes 1179656 | tf_op jit(solution)/shard_map/ppermute | solution.py:357
  286.9 29.6 %collective-permute-start.33 = (bf16[256,768]{1,0:T(8,128)(2,1)}, bf16[256,768]{1,0:T(8,128)(2,1)}, u32[]{:S(2)}, u32[]{:S(2)}) collective-permute-start(bf16[256,768]{1,0:T(8,128)(2,1)} %get-tuple-element.165), channel_id=1, source_target_pairs={{0,3},{1,0},{2,1},{3,2},{4,7},{5,4},{6,5},{7,6},{8,11},{9,8},{10,9... | collective-permute-start | bytes 1179656 | tf_op jit(solution)/shard_map/ppermute | solution.py:357
  288.7 27.8 %copy-start.43 = (f32[2,1,256,768]{3,2,1,0:T(8,128)S(1)}, f32[2,1,256,768]{3,2,1,0:T(8,128)}, u32[]{:S(2)}) copy-start(f32[2,1,256,768]{3,2,1,0:T(8,128)} %copy-done.42) | copy-start | bytes 4718596
  288.8 27.8 %copy-start.48 = (bf16[2,256,768]{2,1,0:T(8,128)(2,1)S(1)}, bf16[2,256,768]{2,1,0:T(8,128)(2,1)}, u32[]{:S(2)}) copy-start(bf16[2,256,768]{2,1,0:T(8,128)(2,1)} %copy-done.47) | copy-start | bytes 2359300
  288.8 30.0 %copy-start.1 = (s32[4]{0:T(128)S(1)}, s32[4]{0:T(128)}, u32[]{:S(2)}) copy-start(s32[4]{0:T(128)} %param.16) | copy-start | bytes 52
  (44 other events, 52.6 us)

commit v4 on v3

--- a/solution.py
+++ b/solution.py
@@ -40,6 +40,10 @@
             name="tick",
         )(*held, *wait)
         return out
+
+
+def far_off(values):
+    return [pltpu.with_memory_space_constraint(value, pltpu.HBM) for value in values]
 
 
 def blank(shape):
@@ -205,7 +209,7 @@
             transcendentals=0,
         ),
         name=name,
-    )(prefetch, *first, *parts, *blocks)
+    )(prefetch, *first, *far_off(parts), *far_off(blocks))
 
 
 def forward(info, count, x_parts, blocks):
@@ -252,7 +256,7 @@
             transcendentals=0,
         ),
         name="produce",
-    )(me, ids, hidden, *blocks)
+    )(me, ids, hidden, *far_off(blocks))
 
 
 def back_kernel(n, me_ref, ids_ref, pre_ref, up_ref, *refs):
@@ -306,7 +310,7 @@
             transcendentals=0,
         ),
         name="back",
-    )(me, ids, d_pre, d_up, *blocks)
+    )(me, ids, d_pre, d_up, *far_off(blocks))
 
 
 def pack_kernel(value_ref, scale_ref, tick_ref, out_ref):
@@ -431,18 +435,20 @@
         first, second = [0, top], [bit, bit ^ top]
         tick(7, [hidden])
         keep_a, send_a = run([0, 1, top, top + 1], jnp.stack([chip ^ (key // 2) for key in first]), hidden)
-        (send_a,) = clock.tick([send_a], [have["u far"], have["turned", top + 1 + bit]])
+        (send_a,) = clock.tick([send_a])
         near_a = swap(send_a, 1, n)
+        clock.tick([], [have["u far"], have["turned", top + 1 + bit]])
         tick(8)
-        tick(9)
+        clock.tick([], [near_a])
+        other, own_a = add(keep_a, near_a)
+        (other,) = clock.tick([other])
+        far_a = swap(other, top, n)
         keys = [bit, bit + 1, bit + top, bit + top + 1]
-        have["turned", bit] = hold([have["turned", bit]], near_a)[0]
+        have["turned", bit] = hold([have["turned", bit]])[0]
         keep, send = run(keys, jnp.stack([chip ^ (key // 2) for key in second]), hidden)
         (send,) = clock.tick([send])
         near = swap(send, 1, n)
-        other, own_a = add(keep_a, near_a)
-        (other,) = clock.tick([other])
-        far_a = swap(other, top, n)
+        tick(9)
     else:
         keep, send = run(list(range(n)), jnp.arange(m, dtype=jnp.int32), hidden)
         near = swap(send, 1, n)
@@ -480,7 +486,7 @@
     got_0 = swap(other, top, n)
     blocks = hold(blocks)
     keep_1, send_1 = back(here, lax.rem(z + steps[1], m), m, d_pre, d_up, blocks)
-    (send_1,) = clock.tick([send_1], [got_0, *late[1:]])
+    (send_1,) = clock.tick([send_1], [got_0, *late])
     near_1 = swap(send_1, 1, n)
     clock.tick([], [near_1])
     other, own_1 = add(keep_1, near_1)
@@ -494,7 +500,7 @@
         half, at = divmod(i, m // 2)
         value = owns[half][at] + wide(gots[half][at])
         if step:
-            (value,) = clock.tick([value.astype(jnp.bfloat16)], late[:1] if i == 0 else [])
+            (value,) = clock.tick([value.astype(jnp.bfloat16)])
             value = wide(shift(value, step))
         grad = grad + value
     return combined.astype(jnp.bfloat16), grad.astype(jnp.bfloat16)

time: 320 us -> 315 us (0.984)
  local copies, waits for them, and re-layouts: 37 us -> 31.5 us
  starting transfers between devices: 27.5 us -> 32.7 us
  waiting for transfers between devices: 154 us -> 150 us
    ppermute x6, waiting for transfers between devices: 36.4 us -> 30.8 us  [shift(): return lax.ppermute(value, 'etp', [(i, (i + step) % m) for i in range(m)])]
    unnamed x116 -> x94, local copies, waits for them, and re-layouts: 37 us -> 31.5 us
  transfers between devices with their start and end apart: 34 -> 34, of which waited for: 18 -> 18; matrix products, arithmetic and copies ran while one was open for 8% -> 7% of each run, Pallas kernels for 19% -> 21%
where the time goes in v4:
time: 315 us; the launch traced here: 311 us
  waiting for transfers between devices  150 us (48%)
  Pallas kernels  71.2 us (23%)
  starting transfers between devices  32.7 us (10%)
  local copies, waits for them, and re-layouts  31.5 us (10%)
  other arithmetic  24.8 us (8%)
    ppermute x28, waiting for transfers between devices, swap(): return lax.ppermute(value, 'dp', [(i, i ^ mask) for i in range(size)])  119 us
    unnamed x94, local copies, waits for them, and re-layouts  31.5 us
    ppermute x6, waiting for transfers between devices, shift(): return lax.ppermute(value, 'etp', [(i, (i + step) % m) for i in range(m)])  30.8 us
    pallas_call x2, Pallas kernels, on_tokens(): pl.pallas_call(functools.partial(kernel, n), grid_spec=pltpu.PrefetchScal...  29.1 us
    ppermute x28, starting transfers between devices, swap(): return lax.ppermute(value, 'dp', [(i, i ^ mask) for i in range(size)])  22.2 us
    pallas_call x2, Pallas kernels, back(): pl.pallas_call(functools.partial(back_kernel, n), grid_spec=pltpu.Prefetc...  18.2 us
    pallas_call x2, Pallas kernels, produce(): pl.pallas_call(functools.partial(produce_kernel, keys), grid_spec=pltpu.P...  15 us
    ppermute x6, starting transfers between devices, shift(): return lax.ppermute(value, 'etp', [(i, (i + step) % m) for i in range(m)])  10.5 us
  transfers between devices with their start and end apart: 34, of which 18 were waited for; matrix products, arithmetic and copies ran while one was open for 7% of the time, Pallas kernels for 21%

profile of v4, /device:TPU:11, one launch (start us, length us, event | category | flops | bytes accessed | tf_op | source)
XLA Modules:
  0.0 311.3 jit_solution(8634968109659419539)
XLA Ops:
  0.8 2.3 copy-done.2
  3.1 5.7 %cast_rows.1 = (bf16[2,384,768]{2,1,0:T(8,128)(2,1)}, bf16[2,384,768]{2,1,0:T(8,128)(2,1)}, bf16[2,384,768]{2,1,0:T(8,128)(2,1)}, bf16[2,384,768]{2,1,0:T(8,128)(2,1)}) custom-call(s32[4]{0:T(128)S(1)} %pad_add_fusion.2.pick_ref, f32[2,384,1536]{2,1,0:T(8,128)S(1)} %copy-done.2, f32[2,384,1536]{2,1,0:T(8,128)} %up_ref.1), custom_call_target="tpu_custom_call" | custom-call | tf_op jit(solution)/shard_map/cast_rows/pallas_call | solution.py:81
  9.5 1.2 collective-permute-start.1
  11.0 2.3 copy-done.3
  14.0 3.0 cast_turned.1
  19.5 1.2 collective-permute-start.6
  23.0 14.4 %collective-permute-done.1.refs_2_ = bf16[2,384,768]{2,1,0:T(8,128)(2,1)} collective-permute-done((bf16[2,384,768]{2,1,0:T(8,128)(2,1)}, bf16[2,384,768]{2,1,0:T(8,128)(2,1)}, u32[]{:S(2)}, u32[]{:S(2)}) %collective-permute-start.1) | collective-permute-done | bytes 1179680 | tf_op jit(solution)/shard_map/ppermute | solution.py:59
  41.7 1.2 copy-done.7
  43.0 20.6 %collective-permute-done.4.refs_3_ = bf16[2,384,768]{2,1,0:T(8,128)(2,1)} collective-permute-done((bf16[2,384,768]{2,1,0:T(8,128)(2,1)}, bf16[2,384,768]{2,1,0:T(8,128)(2,1)}, u32[]{:S(2)}, u32[]{:S(2)}) %collective-permute-start.4) | collective-permute-done | bytes 1179680 | tf_op jit(solution)/shard_map/ppermute | solution.py:59
  63.6 11.7 %collective-permute-done.5.refs_4_.refs_3_ = bf16[384,768]{1,0:T(8,128)(2,1)S(1)} collective-permute-done((bf16[384,768]{1,0:T(8,128)(2,1)}, bf16[384,768]{1,0:T(8,128)(2,1)S(1)}, u32[]{:S(2)}, u32[]{:S(2)}) %collective-permute-start.5) | collective-permute-done | bytes 589856 | tf_op jit(solution)/shard_map/ppermute | solution.py:59
  76.1 1.2 collective-permute-start.9
  79.0 9.8 %collective-permute-done.8.refs_2_.refs_10_.refs_6_ = bf16[2,384,768]{2,1,0:T(8,128)(2,1)} collective-permute-done((bf16[2,384,768]{2,1,0:T(8,128)(2,1)}, bf16[2,384,768]{2,1,0:T(8,128)(2,1)}, u32[]{:S(2)}, u32[]{:S(2)}) %collective-permute-start.8) | collective-permute-done | bytes 1179680 | tf_op jit(solution)/shard_map/ppermute | solution.py:59
  89.1 38.3 %collective-permute-done.10.refs_5_.refs_2_ = bf16[384,768]{1,0:T(8,128)(2,1)} collective-permute-done((bf16[384,768]{1,0:T(8,128)(2,1)}, bf16[384,768]{1,0:T(8,128)(2,1)}, u32[]{:S(2)}, u32[]{:S(2)}) %collective-permute-start.10) | collective-permute-done | bytes 589856 | tf_op jit(solution)/shard_map/ppermute | solution.py:59
  130.2 1.2 collective-permute-start.15
  131.5 1.8 collective-permute-done.13.refs_3_
  133.2 1.2 copy-done.37
  136.3 17.4 %forward.1 = (bf16[4,256,768]{2,1,0:T(8,128)(2,1)S(1)}, bf16[4,256,768]{2,1,0:T(8,128)(2,1)S(1)}, bf16[4,256,768]{2,1,0:T(8,128)(2,1)S(1)}) custom-call(s32[2]{0:T(128)S(1)} %pad_add_fusion.1.info_ref.me_ref, bf16[272,3072]{1,0:T(8,128)(2,1)} %get-tuple-element.101.refs_0_, bf16[272,3072]{1,0:T(8,128)(2,1)} %copy-done.36, ...), custom_call_target="tpu_custom_call" | custom-call | flops 9663676416 | bytes 15728640 | tf_op jit(solution)/shard_map/forward/pallas_call | solution.py:190
  158.6 1.4 copy-done.17
  160.0 7.5 %produce.2 = (bf16[2,2,256,768]{3,2,1,0:T(8,128)(2,1)}, bf16[2,2,256,768]{3,2,1,0:T(8,128)(2,1)}) custom-call(s32[1]{0:T(128)} %bitcast.me_ref, s32[2]{0:T(128)S(1)} %pad_add_fusion.3.ids_ref, bf16[4,256,768]{2,1,0:T(8,128)(2,1)S(1)} %copy-done.17, bf16[384,768]{1,0:T(8,128)(2,1)} %get-tuple-element.108.refs_0_.refs_4_, ...), custom_call_target="tpu_custom_call" | custom-call | flops 2415919104 | bytes 4718592 | tf_op jit(solution)/shard_map/produce/pallas_call | solution.py:242
  167.5 1.5 collective-permute-start.19
  169.0 1.3 collective-permute-done.17.refs_2_.refs_3_.refs_11_
  173.4 1.4 copy-done.24
  174.8 3.1 convert_add_fusion.2
  177.9 7.5 %produce.3 = (bf16[2,2,256,768]{3,2,1,0:T(8,128)(2,1)}, bf16[2,2,256,768]{3,2,1,0:T(8,128)(2,1)}) custom-call(s32[1]{0:T(128)} %bitcast.me_ref, s32[2]{0:T(128)S(1)} %pad_add_fusion.ids_ref, bf16[4,256,768]{2,1,0:T(8,128)(2,1)S(1)} %copy-done.17, bf16[384,768]{1,0:T(8,128)(2,1)} %get-tuple-element.125.refs_0_.refs_6_, bf16[384,768]{1,0:T(8,128)(2,1)} %copy-done.42, ...), custom_call_target="tpu_custom_call" | custom-call | flops 2415919104 | bytes 4718592 | tf_op jit(solution)/shard_map/produce/pallas_call | solution.py:242
  187.3 1.8 collective-permute-done.20.refs_1_
  190.3 3.2 %convert_add_fusion.3 = (f32[2,1,256,768]{3,2,1,0:T(8,128)}, bf16[2,256,768]{2,1,0:T(8,128)(2,1)}) fusion(bf16[2,2,256,768]{3,2,1,0:T(8,128)(2,1)} %copy-done.27, bf16[2,2,256,768]{3,2,1,0:T(8,128)(2,1)S(1)} %copy-done.25), kind=kLoop, calls=%fused_computation.6 | loop fusion | flops 2752512 | bytes 5505024 | tf_op jit(solution)/shard_map/add | solution.py:429
  194.6 1.4 copy-done.14
  196.0 11.7 %grow.1 = (bf16[4,256,768]{2,1,0:T(8,128)(2,1)S(1)}, bf16[4,256,768]{2,1,0:T(8,128)(2,1)S(1)}) custom-call(s32[2]{0:T(128)S(1)} %pad_add_fusion.1.info_ref.me_ref, bf16[4,256,768]{2,1,0:T(8,128)(2,1)S(1)} %copy-done.14, bf16[4,256,768]{2,1,0:T(8,128)(2,1)} %copy-done.15, bf16[256,3072]{1,0:T(8,128)(2,1)} %get-tuple-element.138.refs_0_, ...), custom_call_target="tpu_custom_call" | custom-call | flops 4831838208 | bytes 11010048 | tf_op jit(solution)/shard_map/grow/pallas_call | solution.py:190
  208.9 1.4 copy-done.12
  210.3 9.1 %back.2 = (bf16[2,2,256,768]{3,2,1,0:T(8,128)(2,1)}, bf16[2,2,256,768]{3,2,1,0:T(8,128)(2,1)}) custom-call(s32[1]{0:T(128)} %bitcast.me_ref, s32[2]{0:T(128)S(1)} %get-tuple-element.184.ids_ref, bf16[4,256,768]{2,1,0:T(8,128)(2,1)S(1)} %copy-done.12, bf16[4,256,768]{2,1,0:T(8,128)(2,1)S(1)} %get-tuple-element.141.up_ref, ...), custom_call_target="tpu_custom_call" | custom-call | flops 4831838208 | bytes 7864320 | tf_op jit(solution)/shard_map/back/pallas_call | solution.py:293
  219.4 2.7 collective-permute-done.22.refs_3_
  222.1 1.2 collective-permute-start.27
  223.3 3.4 %select_bitcast_fusion = (bf16[256,768]{1,0:T(8,128)(2,1)}, bf16[1,256,768]{2,1,0:T(8,128)(2,1)S(1)}, bf16[1,256,768]{2,1,0:T(8,128)(2,1)S(1)}, bf16[1,256,768]{2,1,0:T(8,128)(2,1)S(1)}, bf16[1,256,768]{2,1,0:T(8,128)(2,1)S(1)}) fusion(pred[]{:T(512)S(6)} %eq.80, pred[]{:T(512)S(6)} %eq.81, pred[]{:T(512)S(6)} %eq.82, ...), kind=kLoop, calls=%fused_computation.47 | loop fusion | flops 2949120 | bytes 6684675 | tf_op jit(solution)/shard_map/jit(_where)/select_n | solution.py:476
  227.9 1.3 collective-permute-start.25
  229.2 4.1 %collective-permute-start.24 = (bf16[256,768]{1,0:T(8,128)(2,1)}, bf16[256,768]{1,0:T(8,128)(2,1)}, u32[]{:S(2)}, u32[]{:S(2)}) collective-permute-start(bf16[256,768]{1,0:T(8,128)(2,1)} %get-tuple-element.145), channel_id=1, source_target_pairs={{0,2},{1,3},{2,0},{3,1},{4,6},{5,7},{6,4},{7,5},{8,10},{9,11},{10,... | collective-permute-start | bytes 1179656 | tf_op jit(solution)/shard_map/ppermute | solution.py:361
  233.3 3.7 %convert_add_fusion.1 = (f32[2,1,256,768]{3,2,1,0:T(8,128)}, bf16[2,256,768]{2,1,0:T(8,128)(2,1)}) fusion(bf16[2,2,256,768]{3,2,1,0:T(8,128)(2,1)} %collective-permute-done.27.refs_1_, bf16[2,2,256,768]{3,2,1,0:T(8,128)(2,1)} %get-tuple-element.150), kind=kLoop, calls=%fused_computation.1 | loop fusion | flops 2752512 | bytes 5505024 | tf_op jit(solution)/shard_map/add | solution.py:429
  238.1 9.1 %back.3 = (bf16[2,2,256,768]{3,2,1,0:T(8,128)(2,1)}, bf16[2,2,256,768]{3,2,1,0:T(8,128)(2,1)}) custom-call(s32[1]{0:T(128)} %bitcast.me_ref, s32[2]{0:T(128)S(1)} %get-tuple-element.183.ids_ref, bf16[4,256,768]{2,1,0:T(8,128)(2,1)S(1)} %copy-done.12, bf16[4,256,768]{2,1,0:T(8,128)(2,1)S(1)} %get-tuple-element.141.up_ref, ...), custom_call_target="tpu_custom_call" | custom-call | flops 4831838208 | bytes 7864320 | tf_op jit(solution)/shard_map/back/pallas_call | solution.py:293
  247.2 2.1 collective-permute-done.25.refs_4_
  249.2 13.7 %collective-permute-done.24.refs_3_ = bf16[256,768]{1,0:T(8,128)(2,1)} collective-permute-done((bf16[256,768]{1,0:T(8,128)(2,1)}, bf16[256,768]{1,0:T(8,128)(2,1)}, u32[]{:S(2)}, u32[]{:S(2)}) %collective-permute-start.24) | collective-permute-done | bytes 393248 | tf_op jit(solution)/shard_map/ppermute | solution.py:361
  264.4 2.3 fusion.27
  267.4 1.5 fusion.3
  271.1 3.1 collective-permute-start.30
  274.2 13.8 %collective-permute-done.32 = bf16[2,256,768]{2,1,0:T(8,128)(2,1)S(1)} collective-permute-done((bf16[2,256,768]{2,1,0:T(8,128)(2,1)}, bf16[2,256,768]{2,1,0:T(8,128)(2,1)S(1)}, u32[]{:S(2)}, u32[]{:S(2)}) %collective-permute-start.32) | collective-permute-done | bytes 786464 | tf_op jit(solution)/shard_map/ppermute | solution.py:59
  289.0 1.8 collective-permute-start.33
  290.9 3.1 %fusion.20 = bf16[256,768]{1,0:T(8,128)(2,1)} fusion(bf16[256,768]{1,0:T(8,128)(2,1)} %copy-done.32, bf16[256,768]{1,0:T(8,128)(2,1)} %collective-permute-done.25.refs_4_, bf16[256,768]{1,0:T(8,128)(2,1)} %collective-permute-done.24.refs_3_, f32[2,1,256,768]{3,2,1,0:T(8,128)S(1)} %copy-done.19, f32[2,1,256,768]{3,2,1,0:T(8,128)S(1)} %copy-done.18, ...), kind=kLoop, calls=%fused_computation.37 | loop fusion | flops 3538944 | bytes 6291459 | tf_op jit(solution)/shard_map/convert_element_type | solution.py:506
  294.0 9.3 %collective-permute-done.30 = bf16[256,768]{1,0:T(8,128)(2,1)} collective-permute-done((bf16[256,768]{1,0:T(8,128)(2,1)S(1)}, bf16[256,768]{1,0:T(8,128)(2,1)}, u32[]{:S(2)}, u32[]{:S(2)}) %collective-permute-start.30) | collective-permute-done | bytes 393248 | tf_op jit(solution)/shard_map/ppermute | solution.py:361
  303.3 5.7 %collective-permute-done.33 = bf16[256,768]{1,0:T(8,128)(2,1)} collective-permute-done((bf16[256,768]{1,0:T(8,128)(2,1)}, bf16[256,768]{1,0:T(8,128)(2,1)}, u32[]{:S(2)}, u32[]{:S(2)}) %collective-permute-start.33) | collective-permute-done | bytes 393248 | tf_op jit(solution)/shard_map/ppermute | solution.py:361
  309.1 2.2 fusion.7
  (175 shorter events, 39.1 us)
Async XLA Ops:
  0.6 18.1 %copy-start = (s32[4]{0:T(128)S(1)}, s32[4]{0:T(128)}, u32[]{:S(2)}) copy-start(s32[4]{0:T(128)} %param.16) | copy-start | bytes 52
  0.8 2.3 copy-start.2
  8.8 8.2 %collective-permute-start = (bf16[2,384,768]{2,1,0:T(8,128)(2,1)}, bf16[2,384,768]{2,1,0:T(8,128)(2,1)S(1)}, u32[]{:S(2)}, u32[]{:S(2)}) collective-permute-start(bf16[2,384,768]{2,1,0:T(8,128)(2,1)} %get-tuple-element.90), channel_id=1, source_target_pairs={{0,4},{4,0},{8,12},{12,8},{16,20},{20,16},{24,28},{28,24},{1,5},{5... | collective-permute-start | bytes 3538952 | tf_op jit(solution)/shard_map/ppermute | solution.py:59
  9.5 27.8 %collective-permute-start.1 = (bf16[2,384,768]{2,1,0:T(8,128)(2,1)}, bf16[2,384,768]{2,1,0:T(8,128)(2,1)}, u32[]{:S(2)}, u32[]{:S(2)}) collective-permute-start(bf16[2,384,768]{2,1,0:T(8,128)(2,1)} %get-tuple-element.93), channel_id=1, source_target_pairs={{0,16},{4,20},{8,24},{12,28},{16,0},{20,4},{24,8},{28,12},{1,17},{... | collective-permute-start | bytes 3538952 | tf_op jit(solution)/shard_map/ppermute | solution.py:59
  10.8 27.5 %collective-permute-start.3 = (bf16[2,384,768]{2,1,0:T(8,128)(2,1)}, bf16[2,384,768]{2,1,0:T(8,128)(2,1)S(1)}, u32[]{:S(2)}, u32[]{:S(2)}) collective-permute-start(bf16[2,384,768]{2,1,0:T(8,128)(2,1)} %get-tuple-element.95.refs_1_), channel_id=1, source_target_pairs={{0,8},{4,12},{8,0},{12,4},{16,24},{20,28},{24,16},{28,20},{1,9},{5... | collective-permute-start | bytes 3538952 | tf_op jit(solution)/shard_map/ppermute | solution.py:59
  11.0 2.3 copy-start.3
  18.1 2.6 copy-start.46
  18.1 2.9 copy-start.5
  18.1 20.2 %collective-permute-start.2 = (bf16[384,768]{1,0:T(8,128)(2,1)}, bf16[384,768]{1,0:T(8,128)(2,1)S(1)}, u32[]{:S(2)}, u32[]{:S(2)}) collective-permute-start(bf16[384,768]{1,0:T(8,128)(2,1)} %get-tuple-element.94), channel_id=1, source_target_pairs={{0,4},{4,0},{8,12},{12,8},{16,20},{20,16},{24,28},{28,24},{1,5},{5... | collective-permute-start | bytes 1769480 | tf_op jit(solution)/shard_map/ppermute | solution.py:59
  18.8 44.7 %collective-permute-start.4 = (bf16[2,384,768]{2,1,0:T(8,128)(2,1)}, bf16[2,384,768]{2,1,0:T(8,128)(2,1)}, u32[]{:S(2)}, u32[]{:S(2)}) collective-permute-start(bf16[2,384,768]{2,1,0:T(8,128)(2,1)} %get-tuple-element.98), channel_id=1, source_target_pairs={{0,20},{4,16},{8,28},{12,24},{16,4},{20,0},{24,12},{28,8},{1,21},{... | collective-permute-start | bytes 3538952 | tf_op jit(solution)/shard_map/ppermute | solution.py:59
  19.5 55.8 %collective-permute-start.6 = (bf16[2,384,768]{2,1,0:T(8,128)(2,1)}, bf16[2,384,768]{2,1,0:T(8,128)(2,1)}, u32[]{:S(2)}, u32[]{:S(2)}) collective-permute-start(bf16[2,384,768]{2,1,0:T(8,128)(2,1)} %get-tuple-element.100.refs_5_.refs_1_), channel_id=1, source_target_pairs={{0,8},{4,12},{8,0},{12,4},{16,24},{20,28},{24,16},{28,20},{1,9},{5... | collective-permute-start | bytes 3538952 | tf_op jit(solution)/shard_map/ppermute | solution.py:59
  39.5 35.7 %collective-permute-start.5 = (bf16[384,768]{1,0:T(8,128)(2,1)}, bf16[384,768]{1,0:T(8,128)(2,1)S(1)}, u32[]{:S(2)}, u32[]{:S(2)}) collective-permute-start(bf16[384,768]{1,0:T(8,128)(2,1)} %get-tuple-element.99), channel_id=1, source_target_pairs={{0,16},{4,20},{8,24},{12,28},{16,0},{20,4},{24,8},{28,12},{1,17},{... | collective-permute-start | bytes 1769480 | tf_op jit(solution)/shard_map/ppermute | solution.py:59
  39.9 49.0 %collective-permute-start.8 = (bf16[2,384,768]{2,1,0:T(8,128)(2,1)}, bf16[2,384,768]{2,1,0:T(8,128)(2,1)}, u32[]{:S(2)}, u32[]{:S(2)}) collective-permute-start(bf16[2,384,768]{2,1,0:T(8,128)(2,1)} %get-tuple-element.104.refs_8_.refs_4_), channel_id=1, source_target_pairs={{0,8},{4,12},{8,0},{12,4},{16,24},{20,28},{24,16},{28,20},{1,9},{5... | collective-permute-start | bytes 3538952 | tf_op jit(solution)/shard_map/ppermute | solution.py:59
  76.1 51.3 %collective-permute-start.9 = (bf16[272,3072]{1,0:T(8,128)(2,1)}, bf16[272,3072]{1,0:T(8,128)(2,1)S(1)}, u32[]{:S(2)}, u32[]{:S(2)}) collective-permute-start(bf16[272,3072]{1,0:T(8,128)(2,1)} %get-tuple-element.101.refs_0_), channel_id=1, source_target_pairs={{0,16},{4,20},{8,24},{12,28},{16,0},{20,4},{24,8},{28,12},{1,17},{... | collective-permute-start | bytes 5013512 | tf_op jit(solution)/shard_map/ppermute | solution.py:59
  77.4 50.1 %collective-permute-start.7 = (bf16[272,3072]{1,0:T(8,128)(2,1)}, bf16[272,3072]{1,0:T(8,128)(2,1)S(1)}, u32[]{:S(2)}, u32[]{:S(2)}) collective-permute-start(bf16[272,3072]{1,0:T(8,128)(2,1)} %get-tuple-element.101.refs_0_), channel_id=1, source_target_pairs={{0,4},{4,0},{8,12},{12,8},{16,20},{20,16},{24,28},{28,24},{1,5},{5... | collective-permute-start | bytes 5013512 | tf_op jit(solution)/shard_map/ppermute | solution.py:59
  78.4 49.1 %collective-permute-start.11 = (bf16[2,384,768]{2,1,0:T(8,128)(2,1)}, bf16[2,384,768]{2,1,0:T(8,128)(2,1)}, u32[]{:S(2)}, u32[]{:S(2)}) collective-permute-start(bf16[2,384,768]{2,1,0:T(8,128)(2,1)} %get-tuple-element.107.refs_9_.refs_5_), channel_id=1, source_target_pairs={{0,8},{4,12},{8,0},{12,4},{16,24},{20,28},{24,16},{28,20},{1,9},{5... | collective-permute-start | bytes 3538952 | tf_op jit(solution)/shard_map/ppermute | solution.py:59
  78.6 48.8 %collective-permute-start.10 = (bf16[384,768]{1,0:T(8,128)(2,1)}, bf16[384,768]{1,0:T(8,128)(2,1)}, u32[]{:S(2)}, u32[]{:S(2)}) collective-permute-start(bf16[384,768]{1,0:T(8,128)(2,1)} %get-tuple-element.106), channel_id=1, source_target_pairs={{0,20},{4,16},{8,28},{12,24},{16,4},{20,0},{24,12},{28,8},{1,21},{... | collective-permute-start | bytes 1769480 | tf_op jit(solution)/shard_map/ppermute | solution.py:59
  88.8 38.6 %collective-permute-start.12 = (bf16[384,768]{1,0:T(8,128)(2,1)}, bf16[384,768]{1,0:T(8,128)(2,1)S(1)}, u32[]{:S(2)}, u32[]{:S(2)}) collective-permute-start(bf16[384,768]{1,0:T(8,128)(2,1)} %get-tuple-element.108.refs_0_.refs_4_), channel_id=1, source_target_pairs={{0,8},{4,12},{8,0},{12,4},{16,24},{20,28},{24,16},{28,20},{1,9},{5... | collective-permute-start | bytes 1769480 | tf_op jit(solution)/shard_map/ppermute | solution.py:59
  129.5 3.8 %collective-permute-start.13 = (bf16[272,3072]{1,0:T(8,128)(2,1)}, bf16[272,3072]{1,0:T(8,128)(2,1)S(1)}, u32[]{:S(2)}, u32[]{:S(2)}) collective-permute-start(bf16[272,3072]{1,0:T(8,128)(2,1)} %get-tuple-element.109.refs_2_), channel_id=1, source_target_pairs={{0,4},{4,0},{8,12},{12,8},{16,20},{20,16},{24,28},{28,24},{1,5},{5... | collective-permute-start | bytes 5013512 | tf_op jit(solution)/shard_map/ppermute | solution.py:59
  130.0 27.2 %collective-permute-start.14 = (bf16[384,768]{1,0:T(8,128)(2,1)}, bf16[384,768]{1,0:T(8,128)(2,1)S(1)}, u32[]{:S(2)}, u32[]{:S(2)}) collective-permute-start(bf16[384,768]{1,0:T(8,128)(2,1)} %get-tuple-element.115.refs_1_.refs_5_), channel_id=1, source_target_pairs={{0,8},{4,12},{8,0},{12,4},{16,24},{20,28},{24,16},{28,20},{1,9},{5... | collective-permute-start | bytes 1769480 | tf_op jit(solution)/shard_map/ppermute | solution.py:59
  130.2 27.5 %collective-permute-start.15 = (bf16[384,768]{1,0:T(8,128)(2,1)}, bf16[384,768]{1,0:T(8,128)(2,1)S(1)}, u32[]{:S(2)}, u32[]{:S(2)}) collective-permute-start(bf16[384,768]{1,0:T(8,128)(2,1)} %get-tuple-element.116.refs_2_.refs_8_), channel_id=1, source_target_pairs={{0,8},{4,12},{8,0},{12,4},{16,24},{20,28},{24,16},{28,20},{1,9},{5... | collective-permute-start | bytes 1769480 | tf_op jit(solution)/shard_map/ppermute | solution.py:59
  134.5 35.9 %collective-permute-start.16 = (bf16[256,3072]{1,0:T(8,128)(2,1)}, bf16[256,3072]{1,0:T(8,128)(2,1)}, u32[]{:S(2)}, u32[]{:S(2)}) collective-permute-start(bf16[256,3072]{1,0:T(8,128)(2,1)} %get-tuple-element.120.refs_1_), channel_id=1, source_target_pairs={{0,16},{4,20},{8,24},{12,28},{16,0},{20,4},{24,8},{28,12},{1,17},{... | collective-permute-start | bytes 4718600 | tf_op jit(solution)/shard_map/ppermute | solution.py:59
  135.6 34.8 %collective-permute-start.18 = (bf16[256,3072]{1,0:T(8,128)(2,1)}, bf16[256,3072]{1,0:T(8,128)(2,1)}, u32[]{:S(2)}, u32[]{:S(2)}) collective-permute-start(bf16[256,3072]{1,0:T(8,128)(2,1)} %get-tuple-element.120.refs_1_), channel_id=1, source_target_pairs={{0,4},{4,0},{8,12},{12,8},{16,20},{20,16},{24,28},{28,24},{1,5},{5... | collective-permute-start | bytes 4718600 | tf_op jit(solution)/shard_map/ppermute | solution.py:59
  136.0 34.4 %collective-permute-start.17 = (bf16[384,768]{1,0:T(8,128)(2,1)}, bf16[384,768]{1,0:T(8,128)(2,1)}, u32[]{:S(2)}, u32[]{:S(2)}) collective-permute-start(bf16[384,768]{1,0:T(8,128)(2,1)} %get-tuple-element.117.refs_3_.refs_9_), channel_id=1, source_target_pairs={{0,8},{4,12},{8,0},{12,4},{16,24},{20,28},{24,16},{28,20},{1,9},{5... | collective-permute-start | bytes 1769480 | tf_op jit(solution)/shard_map/ppermute | solution.py:59
  167.5 4.7 %collective-permute-start.19 = (bf16[2,2,256,768]{3,2,1,0:T(8,128)(2,1)}, bf16[2,2,256,768]{3,2,1,0:T(8,128)(2,1)S(1)}, u32[]{:S(2)}, u32[]{:S(2)}) collective-permute-start(bf16[2,2,256,768]{3,2,1,0:T(8,128)(2,1)} %get-tuple-element.122), channel_id=1, source_target_pairs={{0,4},{4,0},{8,12},{12,8},{16,20},{20,16},{24,28},{28,24},{1,5},{5... | collective-permute-start | bytes 4718600 | tf_op jit(solution)/shard_map/ppermute | solution.py:59
  170.4 16.9 %collective-permute-start.21 = (bf16[256,3072]{1,0:T(8,128)(2,1)}, bf16[256,3072]{1,0:T(8,128)(2,1)}, u32[]{:S(2)}, u32[]{:S(2)}) collective-permute-start(bf16[256,3072]{1,0:T(8,128)(2,1)} %get-tuple-element.131.refs_2_), channel_id=1, source_target_pairs={{0,4},{4,0},{8,12},{12,8},{16,20},{20,16},{24,28},{28,24},{1,5},{5... | collective-permute-start | bytes 4718600 | tf_op jit(solution)/shard_map/ppermute | solution.py:59
  185.4 3.7 %collective-permute-start.20 = (bf16[2,2,256,768]{3,2,1,0:T(8,128)(2,1)}, bf16[2,2,256,768]{3,2,1,0:T(8,128)(2,1)S(1)}, u32[]{:S(2)}, u32[]{:S(2)}) collective-permute-start(bf16[2,2,256,768]{3,2,1,0:T(8,128)(2,1)} %get-tuple-element.129), channel_id=1, source_target_pairs={{0,4},{4,0},{8,12},{12,8},{16,20},{20,16},{24,28},{28,24},{1,5},{5... | collective-permute-start | bytes 4718600 | tf_op jit(solution)/shard_map/ppermute | solution.py:59
  186.1 33.3 %collective-permute-start.23 = (bf16[2,256,768]{2,1,0:T(8,128)(2,1)}, bf16[2,256,768]{2,1,0:T(8,128)(2,1)}, u32[]{:S(2)}, u32[]{:S(2)}) collective-permute-start(bf16[2,256,768]{2,1,0:T(8,128)(2,1)} %get-tuple-element.133), channel_id=1, source_target_pairs={{0,16},{4,20},{8,24},{12,28},{16,0},{20,4},{24,8},{28,12},{1,17},{... | collective-permute-start | bytes 2359304 | tf_op jit(solution)/shard_map/ppermute | solution.py:59
  187.3 3.0 copy-start.25
  193.5 28.6 %collective-permute-start.22 = (bf16[2,256,768]{2,1,0:T(8,128)(2,1)}, bf16[2,256,768]{2,1,0:T(8,128)(2,1)}, u32[]{:S(2)}, u32[]{:S(2)}) collective-permute-start(bf16[2,256,768]{2,1,0:T(8,128)(2,1)} %get-tuple-element.132), channel_id=1, source_target_pairs={{0,16},{4,20},{8,24},{12,28},{16,0},{20,4},{24,8},{28,12},{1,17},{... | collective-permute-start | bytes 2359304 | tf_op jit(solution)/shard_map/ppermute | solution.py:59
  222.1 11.2 %collective-permute-start.27 = (bf16[2,2,256,768]{3,2,1,0:T(8,128)(2,1)}, bf16[2,2,256,768]{3,2,1,0:T(8,128)(2,1)}, u32[]{:S(2)}, u32[]{:S(2)}) collective-permute-start(bf16[2,2,256,768]{3,2,1,0:T(8,128)(2,1)} %get-tuple-element.149), channel_id=1, source_target_pairs={{0,4},{4,0},{8,12},{12,8},{16,20},{20,16},{24,28},{28,24},{1,5},{5... | collective-permute-start | bytes 4718600 | tf_op jit(solution)/shard_map/ppermute | solution.py:59
  227.7 19.5 %collective-permute-start.26 = (bf16[256,768]{1,0:T(8,128)(2,1)}, bf16[256,768]{1,0:T(8,128)(2,1)S(1)}, u32[]{:S(2)}, u32[]{:S(2)}) collective-permute-start(bf16[256,768]{1,0:T(8,128)(2,1)} %get-tuple-element.147), channel_id=1, source_target_pairs={{0,3},{1,0},{2,1},{3,2},{4,7},{5,4},{6,5},{7,6},{8,11},{9,8},{10,9... | collective-permute-start | bytes 1179656 | tf_op jit(solution)/shard_map/ppermute | solution.py:361
  227.9 21.4 %collective-permute-start.25 = (bf16[256,768]{1,0:T(8,128)(2,1)}, bf16[256,768]{1,0:T(8,128)(2,1)}, u32[]{:S(2)}, u32[]{:S(2)}) collective-permute-start(bf16[256,768]{1,0:T(8,128)(2,1)} %get-tuple-element.146), channel_id=1, source_target_pairs={{0,1},{1,2},{2,3},{3,0},{4,5},{5,6},{6,7},{7,4},{8,9},{9,10},{10,1... | collective-permute-start | bytes 1179656 | tf_op jit(solution)/shard_map/ppermute | solution.py:361
  229.2 33.8 %collective-permute-start.24 = (bf16[256,768]{1,0:T(8,128)(2,1)}, bf16[256,768]{1,0:T(8,128)(2,1)}, u32[]{:S(2)}, u32[]{:S(2)}) collective-permute-start(bf16[256,768]{1,0:T(8,128)(2,1)} %get-tuple-element.145), channel_id=1, source_target_pairs={{0,2},{1,3},{2,0},{3,1},{4,6},{5,7},{6,4},{7,5},{8,10},{9,11},{10,... | collective-permute-start | bytes 1179656 | tf_op jit(solution)/shard_map/ppermute | solution.py:361
  236.9 26.0 %collective-permute-start.28 = (bf16[2,256,768]{2,1,0:T(8,128)(2,1)}, bf16[2,256,768]{2,1,0:T(8,128)(2,1)}, u32[]{:S(2)}, u32[]{:S(2)}) collective-permute-start(bf16[2,256,768]{2,1,0:T(8,128)(2,1)} %get-tuple-element.155), channel_id=1, source_target_pairs={{0,16},{4,20},{8,24},{12,28},{16,0},{20,4},{24,8},{28,12},{1,17},{... | collective-permute-start | bytes 2359304 | tf_op jit(solution)/shard_map/ppermute | solution.py:59
  247.2 15.8 %copy-start.32 = (bf16[256,768]{1,0:T(8,128)(2,1)}, bf16[256,768]{1,0:T(8,128)(2,1)S(1)}, u32[]{:S(2)}) copy-start(bf16[256,768]{1,0:T(8,128)(2,1)S(1)} %collective-permute-done.26.refs_5_) | copy-start | bytes 1179652
  263.0 4.4 %collective-permute-start.29 = (bf16[2,2,256,768]{3,2,1,0:T(8,128)(2,1)}, bf16[2,2,256,768]{3,2,1,0:T(8,128)(2,1)S(1)}, u32[]{:S(2)}, u32[]{:S(2)}) collective-permute-start(bf16[2,2,256,768]{3,2,1,0:T(8,128)(2,1)} %get-tuple-element.157), channel_id=1, source_target_pairs={{0,4},{4,0},{8,12},{12,8},{16,20},{20,16},{24,28},{28,24},{1,5},{5... | collective-permute-start | bytes 4718600 | tf_op jit(solution)/shard_map/ppermute | solution.py:59
  264.4 3.0 copy-start.23
  268.9 19.0 %copy-start.21 = (f32[2,1,256,768]{3,2,1,0:T(8,128)}, f32[2,1,256,768]{3,2,1,0:T(8,128)S(1)}, u32[]{:S(2)}) copy-start(f32[2,1,256,768]{3,2,1,0:T(8,128)S(1)} %get-tuple-element.174) | copy-start | bytes 4718596
  268.9 19.0 %collective-permute-start.32 = (bf16[2,256,768]{2,1,0:T(8,128)(2,1)}, bf16[2,256,768]{2,1,0:T(8,128)(2,1)S(1)}, u32[]{:S(2)}, u32[]{:S(2)}) collective-permute-start(bf16[2,256,768]{2,1,0:T(8,128)(2,1)} %get-tuple-element.164), channel_id=1, source_target_pairs={{0,16},{4,20},{8,24},{12,28},{16,0},{20,4},{24,8},{28,12},{1,17},{... | collective-permute-start | bytes 2359304 | tf_op jit(solution)/shard_map/ppermute | solution.py:59
  270.1 24.0 %collective-permute-start.31 = (bf16[256,768]{1,0:T(8,128)(2,1)}, bf16[256,768]{1,0:T(8,128)(2,1)}, u32[]{:S(2)}, u32[]{:S(2)}) collective-permute-start(bf16[256,768]{1,0:T(8,128)(2,1)} %get-tuple-element.162), channel_id=1, source_target_pairs={{0,1},{1,2},{2,3},{3,0},{4,5},{5,6},{6,7},{7,4},{8,9},{9,10},{10,1... | collective-permute-start | bytes 1179656 | tf_op jit(solution)/shard_map/ppermute | solution.py:361
  271.1 32.2 %collective-permute-start.30 = (bf16[256,768]{1,0:T(8,128)(2,1)S(1)}, bf16[256,768]{1,0:T(8,128)(2,1)}, u32[]{:S(2)}, u32[]{:S(2)}) collective-permute-start(bf16[256,768]{1,0:T(8,128)(2,1)S(1)} %copy-done.31), channel_id=1, source_target_pairs={{0,2},{1,3},{2,0},{3,1},{4,6},{5,7},{6,4},{7,5},{8,10},{9,11},{10,... | collective-permute-start | bytes 1179656 | tf_op jit(solution)/shard_map/ppermute | solution.py:361
  289.0 1.8 copy-start.18
  289.0 1.9 copy-start.19
  289.0 20.1 %collective-permute-start.33 = (bf16[256,768]{1,0:T(8,128)(2,1)}, bf16[256,768]{1,0:T(8,128)(2,1)}, u32[]{:S(2)}, u32[]{:S(2)}) collective-permute-start(bf16[256,768]{1,0:T(8,128)(2,1)} %get-tuple-element.165), channel_id=1, source_target_pairs={{0,3},{1,0},{2,1},{3,2},{4,7},{5,4},{6,5},{7,6},{8,11},{9,8},{10,9... | collective-permute-start | bytes 1179656 | tf_op jit(solution)/shard_map/ppermute | solution.py:361
  290.9 18.2 %copy-start.22 = (f32[2,1,256,768]{3,2,1,0:T(8,128)S(1)}, f32[2,1,256,768]{3,2,1,0:T(8,128)}, u32[]{:S(2)}) copy-start(f32[2,1,256,768]{3,2,1,0:T(8,128)} %copy-done.21) | copy-start | bytes 4718596
  290.9 18.2 %copy-start.30 = (bf16[2,256,768]{2,1,0:T(8,128)(2,1)S(1)}, bf16[2,256,768]{2,1,0:T(8,128)(2,1)}, u32[]{:S(2)}) copy-start(bf16[2,256,768]{2,1,0:T(8,128)(2,1)} %copy-done.29) | copy-start | bytes 2359300
  290.9 20.4 %copy-start.1 = (s32[4]{0:T(128)S(1)}, s32[4]{0:T(128)}, u32[]{:S(2)}) copy-start(s32[4]{0:T(128)} %param.16) | copy-start | bytes 52
  (33 other events, 36.1 us)

commit v5 on v4

--- a/solution.py
+++ b/solution.py
@@ -486,8 +486,9 @@
     got_0 = swap(other, top, n)
     blocks = hold(blocks)
     keep_1, send_1 = back(here, lax.rem(z + steps[1], m), m, d_pre, d_up, blocks)
-    (send_1,) = clock.tick([send_1], [got_0, *late])
+    (send_1,) = clock.tick([send_1], late[1:])
     near_1 = swap(send_1, 1, n)
+    clock.tick([], [got_0])
     clock.tick([], [near_1])
     other, own_1 = add(keep_1, near_1)
     (other,) = clock.tick([other])
@@ -500,7 +501,7 @@
         half, at = divmod(i, m // 2)
         value = owns[half][at] + wide(gots[half][at])
         if step:
-            (value,) = clock.tick([value.astype(jnp.bfloat16)])
+            (value,) = clock.tick([value.astype(jnp.bfloat16)], late[:1] if i == 0 else [])
             value = wide(shift(value, step))
         grad = grad + value
     return combined.astype(jnp.bfloat16), grad.astype(jnp.bfloat16)

time: 315 us -> 310 us (0.984)
  starting transfers between devices: 32.7 us -> 29.5 us
    ppermute x28, waiting for transfers between devices: 119 us -> 110 us  [swap(): return lax.ppermute(value, 'dp', [(i, i ^ mask) for i in range(size)])]
    ppermute x6, waiting for transfers between devices: 30.8 us -> 39.1 us  [shift(): return lax.ppermute(value, 'etp', [(i, (i + step) % m) for i in range(m)])]
  transfers between devices with their start and end apart: 34 -> 34, of which waited for: 18 -> 18; matrix products, arithmetic and copies ran while one was open for 7% -> 8% of each run, Pallas kernels for 21% -> 21%
where the time goes in v5:
time: 310 us; the launch traced here: 309 us
  waiting for transfers between devices  149 us (48%)
  Pallas kernels  71.2 us (23%)
  local copies, waits for them, and re-layouts  32.8 us (11%)
  starting transfers between devices  29.5 us (10%)
  other arithmetic  25.7 us (8%)
    ppermute x28, waiting for transfers between devices, swap(): return lax.ppermute(value, 'dp', [(i, i ^ mask) for i in range(size)])  110 us
    ppermute x6, waiting for transfers between devices, shift(): return lax.ppermute(value, 'etp', [(i, (i + step) % m) for i in range(m)])  39.1 us
    unnamed x94, local copies, waits for them, and re-layouts  32.7 us
    pallas_call x2, Pallas kernels, on_tokens(): pl.pallas_call(functools.partial(kernel, n), grid_spec=pltpu.PrefetchScal...  29.1 us
    ppermute x28, starting transfers between devices, swap(): return lax.ppermute(value, 'dp', [(i, i ^ mask) for i in range(size)])  21.8 us
    pallas_call x2, Pallas kernels, back(): pl.pallas_call(functools.partial(back_kernel, n), grid_spec=pltpu.Prefetc...  18.2 us
    pallas_call x2, Pallas kernels, produce(): pl.pallas_call(functools.partial(produce_kernel, keys), grid_spec=pltpu.P...  15 us
    add x3, other arithmetic, add(): wide(keep[:, 0]) + wide(near[:, 0])  9.85 us
  transfers between devices with their start and end apart: 34, of which 18 were waited for; matrix products, arithmetic and copies ran while one was open for 8% of the time, Pallas kernels for 21%

profile of v5, /device:TPU:11, one launch (start us, length us, event | category | flops | bytes accessed | tf_op | source)
XLA Modules:
  0.0 309.1 jit_solution(5985067027805468719)
XLA Ops:
  0.8 2.3 copy-done.2
  3.1 5.7 %cast_rows.1 = (bf16[2,384,768]{2,1,0:T(8,128)(2,1)}, bf16[2,384,768]{2,1,0:T(8,128)(2,1)}, bf16[2,384,768]{2,1,0:T(8,128)(2,1)}, bf16[2,384,768]{2,1,0:T(8,128)(2,1)}) custom-call(s32[4]{0:T(128)S(1)} %pad_add_fusion.2.pick_ref, f32[2,384,1536]{2,1,0:T(8,128)S(1)} %copy-done.2, f32[2,384,1536]{2,1,0:T(8,128)} %up_ref.1), custom_call_target="tpu_custom_call" | custom-call | tf_op jit(solution)/shard_map/cast_rows/pallas_call | solution.py:81
  9.5 1.2 collective-permute-start.1
  11.0 2.3 copy-done.3
  14.0 3.0 cast_turned.1
  19.5 1.2 collective-permute-start.6
  23.0 14.4 %collective-permute-done.1.refs_2_ = bf16[2,384,768]{2,1,0:T(8,128)(2,1)} collective-permute-done((bf16[2,384,768]{2,1,0:T(8,128)(2,1)}, bf16[2,384,768]{2,1,0:T(8,128)(2,1)}, u32[]{:S(2)}, u32[]{:S(2)}) %collective-permute-start.1) | collective-permute-done | bytes 1179680 | tf_op jit(solution)/shard_map/ppermute | solution.py:59
  41.7 1.2 copy-done.7
  43.0 20.6 %collective-permute-done.4.refs_3_ = bf16[2,384,768]{2,1,0:T(8,128)(2,1)} collective-permute-done((bf16[2,384,768]{2,1,0:T(8,128)(2,1)}, bf16[2,384,768]{2,1,0:T(8,128)(2,1)}, u32[]{:S(2)}, u32[]{:S(2)}) %collective-permute-start.4) | collective-permute-done | bytes 1179680 | tf_op jit(solution)/shard_map/ppermute | solution.py:59
  63.6 11.7 %collective-permute-done.5.refs_4_.refs_3_ = bf16[384,768]{1,0:T(8,128)(2,1)S(1)} collective-permute-done((bf16[384,768]{1,0:T(8,128)(2,1)}, bf16[384,768]{1,0:T(8,128)(2,1)S(1)}, u32[]{:S(2)}, u32[]{:S(2)}) %collective-permute-start.5) | collective-permute-done | bytes 589856 | tf_op jit(solution)/shard_map/ppermute | solution.py:59
  76.1 1.2 collective-permute-start.9
  79.0 9.8 %collective-permute-done.8.refs_2_.refs_10_.refs_6_ = bf16[2,384,768]{2,1,0:T(8,128)(2,1)} collective-permute-done((bf16[2,384,768]{2,1,0:T(8,128)(2,1)}, bf16[2,384,768]{2,1,0:T(8,128)(2,1)}, u32[]{:S(2)}, u32[]{:S(2)}) %collective-permute-start.8) | collective-permute-done | bytes 1179680 | tf_op jit(solution)/shard_map/ppermute | solution.py:59
  89.1 38.3 %collective-permute-done.10.refs_5_.refs_2_ = bf16[384,768]{1,0:T(8,128)(2,1)} collective-permute-done((bf16[384,768]{1,0:T(8,128)(2,1)}, bf16[384,768]{1,0:T(8,128)(2,1)}, u32[]{:S(2)}, u32[]{:S(2)}) %collective-permute-start.10) | collective-permute-done | bytes 589856 | tf_op jit(solution)/shard_map/ppermute | solution.py:59
  130.2 1.2 collective-permute-start.15
  131.5 1.8 collective-permute-done.13.refs_3_
  133.2 1.2 copy-done.37
  136.3 17.4 %forward.1 = (bf16[4,256,768]{2,1,0:T(8,128)(2,1)S(1)}, bf16[4,256,768]{2,1,0:T(8,128)(2,1)S(1)}, bf16[4,256,768]{2,1,0:T(8,128)(2,1)S(1)}) custom-call(s32[2]{0:T(128)S(1)} %pad_add_fusion.1.info_ref.me_ref, bf16[272,3072]{1,0:T(8,128)(2,1)} %get-tuple-element.101.refs_0_, bf16[272,3072]{1,0:T(8,128)(2,1)} %copy-done.36, ...), custom_call_target="tpu_custom_call" | custom-call | flops 9663676416 | bytes 15728640 | tf_op jit(solution)/shard_map/forward/pallas_call | solution.py:190
  158.6 1.4 copy-done.17
  160.0 7.5 %produce.2 = (bf16[2,2,256,768]{3,2,1,0:T(8,128)(2,1)}, bf16[2,2,256,768]{3,2,1,0:T(8,128)(2,1)}) custom-call(s32[1]{0:T(128)} %bitcast.me_ref, s32[2]{0:T(128)S(1)} %pad_add_fusion.3.ids_ref, bf16[4,256,768]{2,1,0:T(8,128)(2,1)S(1)} %copy-done.17, bf16[384,768]{1,0:T(8,128)(2,1)} %get-tuple-element.108.refs_0_.refs_4_, ...), custom_call_target="tpu_custom_call" | custom-call | flops 2415919104 | bytes 4718592 | tf_op jit(solution)/shard_map/produce/pallas_call | solution.py:242
  167.5 1.5 collective-permute-start.19
  169.0 1.3 collective-permute-done.17.refs_2_.refs_3_.refs_11_
  173.4 1.4 copy-done.24
  174.8 3.1 %convert_add_fusion.2 = (f32[2,1,256,768]{3,2,1,0:T(8,128)}, bf16[2,256,768]{2,1,0:T(8,128)(2,1)}) fusion(bf16[2,2,256,768]{3,2,1,0:T(8,128)(2,1)} %copy-done.26, bf16[2,2,256,768]{3,2,1,0:T(8,128)(2,1)S(1)} %copy-done.24), kind=kLoop, calls=%fused_computation.4 | loop fusion | flops 2752512 | bytes 5505024 | tf_op jit(solution)/shard_map/add | solution.py:429
  177.9 7.5 %produce.3 = (bf16[2,2,256,768]{3,2,1,0:T(8,128)(2,1)}, bf16[2,2,256,768]{3,2,1,0:T(8,128)(2,1)}) custom-call(s32[1]{0:T(128)} %bitcast.me_ref, s32[2]{0:T(128)S(1)} %pad_add_fusion.ids_ref, bf16[4,256,768]{2,1,0:T(8,128)(2,1)S(1)} %copy-done.17, bf16[384,768]{1,0:T(8,128)(2,1)} %get-tuple-element.125.refs_0_.refs_6_, bf16[384,768]{1,0:T(8,128)(2,1)} %copy-done.42, ...), custom_call_target="tpu_custom_call" | custom-call | flops 2415919104 | bytes 4718592 | tf_op jit(solution)/shard_map/produce/pallas_call | solution.py:242
  187.3 1.8 collective-permute-done.20.refs_1_
  190.3 3.2 %convert_add_fusion.3 = (f32[2,1,256,768]{3,2,1,0:T(8,128)}, bf16[2,256,768]{2,1,0:T(8,128)(2,1)}) fusion(bf16[2,2,256,768]{3,2,1,0:T(8,128)(2,1)} %copy-done.27, bf16[2,2,256,768]{3,2,1,0:T(8,128)(2,1)S(1)} %copy-done.25), kind=kLoop, calls=%fused_computation.6 | loop fusion | flops 2752512 | bytes 5505024 | tf_op jit(solution)/shard_map/add | solution.py:429
  194.6 1.4 copy-done.14
  196.0 11.7 %grow.1 = (bf16[4,256,768]{2,1,0:T(8,128)(2,1)S(1)}, bf16[4,256,768]{2,1,0:T(8,128)(2,1)S(1)}) custom-call(s32[2]{0:T(128)S(1)} %pad_add_fusion.1.info_ref.me_ref, bf16[4,256,768]{2,1,0:T(8,128)(2,1)S(1)} %copy-done.14, bf16[4,256,768]{2,1,0:T(8,128)(2,1)} %copy-done.15, bf16[256,3072]{1,0:T(8,128)(2,1)} %get-tuple-element.138.refs_0_, ...), custom_call_target="tpu_custom_call" | custom-call | flops 4831838208 | bytes 11010048 | tf_op jit(solution)/shard_map/grow/pallas_call | solution.py:190
  208.9 1.4 copy-done.12
  210.3 9.1 %back.2 = (bf16[2,2,256,768]{3,2,1,0:T(8,128)(2,1)}, bf16[2,2,256,768]{3,2,1,0:T(8,128)(2,1)}) custom-call(s32[1]{0:T(128)} %bitcast.me_ref, s32[2]{0:T(128)S(1)} %get-tuple-element.184.ids_ref, bf16[4,256,768]{2,1,0:T(8,128)(2,1)S(1)} %copy-done.12, bf16[4,256,768]{2,1,0:T(8,128)(2,1)S(1)} %get-tuple-element.141.up_ref, ...), custom_call_target="tpu_custom_call" | custom-call | flops 4831838208 | bytes 7864320 | tf_op jit(solution)/shard_map/back/pallas_call | solution.py:293
  219.4 2.7 collective-permute-done.22.refs_3_
  222.1 1.2 collective-permute-start.27
  223.3 3.4 %select_bitcast_fusion = (bf16[256,768]{1,0:T(8,128)(2,1)}, bf16[1,256,768]{2,1,0:T(8,128)(2,1)S(1)}, bf16[1,256,768]{2,1,0:T(8,128)(2,1)S(1)}, bf16[1,256,768]{2,1,0:T(8,128)(2,1)S(1)}, bf16[1,256,768]{2,1,0:T(8,128)(2,1)S(1)}) fusion(pred[]{:T(512)S(6)} %eq.80, pred[]{:T(512)S(6)} %eq.81, pred[]{:T(512)S(6)} %eq.82, ...), kind=kLoop, calls=%fused_computation.47 | loop fusion | flops 2949120 | bytes 6684675 | tf_op jit(solution)/shard_map/jit(_where)/select_n | solution.py:476
  227.9 1.3 collective-permute-start.25
  229.2 3.6 %convert_add_fusion.1 = (f32[2,1,256,768]{3,2,1,0:T(8,128)}, bf16[2,256,768]{2,1,0:T(8,128)(2,1)}) fusion(bf16[2,2,256,768]{3,2,1,0:T(8,128)(2,1)} %collective-permute-done.27.refs_1_, bf16[2,2,256,768]{3,2,1,0:T(8,128)(2,1)} %get-tuple-element.150), kind=kLoop, calls=%fused_computation.1 | loop fusion | flops 2752512 | bytes 5505024 | tf_op jit(solution)/shard_map/add | solution.py:429
  233.9 9.1 %back.3 = (bf16[2,2,256,768]{3,2,1,0:T(8,128)(2,1)}, bf16[2,2,256,768]{3,2,1,0:T(8,128)(2,1)}) custom-call(s32[1]{0:T(128)} %bitcast.me_ref, s32[2]{0:T(128)S(1)} %get-tuple-element.183.ids_ref, bf16[4,256,768]{2,1,0:T(8,128)(2,1)S(1)} %copy-done.12, bf16[4,256,768]{2,1,0:T(8,128)(2,1)S(1)} %get-tuple-element.141.up_ref, ...), custom_call_target="tpu_custom_call" | custom-call | flops 4831838208 | bytes 7864320 | tf_op jit(solution)/shard_map/back/pallas_call | solution.py:293
  243.0 6.3 %collective-permute-done.25.refs_2_ = bf16[256,768]{1,0:T(8,128)(2,1)} collective-permute-done((bf16[256,768]{1,0:T(8,128)(2,1)}, bf16[256,768]{1,0:T(8,128)(2,1)}, u32[]{:S(2)}, u32[]{:S(2)}) %collective-permute-start.25) | collective-permute-done | bytes 393248 | tf_op jit(solution)/shard_map/ppermute | solution.py:361
  251.6 2.2 fusion.27
  253.8 1.4 copy-done.23
  255.2 2.6 fusion.3
  259.0 8.7 %collective-permute-done.24.refs_2_ = bf16[256,768]{1,0:T(8,128)(2,1)} collective-permute-done((bf16[256,768]{1,0:T(8,128)(2,1)S(1)}, bf16[256,768]{1,0:T(8,128)(2,1)}, u32[]{:S(2)}, u32[]{:S(2)}) %collective-permute-start.24) | collective-permute-done | bytes 393248 | tf_op jit(solution)/shard_map/ppermute | solution.py:361
  268.7 3.2 %collective-permute-start.30 = (bf16[256,768]{1,0:T(8,128)(2,1)S(1)}, bf16[256,768]{1,0:T(8,128)(2,1)}, u32[]{:S(2)}, u32[]{:S(2)}) collective-permute-start(bf16[256,768]{1,0:T(8,128)(2,1)S(1)} %copy-done.30), channel_id=1, source_target_pairs={{0,2},{1,3},{2,0},{3,1},{4,6},{5,7},{6,4},{7,5},{8,10},{9,11},{10,... | collective-permute-start | bytes 1179656 | tf_op jit(solution)/shard_map/ppermute | solution.py:361
  271.9 3.9 %collective-permute-done.32 = bf16[2,256,768]{2,1,0:T(8,128)(2,1)S(1)} collective-permute-done((bf16[2,256,768]{2,1,0:T(8,128)(2,1)}, bf16[2,256,768]{2,1,0:T(8,128)(2,1)S(1)}, u32[]{:S(2)}, u32[]{:S(2)}) %collective-permute-start.32) | collective-permute-done | bytes 786464 | tf_op jit(solution)/shard_map/ppermute | solution.py:59
  276.8 2.7 collective-permute-start.33
  279.5 3.2 %fusion.20 = bf16[256,768]{1,0:T(8,128)(2,1)} fusion(bf16[256,768]{1,0:T(8,128)(2,1)} %copy-done.32, bf16[256,768]{1,0:T(8,128)(2,1)} %collective-permute-done.25.refs_2_, bf16[256,768]{1,0:T(8,128)(2,1)} %collective-permute-done.24.refs_2_, f32[2,1,256,768]{3,2,1,0:T(8,128)S(1)} %copy-done.19, f32[2,1,256,768]{3,2,1,0:T(8,128)S(1)} %copy-done.18, ...), kind=kLoop, calls=%fused_computation.37 | loop fusion | flops 3538944 | bytes 6291459 | tf_op jit(solution)/shard_map/convert_element_type | solution.py:507
  282.7 17.4 %collective-permute-done.30 = bf16[256,768]{1,0:T(8,128)(2,1)} collective-permute-done((bf16[256,768]{1,0:T(8,128)(2,1)S(1)}, bf16[256,768]{1,0:T(8,128)(2,1)}, u32[]{:S(2)}, u32[]{:S(2)}) %collective-permute-start.30) | collective-permute-done | bytes 393248 | tf_op jit(solution)/shard_map/ppermute | solution.py:361
  300.1 6.8 %collective-permute-done.33 = bf16[256,768]{1,0:T(8,128)(2,1)} collective-permute-done((bf16[256,768]{1,0:T(8,128)(2,1)}, bf16[256,768]{1,0:T(8,128)(2,1)}, u32[]{:S(2)}, u32[]{:S(2)}) %collective-permute-start.33) | collective-permute-done | bytes 393248 | tf_op jit(solution)/shard_map/ppermute | solution.py:361
  306.8 2.2 fusion.7
  (176 shorter events, 39.3 us)
Async XLA Ops:
  0.6 18.1 %copy-start = (s32[4]{0:T(128)S(1)}, s32[4]{0:T(128)}, u32[]{:S(2)}) copy-start(s32[4]{0:T(128)} %param.16) | copy-start | bytes 52
  0.8 2.3 copy-start.2
  8.8 8.2 %collective-permute-start = (bf16[2,384,768]{2,1,0:T(8,128)(2,1)}, bf16[2,384,768]{2,1,0:T(8,128)(2,1)S(1)}, u32[]{:S(2)}, u32[]{:S(2)}) collective-permute-start(bf16[2,384,768]{2,1,0:T(8,128)(2,1)} %get-tuple-element.90), channel_id=1, source_target_pairs={{0,4},{4,0},{8,12},{12,8},{16,20},{20,16},{24,28},{28,24},{1,5},{5... | collective-permute-start | bytes 3538952 | tf_op jit(solution)/shard_map/ppermute | solution.py:59
  9.5 27.8 %collective-permute-start.1 = (bf16[2,384,768]{2,1,0:T(8,128)(2,1)}, bf16[2,384,768]{2,1,0:T(8,128)(2,1)}, u32[]{:S(2)}, u32[]{:S(2)}) collective-permute-start(bf16[2,384,768]{2,1,0:T(8,128)(2,1)} %get-tuple-element.93), channel_id=1, source_target_pairs={{0,16},{4,20},{8,24},{12,28},{16,0},{20,4},{24,8},{28,12},{1,17},{... | collective-permute-start | bytes 3538952 | tf_op jit(solution)/shard_map/ppermute | solution.py:59
  10.8 27.5 %collective-permute-start.3 = (bf16[2,384,768]{2,1,0:T(8,128)(2,1)}, bf16[2,384,768]{2,1,0:T(8,128)(2,1)S(1)}, u32[]{:S(2)}, u32[]{:S(2)}) collective-permute-start(bf16[2,384,768]{2,1,0:T(8,128)(2,1)} %get-tuple-element.95.refs_1_), channel_id=1, source_target_pairs={{0,8},{4,12},{8,0},{12,4},{16,24},{20,28},{24,16},{28,20},{1,9},{5... | collective-permute-start | bytes 3538952 | tf_op jit(solution)/shard_map/ppermute | solution.py:59
  11.0 2.3 copy-start.3
  18.1 2.6 copy-start.46
  18.1 2.9 copy-start.5
  18.1 20.2 %collective-permute-start.2 = (bf16[384,768]{1,0:T(8,128)(2,1)}, bf16[384,768]{1,0:T(8,128)(2,1)S(1)}, u32[]{:S(2)}, u32[]{:S(2)}) collective-permute-start(bf16[384,768]{1,0:T(8,128)(2,1)} %get-tuple-element.94), channel_id=1, source_target_pairs={{0,4},{4,0},{8,12},{12,8},{16,20},{20,16},{24,28},{28,24},{1,5},{5... | collective-permute-start | bytes 1769480 | tf_op jit(solution)/shard_map/ppermute | solution.py:59
  18.8 44.7 %collective-permute-start.4 = (bf16[2,384,768]{2,1,0:T(8,128)(2,1)}, bf16[2,384,768]{2,1,0:T(8,128)(2,1)}, u32[]{:S(2)}, u32[]{:S(2)}) collective-permute-start(bf16[2,384,768]{2,1,0:T(8,128)(2,1)} %get-tuple-element.98), channel_id=1, source_target_pairs={{0,20},{4,16},{8,28},{12,24},{16,4},{20,0},{24,12},{28,8},{1,21},{... | collective-permute-start | bytes 3538952 | tf_op jit(solution)/shard_map/ppermute | solution.py:59
  19.5 55.8 %collective-permute-start.6 = (bf16[2,384,768]{2,1,0:T(8,128)(2,1)}, bf16[2,384,768]{2,1,0:T(8,128)(2,1)}, u32[]{:S(2)}, u32[]{:S(2)}) collective-permute-start(bf16[2,384,768]{2,1,0:T(8,128)(2,1)} %get-tuple-element.100.refs_5_.refs_1_), channel_id=1, source_target_pairs={{0,8},{4,12},{8,0},{12,4},{16,24},{20,28},{24,16},{28,20},{1,9},{5... | collective-permute-start | bytes 3538952 | tf_op jit(solution)/shard_map/ppermute | solution.py:59
  39.5 35.7 %collective-permute-start.5 = (bf16[384,768]{1,0:T(8,128)(2,1)}, bf16[384,768]{1,0:T(8,128)(2,1)S(1)}, u32[]{:S(2)}, u32[]{:S(2)}) collective-permute-start(bf16[384,768]{1,0:T(8,128)(2,1)} %get-tuple-element.99), channel_id=1, source_target_pairs={{0,16},{4,20},{8,24},{12,28},{16,0},{20,4},{24,8},{28,12},{1,17},{... | collective-permute-start | bytes 1769480 | tf_op jit(solution)/shard_map/ppermute | solution.py:59
  39.9 49.0 %collective-permute-start.8 = (bf16[2,384,768]{2,1,0:T(8,128)(2,1)}, bf16[2,384,768]{2,1,0:T(8,128)(2,1)}, u32[]{:S(2)}, u32[]{:S(2)}) collective-permute-start(bf16[2,384,768]{2,1,0:T(8,128)(2,1)} %get-tuple-element.104.refs_8_.refs_4_), channel_id=1, source_target_pairs={{0,8},{4,12},{8,0},{12,4},{16,24},{20,28},{24,16},{28,20},{1,9},{5... | collective-permute-start | bytes 3538952 | tf_op jit(solution)/shard_map/ppermute | solution.py:59
  76.1 51.3 %collective-permute-start.9 = (bf16[272,3072]{1,0:T(8,128)(2,1)}, bf16[272,3072]{1,0:T(8,128)(2,1)S(1)}, u32[]{:S(2)}, u32[]{:S(2)}) collective-permute-start(bf16[272,3072]{1,0:T(8,128)(2,1)} %get-tuple-element.101.refs_0_), channel_id=1, source_target_pairs={{0,16},{4,20},{8,24},{12,28},{16,0},{20,4},{24,8},{28,12},{1,17},{... | collective-permute-start | bytes 5013512 | tf_op jit(solution)/shard_map/ppermute | solution.py:59
  77.4 50.1 %collective-permute-start.7 = (bf16[272,3072]{1,0:T(8,128)(2,1)}, bf16[272,3072]{1,0:T(8,128)(2,1)S(1)}, u32[]{:S(2)}, u32[]{:S(2)}) collective-permute-start(bf16[272,3072]{1,0:T(8,128)(2,1)} %get-tuple-element.101.refs_0_), channel_id=1, source_target_pairs={{0,4},{4,0},{8,12},{12,8},{16,20},{20,16},{24,28},{28,24},{1,5},{5... | collective-permute-start | bytes 5013512 | tf_op jit(solution)/shard_map/ppermute | solution.py:59
  78.4 49.1 %collective-permute-start.11 = (bf16[2,384,768]{2,1,0:T(8,128)(2,1)}, bf16[2,384,768]{2,1,0:T(8,128)(2,1)}, u32[]{:S(2)}, u32[]{:S(2)}) collective-permute-start(bf16[2,384,768]{2,1,0:T(8,128)(2,1)} %get-tuple-element.107.refs_9_.refs_5_), channel_id=1, source_target_pairs={{0,8},{4,12},{8,0},{12,4},{16,24},{20,28},{24,16},{28,20},{1,9},{5... | collective-permute-start | bytes 3538952 | tf_op jit(solution)/shard_map/ppermute | solution.py:59
  78.6 48.8 %collective-permute-start.10 = (bf16[384,768]{1,0:T(8,128)(2,1)}, bf16[384,768]{1,0:T(8,128)(2,1)}, u32[]{:S(2)}, u32[]{:S(2)}) collective-permute-start(bf16[384,768]{1,0:T(8,128)(2,1)} %get-tuple-element.106), channel_id=1, source_target_pairs={{0,20},{4,16},{8,28},{12,24},{16,4},{20,0},{24,12},{28,8},{1,21},{... | collective-permute-start | bytes 1769480 | tf_op jit(solution)/shard_map/ppermute | solution.py:59
  88.8 38.6 %collective-permute-start.12 = (bf16[384,768]{1,0:T(8,128)(2,1)}, bf16[384,768]{1,0:T(8,128)(2,1)S(1)}, u32[]{:S(2)}, u32[]{:S(2)}) collective-permute-start(bf16[384,768]{1,0:T(8,128)(2,1)} %get-tuple-element.108.refs_0_.refs_4_), channel_id=1, source_target_pairs={{0,8},{4,12},{8,0},{12,4},{16,24},{20,28},{24,16},{28,20},{1,9},{5... | collective-permute-start | bytes 1769480 | tf_op jit(solution)/shard_map/ppermute | solution.py:59
  129.5 3.8 %collective-permute-start.13 = (bf16[272,3072]{1,0:T(8,128)(2,1)}, bf16[272,3072]{1,0:T(8,128)(2,1)S(1)}, u32[]{:S(2)}, u32[]{:S(2)}) collective-permute-start(bf16[272,3072]{1,0:T(8,128)(2,1)} %get-tuple-element.109.refs_2_), channel_id=1, source_target_pairs={{0,4},{4,0},{8,12},{12,8},{16,20},{20,16},{24,28},{28,24},{1,5},{5... | collective-permute-start | bytes 5013512 | tf_op jit(solution)/shard_map/ppermute | solution.py:59
  130.0 27.2 %collective-permute-start.14 = (bf16[384,768]{1,0:T(8,128)(2,1)}, bf16[384,768]{1,0:T(8,128)(2,1)S(1)}, u32[]{:S(2)}, u32[]{:S(2)}) collective-permute-start(bf16[384,768]{1,0:T(8,128)(2,1)} %get-tuple-element.115.refs_1_.refs_5_), channel_id=1, source_target_pairs={{0,8},{4,12},{8,0},{12,4},{16,24},{20,28},{24,16},{28,20},{1,9},{5... | collective-permute-start | bytes 1769480 | tf_op jit(solution)/shard_map/ppermute | solution.py:59
  130.2 27.5 %collective-permute-start.15 = (bf16[384,768]{1,0:T(8,128)(2,1)}, bf16[384,768]{1,0:T(8,128)(2,1)S(1)}, u32[]{:S(2)}, u32[]{:S(2)}) collective-permute-start(bf16[384,768]{1,0:T(8,128)(2,1)} %get-tuple-element.116.refs_2_.refs_8_), channel_id=1, source_target_pairs={{0,8},{4,12},{8,0},{12,4},{16,24},{20,28},{24,16},{28,20},{1,9},{5... | collective-permute-start | bytes 1769480 | tf_op jit(solution)/shard_map/ppermute | solution.py:59
  134.5 35.9 %collective-permute-start.16 = (bf16[256,3072]{1,0:T(8,128)(2,1)}, bf16[256,3072]{1,0:T(8,128)(2,1)}, u32[]{:S(2)}, u32[]{:S(2)}) collective-permute-start(bf16[256,3072]{1,0:T(8,128)(2,1)} %get-tuple-element.120.refs_1_), channel_id=1, source_target_pairs={{0,16},{4,20},{8,24},{12,28},{16,0},{20,4},{24,8},{28,12},{1,17},{... | collective-permute-start | bytes 4718600 | tf_op jit(solution)/shard_map/ppermute | solution.py:59
  135.6 34.8 %collective-permute-start.18 = (bf16[256,3072]{1,0:T(8,128)(2,1)}, bf16[256,3072]{1,0:T(8,128)(2,1)}, u32[]{:S(2)}, u32[]{:S(2)}) collective-permute-start(bf16[256,3072]{1,0:T(8,128)(2,1)} %get-tuple-element.120.refs_1_), channel_id=1, source_target_pairs={{0,4},{4,0},{8,12},{12,8},{16,20},{20,16},{24,28},{28,24},{1,5},{5... | collective-permute-start | bytes 4718600 | tf_op jit(solution)/shard_map/ppermute | solution.py:59
  136.0 34.4 %collective-permute-start.17 = (bf16[384,768]{1,0:T(8,128)(2,1)}, bf16[384,768]{1,0:T(8,128)(2,1)}, u32[]{:S(2)}, u32[]{:S(2)}) collective-permute-start(bf16[384,768]{1,0:T(8,128)(2,1)} %get-tuple-element.117.refs_3_.refs_9_), channel_id=1, source_target_pairs={{0,8},{4,12},{8,0},{12,4},{16,24},{20,28},{24,16},{28,20},{1,9},{5... | collective-permute-start | bytes 1769480 | tf_op jit(solution)/shard_map/ppermute | solution.py:59
  167.5 4.7 %collective-permute-start.19 = (bf16[2,2,256,768]{3,2,1,0:T(8,128)(2,1)}, bf16[2,2,256,768]{3,2,1,0:T(8,128)(2,1)S(1)}, u32[]{:S(2)}, u32[]{:S(2)}) collective-permute-start(bf16[2,2,256,768]{3,2,1,0:T(8,128)(2,1)} %get-tuple-element.122), channel_id=1, source_target_pairs={{0,4},{4,0},{8,12},{12,8},{16,20},{20,16},{24,28},{28,24},{1,5},{5... | collective-permute-start | bytes 4718600 | tf_op jit(solution)/shard_map/ppermute | solution.py:59
  170.4 16.9 %collective-permute-start.21 = (bf16[256,3072]{1,0:T(8,128)(2,1)}, bf16[256,3072]{1,0:T(8,128)(2,1)}, u32[]{:S(2)}, u32[]{:S(2)}) collective-permute-start(bf16[256,3072]{1,0:T(8,128)(2,1)} %get-tuple-element.131.refs_2_), channel_id=1, source_target_pairs={{0,4},{4,0},{8,12},{12,8},{16,20},{20,16},{24,28},{28,24},{1,5},{5... | collective-permute-start | bytes 4718600 | tf_op jit(solution)/shard_map/ppermute | solution.py:59
  185.4 3.7 %collective-permute-start.20 = (bf16[2,2,256,768]{3,2,1,0:T(8,128)(2,1)}, bf16[2,2,256,768]{3,2,1,0:T(8,128)(2,1)S(1)}, u32[]{:S(2)}, u32[]{:S(2)}) collective-permute-start(bf16[2,2,256,768]{3,2,1,0:T(8,128)(2,1)} %get-tuple-element.129), channel_id=1, source_target_pairs={{0,4},{4,0},{8,12},{12,8},{16,20},{20,16},{24,28},{28,24},{1,5},{5... | collective-permute-start | bytes 4718600 | tf_op jit(solution)/shard_map/ppermute | solution.py:59
  186.1 33.3 %collective-permute-start.23 = (bf16[2,256,768]{2,1,0:T(8,128)(2,1)}, bf16[2,256,768]{2,1,0:T(8,128)(2,1)}, u32[]{:S(2)}, u32[]{:S(2)}) collective-permute-start(bf16[2,256,768]{2,1,0:T(8,128)(2,1)} %get-tuple-element.133), channel_id=1, source_target_pairs={{0,16},{4,20},{8,24},{12,28},{16,0},{20,4},{24,8},{28,12},{1,17},{... | collective-permute-start | bytes 2359304 | tf_op jit(solution)/shard_map/ppermute | solution.py:59
  187.3 3.0 copy-start.25
  193.5 28.6 %collective-permute-start.22 = (bf16[2,256,768]{2,1,0:T(8,128)(2,1)}, bf16[2,256,768]{2,1,0:T(8,128)(2,1)}, u32[]{:S(2)}, u32[]{:S(2)}) collective-permute-start(bf16[2,256,768]{2,1,0:T(8,128)(2,1)} %get-tuple-element.132), channel_id=1, source_target_pairs={{0,16},{4,20},{8,24},{12,28},{16,0},{20,4},{24,8},{28,12},{1,17},{... | collective-permute-start | bytes 2359304 | tf_op jit(solution)/shard_map/ppermute | solution.py:59
  222.1 7.1 %collective-permute-start.27 = (bf16[2,2,256,768]{3,2,1,0:T(8,128)(2,1)}, bf16[2,2,256,768]{3,2,1,0:T(8,128)(2,1)}, u32[]{:S(2)}, u32[]{:S(2)}) collective-permute-start(bf16[2,2,256,768]{3,2,1,0:T(8,128)(2,1)} %get-tuple-element.149), channel_id=1, source_target_pairs={{0,4},{4,0},{8,12},{12,8},{16,20},{20,16},{24,28},{28,24},{1,5},{5... | collective-permute-start | bytes 4718600 | tf_op jit(solution)/shard_map/ppermute | solution.py:59
  227.7 15.3 %collective-permute-start.26 = (bf16[256,768]{1,0:T(8,128)(2,1)}, bf16[256,768]{1,0:T(8,128)(2,1)S(1)}, u32[]{:S(2)}, u32[]{:S(2)}) collective-permute-start(bf16[256,768]{1,0:T(8,128)(2,1)} %get-tuple-element.147), channel_id=1, source_target_pairs={{0,3},{1,0},{2,1},{3,2},{4,7},{5,4},{6,5},{7,6},{8,11},{9,8},{10,9... | collective-permute-start | bytes 1179656 | tf_op jit(solution)/shard_map/ppermute | solution.py:361
  227.9 21.4 %collective-permute-start.25 = (bf16[256,768]{1,0:T(8,128)(2,1)}, bf16[256,768]{1,0:T(8,128)(2,1)}, u32[]{:S(2)}, u32[]{:S(2)}) collective-permute-start(bf16[256,768]{1,0:T(8,128)(2,1)} %get-tuple-element.146), channel_id=1, source_target_pairs={{0,1},{1,2},{2,3},{3,0},{4,5},{5,6},{6,7},{7,4},{8,9},{9,10},{10,1... | collective-permute-start | bytes 1179656 | tf_op jit(solution)/shard_map/ppermute | solution.py:361
  232.8 18.9 %collective-permute-start.28 = (bf16[2,256,768]{2,1,0:T(8,128)(2,1)}, bf16[2,256,768]{2,1,0:T(8,128)(2,1)}, u32[]{:S(2)}, u32[]{:S(2)}) collective-permute-start(bf16[2,256,768]{2,1,0:T(8,128)(2,1)} %get-tuple-element.156), channel_id=1, source_target_pairs={{0,16},{4,20},{8,24},{12,28},{16,0},{20,4},{24,8},{28,12},{1,17},{... | collective-permute-start | bytes 2359304 | tf_op jit(solution)/shard_map/ppermute | solution.py:59
  243.0 6.3 %copy-start.32 = (bf16[256,768]{1,0:T(8,128)(2,1)}, bf16[256,768]{1,0:T(8,128)(2,1)S(1)}, u32[]{:S(2)}) copy-start(bf16[256,768]{1,0:T(8,128)(2,1)S(1)} %collective-permute-done.26.refs_3_) | copy-start | bytes 1179652
  249.3 2.3 copy-start.20
  249.3 4.6 %collective-permute-start.29 = (bf16[2,2,256,768]{3,2,1,0:T(8,128)(2,1)}, bf16[2,2,256,768]{3,2,1,0:T(8,128)(2,1)}, u32[]{:S(2)}, u32[]{:S(2)}) collective-permute-start(bf16[2,2,256,768]{3,2,1,0:T(8,128)(2,1)} %get-tuple-element.157), channel_id=1, source_target_pairs={{0,4},{4,0},{8,12},{12,8},{16,20},{20,16},{24,28},{28,24},{1,5},{5... | collective-permute-start | bytes 4718600 | tf_op jit(solution)/shard_map/ppermute | solution.py:59
  250.3 17.4 %collective-permute-start.24 = (bf16[256,768]{1,0:T(8,128)(2,1)S(1)}, bf16[256,768]{1,0:T(8,128)(2,1)}, u32[]{:S(2)}, u32[]{:S(2)}) collective-permute-start(bf16[256,768]{1,0:T(8,128)(2,1)S(1)} %copy-done.31), channel_id=1, source_target_pairs={{0,2},{1,3},{2,0},{3,1},{4,6},{5,7},{6,4},{7,5},{8,10},{9,11},{10,... | collective-permute-start | bytes 1179656 | tf_op jit(solution)/shard_map/ppermute | solution.py:361
  257.8 17.9 %copy-start.21 = (f32[2,1,256,768]{3,2,1,0:T(8,128)}, f32[2,1,256,768]{3,2,1,0:T(8,128)S(1)}, u32[]{:S(2)}) copy-start(f32[2,1,256,768]{3,2,1,0:T(8,128)S(1)} %get-tuple-element.174) | copy-start | bytes 4718596
  257.9 17.9 %collective-permute-start.32 = (bf16[2,256,768]{2,1,0:T(8,128)(2,1)}, bf16[2,256,768]{2,1,0:T(8,128)(2,1)S(1)}, u32[]{:S(2)}, u32[]{:S(2)}) collective-permute-start(bf16[2,256,768]{2,1,0:T(8,128)(2,1)} %get-tuple-element.164), channel_id=1, source_target_pairs={{0,16},{4,20},{8,24},{12,28},{16,0},{20,4},{24,8},{28,12},{1,17},{... | collective-permute-start | bytes 2359304 | tf_op jit(solution)/shard_map/ppermute | solution.py:59
  267.7 15.0 %collective-permute-start.31 = (bf16[256,768]{1,0:T(8,128)(2,1)}, bf16[256,768]{1,0:T(8,128)(2,1)}, u32[]{:S(2)}, u32[]{:S(2)}) collective-permute-start(bf16[256,768]{1,0:T(8,128)(2,1)} %get-tuple-element.162), channel_id=1, source_target_pairs={{0,1},{1,2},{2,3},{3,0},{4,5},{5,6},{6,7},{7,4},{8,9},{9,10},{10,1... | collective-permute-start | bytes 1179656 | tf_op jit(solution)/shard_map/ppermute | solution.py:361
  268.7 31.4 %collective-permute-start.30 = (bf16[256,768]{1,0:T(8,128)(2,1)S(1)}, bf16[256,768]{1,0:T(8,128)(2,1)}, u32[]{:S(2)}, u32[]{:S(2)}) collective-permute-start(bf16[256,768]{1,0:T(8,128)(2,1)S(1)} %copy-done.30), channel_id=1, source_target_pairs={{0,2},{1,3},{2,0},{3,1},{4,6},{5,7},{6,4},{7,5},{8,10},{9,11},{10,... | collective-permute-start | bytes 1179656 | tf_op jit(solution)/shard_map/ppermute | solution.py:361
  276.8 2.7 copy-start.18
  276.8 2.7 copy-start.19
  276.8 30.0 %collective-permute-start.33 = (bf16[256,768]{1,0:T(8,128)(2,1)}, bf16[256,768]{1,0:T(8,128)(2,1)}, u32[]{:S(2)}, u32[]{:S(2)}) collective-permute-start(bf16[256,768]{1,0:T(8,128)(2,1)} %get-tuple-element.165), channel_id=1, source_target_pairs={{0,3},{1,0},{2,1},{3,2},{4,7},{5,4},{6,5},{7,6},{8,11},{9,8},{10,9... | collective-permute-start | bytes 1179656 | tf_op jit(solution)/shard_map/ppermute | solution.py:361
  279.5 27.3 %copy-start.22 = (f32[2,1,256,768]{3,2,1,0:T(8,128)S(1)}, f32[2,1,256,768]{3,2,1,0:T(8,128)}, u32[]{:S(2)}) copy-start(f32[2,1,256,768]{3,2,1,0:T(8,128)} %copy-done.21) | copy-start | bytes 4718596
  279.5 27.3 %copy-start.29 = (bf16[2,256,768]{2,1,0:T(8,128)(2,1)S(1)}, bf16[2,256,768]{2,1,0:T(8,128)(2,1)}, u32[]{:S(2)}) copy-start(bf16[2,256,768]{2,1,0:T(8,128)(2,1)} %copy-done.28) | copy-start | bytes 2359300
  279.5 29.6 %copy-start.1 = (s32[4]{0:T(128)S(1)}, s32[4]{0:T(128)}, u32[]{:S(2)}) copy-start(s32[4]{0:T(128)} %param.16) | copy-start | bytes 52
  (33 other events, 35.6 us)

commit v6 on v5

--- a/solution.py
+++ b/solution.py
@@ -459,7 +459,7 @@
     u_parts = hold([have[name] for name in ("u", "u near", "u far", "u far near")])
     d_pre, d_up = grow(info, count, u_parts, [have["turned", key] for key in range(n)], factors)
     steps = jnp.array([order[: m // 2], order[m // 2 :]], jnp.int32)
-    blocks = hold(blocks, d_pre)
+    blocks = hold(blocks)
     keep_0, send_0 = back(here, lax.rem(z + steps[0], m), m, d_pre, d_up, blocks)
     (send_0,) = clock.tick([send_0], [far_a, got] if halves else [got])
     near_0 = swap(send_0, 1, n)

time: 310 us -> 333 us (1.074)
  waiting for transfers between devices: 149 us -> 180 us
  local copies, waits for them, and re-layouts: 32.8 us -> 27 us
    ppermute x28, waiting for transfers between devices: 110 us -> 139 us  [swap(): return lax.ppermute(value, 'dp', [(i, i ^ mask) for i in range(size)])]
    unnamed x94 -> x102, local copies, waits for them, and re-layouts: 32.7 us -> 26.9 us
  transfers between devices with their start and end apart: 34 -> 34, of which waited for: 18 -> 16; matrix products, arithmetic and copies ran while one was open for 8% -> 7% of each run, Pallas kernels for 21% -> 18%
where the time goes in v6:
time: 333 us; the launch traced here: 332 us
  waiting for transfers between devices  180 us (54%)
  Pallas kernels  72.1 us (22%)
  starting transfers between devices  27.6 us (8%)
  local copies, waits for them, and re-layouts  27 us (8%)
  other arithmetic  24.8 us (7%)
    ppermute x28, waiting for transfers between devices, swap(): return lax.ppermute(value, 'dp', [(i, i ^ mask) for i in range(size)])  139 us
    ppermute x6, waiting for transfers between devices, shift(): return lax.ppermute(value, 'etp', [(i, (i + step) % m) for i in range(m)])  40.8 us
    pallas_call x2, Pallas kernels, on_tokens(): pl.pallas_call(functools.partial(kernel, n), grid_spec=pltpu.PrefetchScal...  29.1 us
    unnamed x102, local copies, waits for them, and re-layouts  26.9 us
    ppermute x28, starting transfers between devices, swap(): return lax.ppermute(value, 'dp', [(i, i ^ mask) for i in range(size)])  21.3 us
    pallas_call x2, Pallas kernels, back(): pl.pallas_call(functools.partial(back_kernel, n), grid_spec=pltpu.Prefetc...  18.1 us
    pallas_call x2, Pallas kernels, produce(): pl.pallas_call(functools.partial(produce_kernel, keys), grid_spec=pltpu.P...  15.8 us
    add x3, other arithmetic, add(): wide(keep[:, 0]) + wide(near[:, 0])  9.39 us
  transfers between devices with their start and end apart: 34, of which 16 were waited for; matrix products, arithmetic and copies ran while one was open for 7% of the time, Pallas kernels for 18%

profile of v6, /device:TPU:11, one launch (start us, length us, event | category | flops | bytes accessed | tf_op | source)
XLA Modules:
  0.0 332.4 jit_solution(1196225540576377254)
XLA Ops:
  0.8 2.3 copy-done.2
  3.1 5.8 %cast_rows.1 = (bf16[2,384,768]{2,1,0:T(8,128)(2,1)}, bf16[2,384,768]{2,1,0:T(8,128)(2,1)}, bf16[2,384,768]{2,1,0:T(8,128)(2,1)}, bf16[2,384,768]{2,1,0:T(8,128)(2,1)}) custom-call(s32[4]{0:T(128)S(1)} %pad_add_fusion.2.pick_ref, f32[2,384,1536]{2,1,0:T(8,128)S(1)} %copy-done.2, f32[2,384,1536]{2,1,0:T(8,128)} %up_ref.1), custom_call_target="tpu_custom_call" | custom-call | tf_op jit(solution)/shard_map/cast_rows/pallas_call | solution.py:81
  9.6 1.2 collective-permute-start.1
  11.1 2.3 copy-done.3
  14.1 2.9 cast_turned.1
  22.9 14.6 %collective-permute-done.1.refs_2_ = bf16[2,384,768]{2,1,0:T(8,128)(2,1)} collective-permute-done((bf16[2,384,768]{2,1,0:T(8,128)(2,1)}, bf16[2,384,768]{2,1,0:T(8,128)(2,1)}, u32[]{:S(2)}, u32[]{:S(2)}) %collective-permute-start.1) | collective-permute-done | bytes 1179680 | tf_op jit(solution)/shard_map/ppermute | solution.py:59
  42.9 32.5 %collective-permute-done.5.refs_4_.refs_3_ = bf16[384,768]{1,0:T(8,128)(2,1)S(1)} collective-permute-done((bf16[384,768]{1,0:T(8,128)(2,1)}, bf16[384,768]{1,0:T(8,128)(2,1)S(1)}, u32[]{:S(2)}, u32[]{:S(2)}) %collective-permute-start.5) | collective-permute-done | bytes 589856 | tf_op jit(solution)/shard_map/ppermute | solution.py:59
  76.9 1.2 collective-permute-start.9
  79.1 9.8 %collective-permute-done.8.refs_2_.refs_10_.refs_6_ = bf16[2,384,768]{2,1,0:T(8,128)(2,1)} collective-permute-done((bf16[2,384,768]{2,1,0:T(8,128)(2,1)}, bf16[2,384,768]{2,1,0:T(8,128)(2,1)}, u32[]{:S(2)}, u32[]{:S(2)}) %collective-permute-start.8) | collective-permute-done | bytes 1179680 | tf_op jit(solution)/shard_map/ppermute | solution.py:59
  89.2 39.0 %collective-permute-done.10.refs_5_.refs_2_ = bf16[384,768]{1,0:T(8,128)(2,1)} collective-permute-done((bf16[384,768]{1,0:T(8,128)(2,1)}, bf16[384,768]{1,0:T(8,128)(2,1)}, u32[]{:S(2)}, u32[]{:S(2)}) %collective-permute-start.10) | collective-permute-done | bytes 589856 | tf_op jit(solution)/shard_map/ppermute | solution.py:59
  132.1 1.8 collective-permute-done.13.refs_3_
  133.9 1.2 copy-done.41
  135.2 17.5 %forward.1 = (bf16[4,256,768]{2,1,0:T(8,128)(2,1)S(1)}, bf16[4,256,768]{2,1,0:T(8,128)(2,1)S(1)}, bf16[4,256,768]{2,1,0:T(8,128)(2,1)S(1)}) custom-call(s32[2]{0:T(128)S(1)} %pad_add_fusion.1.info_ref.me_ref, bf16[272,3072]{1,0:T(8,128)(2,1)} %get-tuple-element.101.refs_0_, bf16[272,3072]{1,0:T(8,128)(2,1)} %copy-done.40, ...), custom_call_target="tpu_custom_call" | custom-call | flops 9663676416 | bytes 15728640 | tf_op jit(solution)/shard_map/forward/pallas_call | solution.py:190
  152.7 8.4 %produce.2 = (bf16[2,2,256,768]{3,2,1,0:T(8,128)(2,1)}, bf16[2,2,256,768]{3,2,1,0:T(8,128)(2,1)}) custom-call(s32[1]{0:T(128)} %bitcast.me_ref, s32[2]{0:T(128)S(1)} %pad_add_fusion.3.ids_ref, bf16[4,256,768]{2,1,0:T(8,128)(2,1)S(1)} %get-tuple-element.113.refs_3_.hidden_ref, bf16[384,768]{1,0:T(8,128)(2,1)} %get-tuple-element.108.refs_0_.refs_4_, ...), custom_call_target="tpu_custom_call" | custom-call | flops 2415919104 | bytes 4718592 | tf_op jit(solution)/shard_map/produce/pallas_call | solution.py:242
  163.5 1.2 collective-permute-start.16
  165.8 3.1 convert_add_fusion.2
  169.0 11.6 %collective-permute-done.17.refs_2_.refs_3_.refs_11_ = bf16[384,768]{1,0:T(8,128)(2,1)} collective-permute-done((bf16[384,768]{1,0:T(8,128)(2,1)}, bf16[384,768]{1,0:T(8,128)(2,1)}, u32[]{:S(2)}, u32[]{:S(2)}) %collective-permute-start.17) | collective-permute-done | bytes 589856 | tf_op jit(solution)/shard_map/ppermute | solution.py:59
  180.6 18.7 %collective-permute-done.16.refs_1_ = bf16[256,3072]{1,0:T(8,128)(2,1)} collective-permute-done((bf16[256,3072]{1,0:T(8,128)(2,1)S(1)}, bf16[256,3072]{1,0:T(8,128)(2,1)}, u32[]{:S(2)}, u32[]{:S(2)}) %collective-permute-start.16) | collective-permute-done | bytes 1572896 | tf_op jit(solution)/shard_map/ppermute | solution.py:59
  199.3 1.4 copy-done.18
  200.7 7.5 %produce.3 = (bf16[2,2,256,768]{3,2,1,0:T(8,128)(2,1)}, bf16[2,2,256,768]{3,2,1,0:T(8,128)(2,1)}) custom-call(s32[1]{0:T(128)} %bitcast.me_ref, s32[2]{0:T(128)S(1)} %pad_add_fusion.ids_ref, bf16[4,256,768]{2,1,0:T(8,128)(2,1)S(1)} %copy-done.18, bf16[384,768]{1,0:T(8,128)(2,1)} %get-tuple-element.125.refs_0_.refs_6_, bf16[384,768]{1,0:T(8,128)(2,1)} %copy-done.46, ...), custom_call_target="tpu_custom_call" | custom-call | flops 2415919104 | bytes 4718592 | tf_op jit(solution)/shard_map/produce/pallas_call | solution.py:242
  209.5 1.3 collective-permute-start.23
  210.8 2.0 collective-permute-done.20.refs_1_
  212.8 3.2 convert_add_fusion.3
  216.0 1.3 collective-permute-start.22
  217.3 1.4 copy-done.15
  218.7 11.7 %grow.1 = (bf16[4,256,768]{2,1,0:T(8,128)(2,1)S(1)}, bf16[4,256,768]{2,1,0:T(8,128)(2,1)S(1)}) custom-call(s32[2]{0:T(128)S(1)} %pad_add_fusion.1.info_ref.me_ref, bf16[4,256,768]{2,1,0:T(8,128)(2,1)S(1)} %copy-done.15, bf16[4,256,768]{2,1,0:T(8,128)(2,1)} %copy-done.16, bf16[256,3072]{1,0:T(8,128)(2,1)} %get-tuple-element.139.refs_0_, ...), custom_call_target="tpu_custom_call" | custom-call | flops 4831838208 | bytes 11010048 | tf_op jit(solution)/shard_map/grow/pallas_call | solution.py:190
  230.4 9.1 %back.2 = (bf16[2,2,256,768]{3,2,1,0:T(8,128)(2,1)}, bf16[2,2,256,768]{3,2,1,0:T(8,128)(2,1)}) custom-call(s32[1]{0:T(128)} %bitcast.me_ref, s32[2]{0:T(128)S(1)} %get-tuple-element.184.ids_ref, bf16[4,256,768]{2,1,0:T(8,128)(2,1)S(1)} %get-tuple-element.140.pre_ref, bf16[4,256,768]{2,1,0:T(8,128)(2,1)S(1)} %get-tuple-element.141.up_ref, ...), custom_call_target="tpu_custom_call" | custom-call | flops 4831838208 | bytes 7864320 | tf_op jit(solution)/shard_map/back/pallas_call | solution.py:293
  239.5 5.1 %collective-permute-done.22.refs_3_ = bf16[2,256,768]{2,1,0:T(8,128)(2,1)S(1)} collective-permute-done((bf16[2,256,768]{2,1,0:T(8,128)(2,1)}, bf16[2,256,768]{2,1,0:T(8,128)(2,1)S(1)}, u32[]{:S(2)}, u32[]{:S(2)}) %collective-permute-start.22) | collective-permute-done | bytes 786464 | tf_op jit(solution)/shard_map/ppermute | solution.py:59
  245.5 1.8 collective-permute-start.27
  247.3 3.0 select_bitcast_fusion
  251.3 1.3 collective-permute-start.25
  252.8 3.1 convert_add_fusion.1
  255.9 1.2 collective-permute-start.28
  257.3 9.0 %back.3 = (bf16[2,2,256,768]{3,2,1,0:T(8,128)(2,1)}, bf16[2,2,256,768]{3,2,1,0:T(8,128)(2,1)}) custom-call(s32[1]{0:T(128)} %bitcast.me_ref, s32[2]{0:T(128)S(1)} %get-tuple-element.183.ids_ref, bf16[4,256,768]{2,1,0:T(8,128)(2,1)S(1)} %get-tuple-element.140.pre_ref, bf16[4,256,768]{2,1,0:T(8,128)(2,1)S(1)} %copy-done.13, ...), custom_call_target="tpu_custom_call" | custom-call | flops 4831838208 | bytes 7864320 | tf_op jit(solution)/shard_map/back/pallas_call | solution.py:293
  266.4 5.6 %collective-permute-done.26.refs_3_ = bf16[256,768]{1,0:T(8,128)(2,1)} collective-permute-done((bf16[256,768]{1,0:T(8,128)(2,1)}, bf16[256,768]{1,0:T(8,128)(2,1)}, u32[]{:S(2)}, u32[]{:S(2)}) %collective-permute-start.26) | collective-permute-done | bytes 393248 | tf_op jit(solution)/shard_map/ppermute | solution.py:361
  272.9 1.6 collective-permute-start.24
  274.5 2.2 fusion.27
  276.8 1.4 copy-done.28
  278.2 2.6 fusion.3
  280.8 1.2 collective-permute-start.32
  282.0 9.7 %collective-permute-done.24.refs_2_ = bf16[256,768]{1,0:T(8,128)(2,1)} collective-permute-done((bf16[256,768]{1,0:T(8,128)(2,1)S(1)}, bf16[256,768]{1,0:T(8,128)(2,1)}, u32[]{:S(2)}, u32[]{:S(2)}) %collective-permute-start.24) | collective-permute-done | bytes 393248 | tf_op jit(solution)/shard_map/ppermute | solution.py:361
  292.7 3.2 collective-permute-start.30
  295.9 2.6 collective-permute-done.32
  299.6 1.4 copy-done.20
  301.4 3.1 fusion.20
  304.6 20.8 %collective-permute-done.30 = bf16[256,768]{1,0:T(8,128)(2,1)} collective-permute-done((bf16[256,768]{1,0:T(8,128)(2,1)S(1)}, bf16[256,768]{1,0:T(8,128)(2,1)}, u32[]{:S(2)}, u32[]{:S(2)}) %collective-permute-start.30) | collective-permute-done | bytes 393248 | tf_op jit(solution)/shard_map/ppermute | solution.py:361
  325.3 4.8 %collective-permute-done.33 = bf16[256,768]{1,0:T(8,128)(2,1)} collective-permute-done((bf16[256,768]{1,0:T(8,128)(2,1)}, bf16[256,768]{1,0:T(8,128)(2,1)}, u32[]{:S(2)}, u32[]{:S(2)}) %collective-permute-start.33) | collective-permute-done | bytes 393248 | tf_op jit(solution)/shard_map/ppermute | solution.py:361
  330.1 2.2 fusion.7
  (184 shorter events, 30.3 us)
Async XLA Ops:
  0.6 18.0 %copy-start = (s32[4]{0:T(128)S(1)}, s32[4]{0:T(128)}, u32[]{:S(2)}) copy-start(s32[4]{0:T(128)} %param.16) | copy-start | bytes 52
  8.9 8.1 %collective-permute-start = (bf16[2,384,768]{2,1,0:T(8,128)(2,1)}, bf16[2,384,768]{2,1,0:T(8,128)(2,1)S(1)}, u32[]{:S(2)}, u32[]{:S(2)}) collective-permute-start(bf16[2,384,768]{2,1,0:T(8,128)(2,1)} %get-tuple-element.90), channel_id=1, source_target_pairs={{0,4},{4,0},{8,12},{12,8},{16,20},{20,16},{24,28},{28,24},{1,5},{5... | collective-permute-start | bytes 3538952 | tf_op jit(solution)/shard_map/ppermute | solution.py:59
  9.6 27.8 %collective-permute-start.1 = (bf16[2,384,768]{2,1,0:T(8,128)(2,1)}, bf16[2,384,768]{2,1,0:T(8,128)(2,1)}, u32[]{:S(2)}, u32[]{:S(2)}) collective-permute-start(bf16[2,384,768]{2,1,0:T(8,128)(2,1)} %get-tuple-element.93), channel_id=1, source_target_pairs={{0,16},{4,20},{8,24},{12,28},{16,0},{20,4},{24,8},{28,12},{1,17},{... | collective-permute-start | bytes 3538952 | tf_op jit(solution)/shard_map/ppermute | solution.py:59
  10.8 27.5 %collective-permute-start.3 = (bf16[2,384,768]{2,1,0:T(8,128)(2,1)}, bf16[2,384,768]{2,1,0:T(8,128)(2,1)S(1)}, u32[]{:S(2)}, u32[]{:S(2)}) collective-permute-start(bf16[2,384,768]{2,1,0:T(8,128)(2,1)} %get-tuple-element.95.refs_1_), channel_id=1, source_target_pairs={{0,8},{4,12},{8,0},{12,4},{16,24},{20,28},{24,16},{28,20},{1,9},{5... | collective-permute-start | bytes 3538952 | tf_op jit(solution)/shard_map/ppermute | solution.py:59
  18.0 2.9 copy-start.5
  18.0 20.3 %collective-permute-start.2 = (bf16[384,768]{1,0:T(8,128)(2,1)}, bf16[384,768]{1,0:T(8,128)(2,1)S(1)}, u32[]{:S(2)}, u32[]{:S(2)}) collective-permute-start(bf16[384,768]{1,0:T(8,128)(2,1)} %get-tuple-element.94), channel_id=1, source_target_pairs={{0,4},{4,0},{8,12},{12,8},{16,20},{20,16},{24,28},{28,24},{1,5},{5... | collective-permute-start | bytes 1769480 | tf_op jit(solution)/shard_map/ppermute | solution.py:59
  18.7 56.6 %collective-permute-start.4 = (bf16[2,384,768]{2,1,0:T(8,128)(2,1)}, bf16[2,384,768]{2,1,0:T(8,128)(2,1)}, u32[]{:S(2)}, u32[]{:S(2)}) collective-permute-start(bf16[2,384,768]{2,1,0:T(8,128)(2,1)} %get-tuple-element.98), channel_id=1, source_target_pairs={{0,20},{4,16},{8,28},{12,24},{16,4},{20,0},{24,12},{28,8},{1,21},{... | collective-permute-start | bytes 3538952 | tf_op jit(solution)/shard_map/ppermute | solution.py:59
  19.4 55.9 %collective-permute-start.6 = (bf16[2,384,768]{2,1,0:T(8,128)(2,1)}, bf16[2,384,768]{2,1,0:T(8,128)(2,1)}, u32[]{:S(2)}, u32[]{:S(2)}) collective-permute-start(bf16[2,384,768]{2,1,0:T(8,128)(2,1)} %get-tuple-element.100.refs_5_.refs_1_), channel_id=1, source_target_pairs={{0,8},{4,12},{8,0},{12,4},{16,24},{20,28},{24,16},{28,20},{1,9},{5... | collective-permute-start | bytes 3538952 | tf_op jit(solution)/shard_map/ppermute | solution.py:59
  39.5 35.8 %collective-permute-start.5 = (bf16[384,768]{1,0:T(8,128)(2,1)}, bf16[384,768]{1,0:T(8,128)(2,1)S(1)}, u32[]{:S(2)}, u32[]{:S(2)}) collective-permute-start(bf16[384,768]{1,0:T(8,128)(2,1)} %get-tuple-element.99), channel_id=1, source_target_pairs={{0,16},{4,20},{8,24},{12,28},{16,0},{20,4},{24,8},{28,12},{1,17},{... | collective-permute-start | bytes 1769480 | tf_op jit(solution)/shard_map/ppermute | solution.py:59
  39.9 49.0 %collective-permute-start.8 = (bf16[2,384,768]{2,1,0:T(8,128)(2,1)}, bf16[2,384,768]{2,1,0:T(8,128)(2,1)}, u32[]{:S(2)}, u32[]{:S(2)}) collective-permute-start(bf16[2,384,768]{2,1,0:T(8,128)(2,1)} %get-tuple-element.104.refs_8_.refs_4_), channel_id=1, source_target_pairs={{0,8},{4,12},{8,0},{12,4},{16,24},{20,28},{24,16},{28,20},{1,9},{5... | collective-permute-start | bytes 3538952 | tf_op jit(solution)/shard_map/ppermute | solution.py:59
  76.2 51.9 %collective-permute-start.7 = (bf16[272,3072]{1,0:T(8,128)(2,1)}, bf16[272,3072]{1,0:T(8,128)(2,1)S(1)}, u32[]{:S(2)}, u32[]{:S(2)}) collective-permute-start(bf16[272,3072]{1,0:T(8,128)(2,1)} %get-tuple-element.101.refs_0_), channel_id=1, source_target_pairs={{0,4},{4,0},{8,12},{12,8},{16,20},{20,16},{24,28},{28,24},{1,5},{5... | collective-permute-start | bytes 5013512 | tf_op jit(solution)/shard_map/ppermute | solution.py:59
  76.9 51.2 %collective-permute-start.9 = (bf16[272,3072]{1,0:T(8,128)(2,1)}, bf16[272,3072]{1,0:T(8,128)(2,1)S(1)}, u32[]{:S(2)}, u32[]{:S(2)}) collective-permute-start(bf16[272,3072]{1,0:T(8,128)(2,1)} %get-tuple-element.101.refs_0_), channel_id=1, source_target_pairs={{0,16},{4,20},{8,24},{12,28},{16,0},{20,4},{24,8},{28,12},{1,17},{... | collective-permute-start | bytes 5013512 | tf_op jit(solution)/shard_map/ppermute | solution.py:59
  78.2 50.0 %collective-permute-start.11 = (bf16[2,384,768]{2,1,0:T(8,128)(2,1)}, bf16[2,384,768]{2,1,0:T(8,128)(2,1)}, u32[]{:S(2)}, u32[]{:S(2)}) collective-permute-start(bf16[2,384,768]{2,1,0:T(8,128)(2,1)} %get-tuple-element.107.refs_9_.refs_5_), channel_id=1, source_target_pairs={{0,8},{4,12},{8,0},{12,4},{16,24},{20,28},{24,16},{28,20},{1,9},{5... | collective-permute-start | bytes 3538952 | tf_op jit(solution)/shard_map/ppermute | solution.py:59
  78.4 49.7 %collective-permute-start.10 = (bf16[384,768]{1,0:T(8,128)(2,1)}, bf16[384,768]{1,0:T(8,128)(2,1)}, u32[]{:S(2)}, u32[]{:S(2)}) collective-permute-start(bf16[384,768]{1,0:T(8,128)(2,1)} %get-tuple-element.106), channel_id=1, source_target_pairs={{0,20},{4,16},{8,28},{12,24},{16,4},{20,0},{24,12},{28,8},{1,21},{... | collective-permute-start | bytes 1769480 | tf_op jit(solution)/shard_map/ppermute | solution.py:59
  88.9 39.2 %collective-permute-start.12 = (bf16[384,768]{1,0:T(8,128)(2,1)}, bf16[384,768]{1,0:T(8,128)(2,1)S(1)}, u32[]{:S(2)}, u32[]{:S(2)}) collective-permute-start(bf16[384,768]{1,0:T(8,128)(2,1)} %get-tuple-element.108.refs_0_.refs_4_), channel_id=1, source_target_pairs={{0,8},{4,12},{8,0},{12,4},{16,24},{20,28},{24,16},{28,20},{1,9},{5... | collective-permute-start | bytes 1769480 | tf_op jit(solution)/shard_map/ppermute | solution.py:59
  130.2 3.8 %collective-permute-start.13 = (bf16[272,3072]{1,0:T(8,128)(2,1)}, bf16[272,3072]{1,0:T(8,128)(2,1)S(1)}, u32[]{:S(2)}, u32[]{:S(2)}) collective-permute-start(bf16[272,3072]{1,0:T(8,128)(2,1)} %get-tuple-element.109.refs_2_), channel_id=1, source_target_pairs={{0,4},{4,0},{8,12},{12,8},{16,20},{20,16},{24,28},{28,24},{1,5},{5... | collective-permute-start | bytes 5013512 | tf_op jit(solution)/shard_map/ppermute | solution.py:59
  130.6 30.4 %collective-permute-start.14 = (bf16[384,768]{1,0:T(8,128)(2,1)}, bf16[384,768]{1,0:T(8,128)(2,1)S(1)}, u32[]{:S(2)}, u32[]{:S(2)}) collective-permute-start(bf16[384,768]{1,0:T(8,128)(2,1)} %get-tuple-element.115.refs_1_.refs_5_), channel_id=1, source_target_pairs={{0,8},{4,12},{8,0},{12,4},{16,24},{20,28},{24,16},{28,20},{1,9},{5... | collective-permute-start | bytes 1769480 | tf_op jit(solution)/shard_map/ppermute | solution.py:59
  130.9 30.2 %collective-permute-start.15 = (bf16[384,768]{1,0:T(8,128)(2,1)}, bf16[384,768]{1,0:T(8,128)(2,1)S(1)}, u32[]{:S(2)}, u32[]{:S(2)}) collective-permute-start(bf16[384,768]{1,0:T(8,128)(2,1)} %get-tuple-element.116.refs_2_.refs_8_), channel_id=1, source_target_pairs={{0,8},{4,12},{8,0},{12,4},{16,24},{20,28},{24,16},{28,20},{1,9},{5... | collective-permute-start | bytes 1769480 | tf_op jit(solution)/shard_map/ppermute | solution.py:59
  152.6 8.4 %copy-start.14 = (bf16[4,256,768]{2,1,0:T(8,128)(2,1)}, bf16[4,256,768]{2,1,0:T(8,128)(2,1)S(1)}, u32[]{:S(2)}) copy-start(bf16[4,256,768]{2,1,0:T(8,128)(2,1)S(1)} %get-tuple-element.137.slope_ref) | copy-start | bytes 4718596
  152.6 8.4 %copy-start.16 = (bf16[4,256,768]{2,1,0:T(8,128)(2,1)}, bf16[4,256,768]{2,1,0:T(8,128)(2,1)S(1)}, u32[]{:S(2)}) copy-start(bf16[4,256,768]{2,1,0:T(8,128)(2,1)S(1)} %get-tuple-element.138.active_ref) | copy-start | bytes 4718596
  152.7 8.4 %copy-start.17 = (bf16[4,256,768]{2,1,0:T(8,128)(2,1)}, bf16[4,256,768]{2,1,0:T(8,128)(2,1)S(1)}, u32[]{:S(2)}) copy-start(bf16[4,256,768]{2,1,0:T(8,128)(2,1)S(1)} %get-tuple-element.113.refs_3_.hidden_ref) | copy-start | bytes 4718596
  162.1 3.8 %copy-start.29 = (bf16[2,2,256,768]{3,2,1,0:T(8,128)(2,1)S(1)}, bf16[2,2,256,768]{3,2,1,0:T(8,128)(2,1)}, u32[]{:S(2)}) copy-start(bf16[2,2,256,768]{3,2,1,0:T(8,128)(2,1)} %get-tuple-element.123) | copy-start | bytes 4718596
  162.1 3.8 %collective-permute-start.19 = (bf16[2,2,256,768]{3,2,1,0:T(8,128)(2,1)}, bf16[2,2,256,768]{3,2,1,0:T(8,128)(2,1)}, u32[]{:S(2)}, u32[]{:S(2)}) collective-permute-start(bf16[2,2,256,768]{3,2,1,0:T(8,128)(2,1)} %get-tuple-element.122), channel_id=1, source_target_pairs={{0,4},{4,0},{8,12},{12,8},{16,20},{20,16},{24,28},{28,24},{1,5},{5... | collective-permute-start | bytes 4718600 | tf_op jit(solution)/shard_map/ppermute | solution.py:59
  163.5 35.8 %collective-permute-start.16 = (bf16[256,3072]{1,0:T(8,128)(2,1)S(1)}, bf16[256,3072]{1,0:T(8,128)(2,1)}, u32[]{:S(2)}, u32[]{:S(2)}) collective-permute-start(bf16[256,3072]{1,0:T(8,128)(2,1)S(1)} %copy-done.8), channel_id=1, source_target_pairs={{0,16},{4,20},{8,24},{12,28},{16,0},{20,4},{24,8},{28,12},{1,17},{... | collective-permute-start | bytes 4718600 | tf_op jit(solution)/shard_map/ppermute | solution.py:59
  164.7 34.5 %collective-permute-start.18 = (bf16[256,3072]{1,0:T(8,128)(2,1)S(1)}, bf16[256,3072]{1,0:T(8,128)(2,1)}, u32[]{:S(2)}, u32[]{:S(2)}) collective-permute-start(bf16[256,3072]{1,0:T(8,128)(2,1)S(1)} %copy-done.8), channel_id=1, source_target_pairs={{0,4},{4,0},{8,12},{12,8},{16,20},{20,16},{24,28},{28,24},{1,5},{5... | collective-permute-start | bytes 4718600 | tf_op jit(solution)/shard_map/ppermute | solution.py:59
  165.3 15.3 %collective-permute-start.17 = (bf16[384,768]{1,0:T(8,128)(2,1)}, bf16[384,768]{1,0:T(8,128)(2,1)}, u32[]{:S(2)}, u32[]{:S(2)}) collective-permute-start(bf16[384,768]{1,0:T(8,128)(2,1)} %get-tuple-element.117.refs_3_.refs_9_), channel_id=1, source_target_pairs={{0,8},{4,12},{8,0},{12,4},{16,24},{20,28},{24,16},{28,20},{1,9},{5... | collective-permute-start | bytes 1769480 | tf_op jit(solution)/shard_map/ppermute | solution.py:59
  208.2 4.6 %copy-start.30 = (bf16[2,2,256,768]{3,2,1,0:T(8,128)(2,1)S(1)}, bf16[2,2,256,768]{3,2,1,0:T(8,128)(2,1)}, u32[]{:S(2)}) copy-start(bf16[2,2,256,768]{3,2,1,0:T(8,128)(2,1)} %get-tuple-element.126) | copy-start | bytes 4718596
  208.2 4.6 %collective-permute-start.20 = (bf16[2,2,256,768]{3,2,1,0:T(8,128)(2,1)}, bf16[2,2,256,768]{3,2,1,0:T(8,128)(2,1)}, u32[]{:S(2)}, u32[]{:S(2)}) collective-permute-start(bf16[2,2,256,768]{3,2,1,0:T(8,128)(2,1)} %get-tuple-element.129), channel_id=1, source_target_pairs={{0,4},{4,0},{8,12},{12,8},{16,20},{20,16},{24,28},{28,24},{1,5},{5... | collective-permute-start | bytes 4718600 | tf_op jit(solution)/shard_map/ppermute | solution.py:59
  209.4 6.6 %collective-permute-start.21 = (bf16[256,3072]{1,0:T(8,128)(2,1)}, bf16[256,3072]{1,0:T(8,128)(2,1)}, u32[]{:S(2)}, u32[]{:S(2)}) collective-permute-start(bf16[256,3072]{1,0:T(8,128)(2,1)} %get-tuple-element.131.refs_2_), channel_id=1, source_target_pairs={{0,4},{4,0},{8,12},{12,8},{16,20},{20,16},{24,28},{28,24},{1,5},{5... | collective-permute-start | bytes 4718600 | tf_op jit(solution)/shard_map/ppermute | solution.py:59
  209.5 30.0 %collective-permute-start.23 = (bf16[2,256,768]{2,1,0:T(8,128)(2,1)S(1)}, bf16[2,256,768]{2,1,0:T(8,128)(2,1)S(1)}, u32[]{:S(2)}, u32[]{:S(2)}) collective-permute-start(bf16[2,256,768]{2,1,0:T(8,128)(2,1)S(1)} %copy-done.33), channel_id=1, source_target_pairs={{0,16},{4,20},{8,24},{12,28},{16,0},{20,4},{24,8},{28,12},{1,17},{... | collective-permute-start | bytes 2359304 | tf_op jit(solution)/shard_map/ppermute | solution.py:59
  216.0 28.6 %collective-permute-start.22 = (bf16[2,256,768]{2,1,0:T(8,128)(2,1)}, bf16[2,256,768]{2,1,0:T(8,128)(2,1)S(1)}, u32[]{:S(2)}, u32[]{:S(2)}) collective-permute-start(bf16[2,256,768]{2,1,0:T(8,128)(2,1)} %get-tuple-element.132), channel_id=1, source_target_pairs={{0,16},{4,20},{8,24},{12,28},{16,0},{20,4},{24,8},{28,12},{1,17},{... | collective-permute-start | bytes 2359304 | tf_op jit(solution)/shard_map/ppermute | solution.py:59
  230.4 9.1 %copy-start.12 = (bf16[4,256,768]{2,1,0:T(8,128)(2,1)}, bf16[4,256,768]{2,1,0:T(8,128)(2,1)S(1)}, u32[]{:S(2)}) copy-start(bf16[4,256,768]{2,1,0:T(8,128)(2,1)S(1)} %get-tuple-element.141.up_ref) | copy-start | bytes 4718596
  239.5 5.1 %copy-start.25 = (bf16[2,256,768]{2,1,0:T(8,128)(2,1)}, bf16[2,256,768]{2,1,0:T(8,128)(2,1)S(1)}, u32[]{:S(2)}) copy-start(bf16[2,256,768]{2,1,0:T(8,128)(2,1)S(1)} %collective-permute-done.23.refs_2_) | copy-start | bytes 2359300
  245.5 7.2 %collective-permute-start.27 = (bf16[2,2,256,768]{3,2,1,0:T(8,128)(2,1)}, bf16[2,2,256,768]{3,2,1,0:T(8,128)(2,1)}, u32[]{:S(2)}, u32[]{:S(2)}) collective-permute-start(bf16[2,2,256,768]{3,2,1,0:T(8,128)(2,1)} %get-tuple-element.149), channel_id=1, source_target_pairs={{0,4},{4,0},{8,12},{12,8},{16,20},{20,16},{24,28},{28,24},{1,5},{5... | collective-permute-start | bytes 4718600 | tf_op jit(solution)/shard_map/ppermute | solution.py:59
  251.3 15.1 %collective-permute-start.25 = (bf16[256,768]{1,0:T(8,128)(2,1)}, bf16[256,768]{1,0:T(8,128)(2,1)S(1)}, u32[]{:S(2)}, u32[]{:S(2)}) collective-permute-start(bf16[256,768]{1,0:T(8,128)(2,1)} %get-tuple-element.146), channel_id=1, source_target_pairs={{0,1},{1,2},{2,3},{3,0},{4,5},{5,6},{6,7},{7,4},{8,9},{9,10},{10,1... | collective-permute-start | bytes 1179656 | tf_op jit(solution)/shard_map/ppermute | solution.py:361
  252.6 19.3 %collective-permute-start.26 = (bf16[256,768]{1,0:T(8,128)(2,1)}, bf16[256,768]{1,0:T(8,128)(2,1)}, u32[]{:S(2)}, u32[]{:S(2)}) collective-permute-start(bf16[256,768]{1,0:T(8,128)(2,1)} %get-tuple-element.147), channel_id=1, source_target_pairs={{0,3},{1,0},{2,1},{3,2},{4,7},{5,4},{6,5},{7,6},{8,11},{9,8},{10,9... | collective-permute-start | bytes 1179656 | tf_op jit(solution)/shard_map/ppermute | solution.py:361
  255.9 18.7 %collective-permute-start.28 = (bf16[2,256,768]{2,1,0:T(8,128)(2,1)}, bf16[2,256,768]{2,1,0:T(8,128)(2,1)}, u32[]{:S(2)}, u32[]{:S(2)}) collective-permute-start(bf16[2,256,768]{2,1,0:T(8,128)(2,1)} %get-tuple-element.156), channel_id=1, source_target_pairs={{0,16},{4,20},{8,24},{12,28},{16,0},{20,4},{24,8},{28,12},{1,17},{... | collective-permute-start | bytes 2359304 | tf_op jit(solution)/shard_map/ppermute | solution.py:59
  266.4 5.6 %copy-start.36 = (bf16[256,768]{1,0:T(8,128)(2,1)}, bf16[256,768]{1,0:T(8,128)(2,1)S(1)}, u32[]{:S(2)}) copy-start(bf16[256,768]{1,0:T(8,128)(2,1)S(1)} %collective-permute-done.25.refs_2_) | copy-start | bytes 1179652
  271.9 4.8 %collective-permute-start.29 = (bf16[2,2,256,768]{3,2,1,0:T(8,128)(2,1)}, bf16[2,2,256,768]{3,2,1,0:T(8,128)(2,1)}, u32[]{:S(2)}, u32[]{:S(2)}) collective-permute-start(bf16[2,2,256,768]{3,2,1,0:T(8,128)(2,1)} %get-tuple-element.157), channel_id=1, source_target_pairs={{0,4},{4,0},{8,12},{12,8},{16,20},{20,16},{24,28},{28,24},{1,5},{5... | collective-permute-start | bytes 4718600 | tf_op jit(solution)/shard_map/ppermute | solution.py:59
  272.9 18.8 %collective-permute-start.24 = (bf16[256,768]{1,0:T(8,128)(2,1)S(1)}, bf16[256,768]{1,0:T(8,128)(2,1)}, u32[]{:S(2)}, u32[]{:S(2)}) collective-permute-start(bf16[256,768]{1,0:T(8,128)(2,1)S(1)} %copy-done.35), channel_id=1, source_target_pairs={{0,2},{1,3},{2,0},{3,1},{4,6},{5,7},{6,4},{7,5},{8,10},{9,11},{10,... | collective-permute-start | bytes 1179656 | tf_op jit(solution)/shard_map/ppermute | solution.py:361
  280.8 17.7 %copy-start.23 = (f32[2,1,256,768]{3,2,1,0:T(8,128)}, f32[2,1,256,768]{3,2,1,0:T(8,128)S(1)}, u32[]{:S(2)}) copy-start(f32[2,1,256,768]{3,2,1,0:T(8,128)S(1)} %get-tuple-element.174) | copy-start | bytes 4718596
  280.8 17.7 %collective-permute-start.32 = (bf16[2,256,768]{2,1,0:T(8,128)(2,1)}, bf16[2,256,768]{2,1,0:T(8,128)(2,1)S(1)}, u32[]{:S(2)}, u32[]{:S(2)}) collective-permute-start(bf16[2,256,768]{2,1,0:T(8,128)(2,1)} %get-tuple-element.164), channel_id=1, source_target_pairs={{0,16},{4,20},{8,24},{12,28},{16,0},{20,4},{24,8},{28,12},{1,17},{... | collective-permute-start | bytes 2359304 | tf_op jit(solution)/shard_map/ppermute | solution.py:59
  291.7 12.9 %collective-permute-start.31 = (bf16[256,768]{1,0:T(8,128)(2,1)}, bf16[256,768]{1,0:T(8,128)(2,1)}, u32[]{:S(2)}, u32[]{:S(2)}) collective-permute-start(bf16[256,768]{1,0:T(8,128)(2,1)} %get-tuple-element.162), channel_id=1, source_target_pairs={{0,1},{1,2},{2,3},{3,0},{4,5},{5,6},{6,7},{7,4},{8,9},{9,10},{10,1... | collective-permute-start | bytes 1179656 | tf_op jit(solution)/shard_map/ppermute | solution.py:361
  292.7 32.6 %collective-permute-start.30 = (bf16[256,768]{1,0:T(8,128)(2,1)S(1)}, bf16[256,768]{1,0:T(8,128)(2,1)}, u32[]{:S(2)}, u32[]{:S(2)}) collective-permute-start(bf16[256,768]{1,0:T(8,128)(2,1)S(1)} %copy-done.34), channel_id=1, source_target_pairs={{0,2},{1,3},{2,0},{3,1},{4,6},{5,7},{6,4},{7,5},{8,10},{9,11},{10,... | collective-permute-start | bytes 1179656 | tf_op jit(solution)/shard_map/ppermute | solution.py:361
  299.5 30.6 %collective-permute-start.33 = (bf16[256,768]{1,0:T(8,128)(2,1)}, bf16[256,768]{1,0:T(8,128)(2,1)}, u32[]{:S(2)}, u32[]{:S(2)}) collective-permute-start(bf16[256,768]{1,0:T(8,128)(2,1)} %get-tuple-element.165), channel_id=1, source_target_pairs={{0,3},{1,0},{2,1},{3,2},{4,7},{5,4},{6,5},{7,6},{8,11},{9,8},{10,9... | collective-permute-start | bytes 1179656 | tf_op jit(solution)/shard_map/ppermute | solution.py:361
  301.4 28.7 %copy-start.24 = (f32[2,1,256,768]{3,2,1,0:T(8,128)S(1)}, f32[2,1,256,768]{3,2,1,0:T(8,128)}, u32[]{:S(2)}) copy-start(f32[2,1,256,768]{3,2,1,0:T(8,128)} %copy-done.23) | copy-start | bytes 4718596
  301.4 28.7 %copy-start.32 = (bf16[2,256,768]{2,1,0:T(8,128)(2,1)S(1)}, bf16[2,256,768]{2,1,0:T(8,128)(2,1)}, u32[]{:S(2)}) copy-start(bf16[2,256,768]{2,1,0:T(8,128)(2,1)} %copy-done.31) | copy-start | bytes 2359300
  301.4 31.0 %copy-start.1 = (s32[4]{0:T(128)S(1)}, s32[4]{0:T(128)}, u32[]{:S(2)}) copy-start(s32[4]{0:T(128)} %param.16) | copy-start | bytes 52
  (37 other events, 48.4 us)
